TPU v7x, 32 devices: a whole 2x2x4 slice. The times are simulated.
32 devices in a mesh: groups: 2 (over x), slab: 16 (over z, y, core).
Axes of the slice: x: 2, y: 2, z: 4, core: 2. Of those that a mesh axis runs over, the one named last changes fastest.
Arguments:
- latent: bfloat16 [64, 32, 2048], P(None, ('groups', 'slab')), parts along dimension 1, may hold values from -6 to 6
- conv1_weight: bfloat16 [27, 64, 64], replicated, may hold values from -0.15625 to 0.15625
- conv2_weight: bfloat16 [27, 64, 64], replicated, may hold values from -0.15625 to 0.15625
- head: bfloat16 [64], replicated, may hold values from -2 to 2
- p_prev: float32 [32, 16, 64, 128], P(('groups', 'slab')), parts along dimension 0, may hold values from -6 to 6
- p_cur: float32 [32, 16, 64, 128], P(('groups', 'slab')), parts along dimension 0, may hold values from -6 to 6
- adjoint: bfloat16 [4, 32, 16, 64, 128], P(None, ('groups', 'slab')), parts along dimension 1, may hold values from -6 to 6
- wavelet: float32 [16, 4], P('groups'), parts along dimension 0, may hold values from -12 to 12
- sources: int32 [16, 3], P('groups'), parts along dimension 0, may hold values from 0 to 127, as said below
- receivers: int32 [16, 3, 128], P('groups'), parts along dimension 0, may hold values from 0 to 127, as said below
Outputs:
- pressure_final: float32 [32, 16, 64, 128], P(('groups', 'slab')), parts along dimension 0
- traces: float32 [16, 4, 128], P('groups'), parts along dimension 0
- gradient: float32 [32, 2048], P(('groups', 'slab')), parts along dimension 0
There are 2 independent parts, one for each index of `groups`. A program takes and returns all parts, laid end to end along the dimension named above; an argument that names none is the same for every part. Nothing has to cross between parts.
Inputs may be any that keep to these rules, and one draw needn't show every extreme that they name: sources[s] is the source cell (depth, row, column) of shot s on the fine grid: depth below 32, row below 64, column below 128. receivers[s, :, k] is the cell (depth, row, column) of receiver k of shot s on the fine grid: depth below 32, row below 64, column below 128.
All inputs are finite; a program needn't handle non-finite values.
Results may differ from a plain program's by a relative error of at most 0.006.
Values may be sent and summed in bfloat16 or wider, within the bound.
No kernel may reach another device: no remote copies, remote signals or barrier semaphores. Data moves between devices by JAX's collectives and lax.ppermute only.
A program may use at most 64 MiB of HBM per device.

v0:
```python
import jax
import jax.numpy as jnp
from jax import lax
from jax.sharding import PartitionSpec as P

CY = 32
CX = 64
SHOTS = 8
STEPS = 4


stencil_weights = (-205.0 / 72.0, 8.0 / 5.0, -1.0 / 5.0, 8.0 / 315.0, -1.0 / 560.0)
lowest_speed = 1.5
speed_range = 3.0
courant = 0.088
leak_slope = 0.2


def extended_2(block, sides, width):
    for axis, dim in sides:
        count = lax.axis_size(axis)
        forward = [(i, i + 1) for i in range(count - 1)]
        backward = [(target, source) for source, target in forward]
        low = lax.ppermute(
            lax.slice_in_dim(block, block.shape[dim] - width, None, axis=dim), axis, forward
        )
        high = lax.ppermute(lax.slice_in_dim(block, 0, width, axis=dim), axis, backward)
        block = jnp.concatenate([low, block, high], axis=dim)
    return block


def from_partner(value, axis, apart):
    mask = 2**apart
    pairs = [(source, source ^ mask) for source in range(lax.axis_size(axis))]
    return lax.ppermute(value, axis, pairs)


def for_sending(shard):
    return jax.tree.map(lambda a: a.astype(jnp.bfloat16) if a.dtype == jnp.float32 else a, shard)


def from_behind(value, axis, steps):
    count = lax.axis_size(axis)
    leading, last = (max(0, -steps), min(count, count - steps))
    return lax.ppermute(value, axis, [(source, source + steps) for source in range(leading, last)])


def conv_taps(extended_in, weight):
    planes = extended_in.shape[1] - 2
    cell_count = extended_in.shape[2]
    extended = jnp.pad(extended_in, ((0, 0), (0, 0), (CX + 1, CX + 1)))
    columns = jnp.arange(cell_count) % CX
    accumulated = jnp.zeros((weight.shape[1], planes, cell_count), jnp.float32)
    tap_index = 0
    for depth_off in range(3):
        for row_off in (-1, 0, 1):
            for col_off in (-1, 0, 1):
                begin_at = CX + 1 + row_off * CX + col_off
                piece = extended[
                    :, depth_off : depth_off + planes, begin_at : begin_at + cell_count
                ]
                column_valid = ((columns + col_off >= 0) & (columns + col_off < CX)).astype(
                    extended.dtype
                )
                accumulated = accumulated + jnp.einsum(
                    "oi,izn->ozn",
                    weight[tap_index],
                    piece * column_valid,
                    preferred_element_type=jnp.float32,
                )
                tap_index += 1
    return accumulated


def double_axis(values, axis):
    length = values.shape[axis]
    lower_side = jnp.concatenate(
        [
            lax.slice_in_dim(values, 0, 1, axis=axis),
            lax.slice_in_dim(values, 0, length - 1, axis=axis),
        ],
        axis=axis,
    )
    upper_side = jnp.concatenate(
        [
            lax.slice_in_dim(values, 1, length, axis=axis),
            lax.slice_in_dim(values, length - 1, length, axis=axis),
        ],
        axis=axis,
    )
    even_part = 0.75 * values + 0.25 * lower_side
    odd_part = 0.75 * values + 0.25 * upper_side
    new_shape = list(values.shape)
    new_shape[axis] = 2 * length
    return jnp.stack([even_part, odd_part], axis=axis + 1).reshape(new_shape)


def double_depth(rimmed):
    inner_planes = rimmed.shape[0] - 2
    middle = rimmed[1:-1]
    even_part = 0.75 * middle + 0.25 * rimmed[:-2]
    odd_part = 0.75 * middle + 0.25 * rimmed[2:]
    return jnp.stack([even_part, odd_part], axis=1).reshape((2 * inner_planes,) + rimmed.shape[1:])


def upsample_slab(rimmed):
    deeper = double_depth(rimmed).reshape(2 * (rimmed.shape[0] - 2), CY, CX)
    return double_axis(double_axis(deeper, 1), 2)


def stencil(extended):
    depth_total = extended.shape[0] - 8
    row_total = extended.shape[1]
    col_total = extended.shape[2]
    padded = jnp.pad(extended, ((0, 0), (4, 4), (4, 4)))

    def window(depth_at, row_at, col_at):
        return padded[
            depth_at : depth_at + depth_total,
            row_at : row_at + row_total,
            col_at : col_at + col_total,
        ]

    accumulated = 3.0 * stencil_weights[0] * window(4, 4, 4)
    for reach in range(1, 5):
        near_sum = window(4 - reach, 4, 4) + window(4 + reach, 4, 4)
        near_sum = near_sum + window(4, 4 - reach, 4) + window(4, 4 + reach, 4)
        near_sum = near_sum + window(4, 4, 4 - reach) + window(4, 4, 4 + reach)
        accumulated = accumulated + stencil_weights[reach] * near_sum
    return accumulated


def body(
    latent, conv1_weight, conv2_weight, head, p_prev, p_cur, adjoint, wavelet, sources, receivers
):
    position = lax.axis_index("slab")
    devices = lax.axis_size("slab")
    my_shot = position % SHOTS
    slab_index = position // SHOTS
    slab_total = devices // SHOTS
    group_bits = SHOTS.bit_length() - 1
    latent_wide = extended_2(latent, (("slab", 1),), 1)
    hidden = jax.nn.leaky_relu(conv_taps(latent_wide, conv1_weight), leak_slope).astype(
        jnp.bfloat16
    )
    hidden_wide = extended_2(hidden, (("slab", 1),), 1)
    second = jax.nn.leaky_relu(conv_taps(hidden_wide, conv2_weight), leak_slope)
    logits = jnp.einsum(
        "c,czn->zn", head.astype(jnp.float32), second, precision=lax.Precision.HIGHEST
    )
    velocity = (lowest_speed + speed_range * jax.nn.sigmoid(logits)).astype(jnp.bfloat16)
    planes = velocity.shape[0]
    slab_planes = planes * SHOTS
    rimmed = extended_2(velocity, (("slab", 0),), 1)
    rimmed = jnp.concatenate(
        [
            jnp.where(position == 0, velocity, rimmed[:1]),
            rimmed[1:-1],
            jnp.where(position == devices - 1, velocity, rimmed[-1:]),
        ],
        axis=0,
    )
    tile_doubled = double_depth(rimmed.astype(jnp.float32))
    bit_order = list(range(group_bits))
    blocks = tile_doubled[None]
    for bit_index in bit_order:
        partner = from_partner(blocks, "slab", bit_index)
        upper_bit = my_shot // (1 << bit_index) % 2 == 1
        blocks = jnp.where(
            upper_bit,
            jnp.concatenate([partner, blocks], axis=0),
            jnp.concatenate([blocks, partner], axis=0),
        )
    placed = []
    for shot_number in range(SHOTS):
        list_index = 0
        for section_number in range(group_bits):
            list_index = list_index + (
                (shot_number >> bit_order[section_number] & 1) << section_number
            )
        placed.append(blocks[list_index])
    deeper = jnp.concatenate(placed, axis=0).reshape(2 * slab_planes, CY, CX)
    fine_speed = double_axis(double_axis(deeper, 1), 2)
    courant_sq = (courant * fine_speed) ** 2
    previous = p_prev[0]
    current = p_cur[0]
    fine_planes = current.shape[0]
    offset = slab_index * fine_planes
    source = lax.dynamic_index_in_dim(sources, my_shot, 0, keepdims=False)
    station = lax.dynamic_index_in_dim(receivers, my_shot, 0, keepdims=False)
    pulses = lax.dynamic_index_in_dim(wavelet, my_shot, 0, keepdims=False)
    source_depth = source[0] - offset
    source_inside = (source_depth >= 0) & (source_depth < fine_planes)
    source_depth = jnp.clip(source_depth, 0, fine_planes - 1)
    station_depth = station[0] - offset
    station_inside = (station_depth >= 0) & (station_depth < fine_planes)
    station_depth = jnp.clip(station_depth, 0, fine_planes - 1)
    correlation = jnp.zeros(current.shape, jnp.float32)
    samples_list = []
    for step_index in range(STEPS):
        rim_below = from_behind(for_sending(current[-4:]), "slab", SHOTS)
        rim_above = from_behind(for_sending(current[:4]), "slab", -SHOTS)
        laplace_term = stencil(jnp.concatenate([rim_below, current, rim_above], axis=0))
        correlation = correlation + adjoint[step_index, 0].astype(jnp.float32) * laplace_term
        advanced = 2.0 * current - previous + courant_sq * laplace_term
        advanced = advanced.at[source_depth, source[1], source[2]].add(
            jnp.where(source_inside, pulses[step_index], 0.0)
        )
        samples_list.append(
            jnp.where(station_inside, advanced[station_depth, station[1], station[2]], 0.0)
        )
        previous, current = (current, advanced)
    record = jnp.stack(samples_list)
    own_traces = jnp.where((jnp.arange(SHOTS) == my_shot)[:, None, None], record[None], 0.0)
    traces = lax.psum(own_traces, "slab")
    fine_gradient = 2.0 * courant * courant * fine_speed * correlation
    shape_holder = jnp.zeros((slab_planes + 2, velocity.shape[1]), jnp.float32)
    unused, pullback = jax.vjp(upsample_slab, shape_holder)
    grad_rim = pullback(fine_gradient)[0]
    first_slab = slab_index == 0
    last_slab = slab_index == slab_total - 1
    folded = jnp.concatenate(
        [
            jnp.where(first_slab, 0.0, grad_rim[:1]),
            grad_rim[1:2] + jnp.where(first_slab, grad_rim[:1], 0.0),
            grad_rim[2:-2],
            grad_rim[-2:-1] + jnp.where(last_slab, grad_rim[-1:], 0.0),
            jnp.where(last_slab, 0.0, grad_rim[-1:]),
        ],
        axis=0,
    )
    from_lower = from_behind(folded[-1:], "slab", SHOTS)
    from_upper = from_behind(folded[:1], "slab", -SHOTS)
    inner = folded[1:-1]
    inner = jnp.concatenate([inner[:1] + from_lower, inner[1:-1], inner[-1:] + from_upper], axis=0)
    blocks = inner.reshape(SHOTS, planes, inner.shape[1])
    for bit_index in reversed(range(group_bits)):
        halfway = blocks.shape[0] // 2
        upper_bit = my_shot // (1 << bit_index) % 2 == 1
        retained = jnp.where(upper_bit, blocks[halfway:], blocks[:halfway])
        outgoing = jnp.where(upper_bit, blocks[:halfway], blocks[halfway:])
        blocks = retained + from_partner(outgoing, "slab", bit_index)
    gradient = blocks[0]
    return (current[None], traces, gradient)


def solution(mesh):
    in_specs = (
        P(None, ("groups", "slab"), None),
        P(),
        P(),
        P(),
        P(("groups", "slab"), None, None, None),
        P(("groups", "slab"), None, None, None),
        P(None, ("groups", "slab"), None, None, None),
        P("groups", None),
        P("groups", None),
        P("groups", None, None),
    )
    out_specs = (
        P(("groups", "slab"), None, None, None),
        P("groups", None, None),
        P(("groups", "slab"), None),
    )
    return jax.shard_map(body, mesh=mesh, in_specs=in_specs, out_specs=out_specs, check_vma=False)
```

profile of v0, /device:TPU:0, one launch (start us, length us, event | category | flops | bytes accessed | tf_op | source)
XLA Modules:
  0.0 228.8 jit_solution(11264955654170186735)
XLA Ops:
  0.7 1.4 collective-permute-start.1
  2.1 3.1 %collective-permute-start = (bf16[64,1,2048]{2,0,1:T(8,128)(2,1)}, bf16[64,1,2048]{2,0,1:T(8,128)(2,1)S(1)}, u32[]{:S(2)}, u32[]{:S(2)}) collective-permute-start(bf16[64,1,2048]{2,0,1:T(8,128)(2,1)} %param.18), channel_id=1, source_target_pairs={{0,1},{1,2},{2,3},{3,4},{4,5},{5,6},{6,7},{7,8},{8,9},{9,10},{10,1... | collective-permute-start | bytes 786440 | tf_op jit(solution)/shard_map/ppermute | solution.py:24
  5.2 1.1 convert.20
  6.5 1.3 fusion.32
  15.2 1.3 collective-permute-start.3
  16.5 9.2 %collective-permute-start.2 = (bf16[64,1,2048]{2,0,1:T(8,128)(2,1)S(1)}, bf16[64,1,2048]{2,0,1:T(8,128)(2,1)S(1)}, u32[]{:S(2)}, u32[]{:S(2)}) collective-permute-start(bf16[64,1,2048]{2,0,1:T(8,128)(2,1)S(1)} %bitcast.577), channel_id=1, source_target_pairs={{0,1},{1,2},{2,3},{3,4},{4,5},{5,6},{6,7},{7,8},{8,9},{9,10},{10,1... | collective-permute-start | bytes 786440 | tf_op jit(solution)/shard_map/ppermute | solution.py:24
  25.7 5.7 %collective-permute-start.9 = (bf16[4,64,128]{2,1,0:T(8,128)(2,1)S(1)}, bf16[4,64,128]{2,1,0:T(8,128)(2,1)S(1)}, u32[]{:S(2)}, u32[]{:S(2)}) collective-permute-start(bf16[4,64,128]{2,1,0:T(8,128)(2,1)S(1)} %get-tuple-element.81), channel_id=1, source_target_pairs={{0,8},{1,9},{2,10},{3,11},{4,12},{5,13},{6,14},{7,15},{16,24},{17,... | collective-permute-start | bytes 196616 | tf_op jit(solution)/shard_map/ppermute | solution.py:45
  31.4 1.3 collective-permute-start.10
  32.8 0.6 fusion.496
  41.6 1.3 collective-permute-start.5
  42.9 3.6 %collective-permute-start.4 = (bf16[1,2048]{1,0:T(2,128)(2,1)S(1)}, bf16[1,2048]{1,0:T(2,128)(2,1)S(1)}, u32[]{:S(2)}, u32[]{:S(2)}) collective-permute-start(bf16[1,2048]{1,0:T(2,128)(2,1)S(1)} %convert_element_type.266), channel_id=1, source_target_pairs={{0,1},{1,2},{2,3},{3,4},{4,5},{5,6},{6,7},{7,8},{8,9},{9,10},{10,1... | collective-permute-start | bytes 12296 | tf_op jit(solution)/shard_map/ppermute | solution.py:24
  46.7 0.5 collective-permute-done.4
  47.4 1.8 collective-permute-start.6
  54.2 2.4 %collective-permute-start.7 = (f32[2,2,2048]{2,1,0:T(2,128)S(1)}, f32[2,2,2048]{2,1,0:T(2,128)S(1)}, u32[]{:S(2)}, u32[]{:S(2)}) collective-permute-start(f32[2,2,2048]{2,1,0:T(2,128)S(1)} %maximum_select_fusion.2), channel_id=1, source_target_pairs={{0,2},{1,3},{2,0},{3,1},{4,6},{5,7},{6,4},{7,5},{8,10},{9,11},{10,... | collective-permute-start | bytes 98312 | tf_op jit(solution)/shard_map/ppermute | solution.py:35
  56.7 0.7 and_reduce_fusion
  60.1 2.2 collective-permute-start.8
  62.3 0.5 select_maximum_fusion.6
  62.8 1.7 collective-permute-done.8
  66.9 1.1 slice_bitcast_fusion.1
  68.0 0.9 fusion.490
  69.2 1.3 copy.54
  71.1 1.1 copy.55
  72.2 1.7 fusion.155
  73.9 1.2 fusion.33
  75.1 1.9 copy.58
  77.0 1.6 copy.59
  78.6 4.4 %fusion.164 = (f32[16,64,128]{2,1,0:T(8,128)S(1)}, f32[16,64,128]{2,1,0:T(8,128)}) fusion(f32[1,16,64,128]{3,2,1,0:T(8,128)} %param.22, f32[16,64,128]{2,1,0:T(8,128)S(1)} %copy.59, f32[1,16,64,128]{3,2,1,0:T(8,128)S(1)} %copy-done.2, f32[24,72,136]{2,1,0:T(8,128)S(1)} %select_maximum_fusion.6, f32[4,64,128]{2,1,0:T(8,128)} %copy-done.11, ...), kind=kLoop, calls=%fused_computation.321 | loop fusion | flops 5373952 | bytes 11796480 | tf_op jit(solution)/shard_map/add | solution.py:205
  83.0 0.6 dynamic-slice.33
  85.7 5.2 %collective-permute-start.11 = (bf16[4,64,128]{2,1,0:T(8,128)(2,1)S(1)}, bf16[4,64,128]{2,1,0:T(8,128)(2,1)S(1)}, u32[]{:S(2)}, u32[]{:S(2)}) collective-permute-start(bf16[4,64,128]{2,1,0:T(8,128)(2,1)S(1)} %get-tuple-element.79), channel_id=1, source_target_pairs={{0,8},{1,9},{2,10},{3,11},{4,12},{5,13},{6,14},{7,15},{16,24},{17,... | collective-permute-start | bytes 196616 | tf_op jit(solution)/shard_map/ppermute | solution.py:45
  90.8 1.3 collective-permute-start.12
  92.1 0.6 collective-permute-done.11
  92.7 5.2 %collective-permute-done.12 = bf16[4,64,128]{2,1,0:T(8,128)(2,1)S(1)} collective-permute-done((bf16[4,64,128]{2,1,0:T(8,128)(2,1)S(1)}, bf16[4,64,128]{2,1,0:T(8,128)(2,1)S(1)}, u32[]{:S(2)}, u32[]{:S(2)}) %collective-permute-start.12) | collective-permute-done | bytes 65568 | tf_op jit(solution)/shard_map/ppermute | solution.py:45
  97.9 0.6 copy-done.13
  99.1 4.2 %multiply_add_fusion.2 = (f32[16,64,128]{2,1,0:T(8,128)S(1)}, f32[16,64,128]{2,1,0:T(8,128)}) fusion(f32[16,64,128]{2,1,0:T(8,128)} %copy-done.3, f32[16,64,128]{2,1,0:T(8,128)S(1)} %scatter-add.14, f32[1,16,64,128]{3,2,1,0:T(8,128)S(1)} %copy-done.2, f32[24,72,136]{2,1,0:T(8,128)S(1)} %select_maximum_fusion.4, f32[4,64,128]{2,1,0:T(8,128)} %copy-done.13, ...), kind=kLoop, calls=%fused_computation.326 | loop fusion | flops 5373952 | bytes 11272192 | tf_op jit(solution)/shard_map/add | solution.py:205
  103.3 0.7 dynamic-slice.34
  106.1 1.6 collective-permute-start.13
  107.7 1.5 collective-permute-start.14
  109.2 0.7 fusion.483
  110.0 1.5 gather_fusion
  111.5 3.3 %collective-permute-done.14 = bf16[4,64,128]{2,1,0:T(8,128)(2,1)S(1)} collective-permute-done((bf16[4,64,128]{2,1,0:T(8,128)(2,1)S(1)}, bf16[4,64,128]{2,1,0:T(8,128)(2,1)S(1)}, u32[]{:S(2)}, u32[]{:S(2)}) %collective-permute-start.14) | collective-permute-done | bytes 65568 | tf_op jit(solution)/shard_map/ppermute | solution.py:45
  114.8 0.6 copy-done.12
  116.0 4.2 %multiply_add_fusion.1 = (f32[16,64,128]{2,1,0:T(8,128)S(1)}, f32[16,64,128]{2,1,0:T(8,128)}) fusion(f32[16,64,128]{2,1,0:T(8,128)} %copy-done.3, f32[16,64,128]{2,1,0:T(8,128)S(1)} %scatter-add.14, f32[16,64,128]{2,1,0:T(8,128)S(1)} %scatter-add.15, f32[24,72,136]{2,1,0:T(8,128)S(1)} %select_maximum_fusion.2, f32[4,64,128]{2,1,0:T(8,128)} %copy-done.12, ...), kind=kLoop, calls=%fused_computation.325 | loop fusion | flops 5373952 | bytes 11272192 | tf_op jit(solution)/shard_map/add | solution.py:205
  120.2 0.7 dynamic-slice.35
  123.0 2.2 collective-permute-start.15
  125.2 1.3 collective-permute-start.16
  126.5 0.7 bitcast_select_fusion.3
  127.2 2.0 copy.63
  129.2 2.4 %copy.64 = f32[16,64,128]{2,1,0:T(8,128)} copy(f32[16,64,128]{1,0,2:T(8,128)} %bitcast.569) | data formatting | bytes 1048576 | tf_op jit(solution)/shard_map/mul | solution.py:216
  131.6 1.5 gather_fusion.1
  133.1 1.5 gather_fusion.2
  134.7 0.5 select_maximum_fusion
  136.0 3.4 %fusion.158 = (f32[16,64,128]{2,1,0:T(8,128)}, f32[16,64,128]{2,1,0:T(8,128)S(1)}) fusion(f32[16,64,128]{2,1,0:T(8,128)S(1)} %copy-done.10, f32[16,64,128]{2,1,0:T(8,128)S(1)} %copy-done.9, f32[16,64,128]{2,1,0:T(8,128)S(1)} %copy-done.8, f32[16,64,128]{2,1,0:T(8,128)S(1)} %copy-done.7, bf16[4,1,16,64,128]{4,3,2,1,0:T(8,128)(2,1)S(1)} %copy-done.14, ...), kind=kLoop, calls=%fused_computation.310 | loop fusion | flops 6422528 | bytes 13369344 | tf_op jit(solution)/shard_map/mul | solution.py:216
  139.6 0.6 dynamic-slice.36
  142.2 1.5 gather_fusion.3
  143.7 1.5 copy.65
  148.5 5.4 %collective-permute-start.18 = (f32[1,2048]{1,0:T(1,128)S(1)}, f32[1,2048]{1,0:T(1,128)S(1)}, u32[]{:S(2)}, u32[]{:S(2)}) collective-permute-start(f32[1,2048]{1,0:T(1,128)S(1)} %get-tuple-element.91), channel_id=1, source_target_pairs={{0,8},{1,9},{2,10},{3,11},{4,12},{5,13},{6,14},{7,15},{16,24},{17,... | collective-permute-start | bytes 24584 | tf_op jit(solution)/shard_map/ppermute | solution.py:45
  153.9 1.3 collective-permute-start.17
  155.3 5.1 %collective-permute-done.17 = f32[1,2048]{1,0:T(1,128)S(1)} collective-permute-done((f32[1,2048]{1,0:T(1,128)S(1)}, f32[1,2048]{1,0:T(1,128)S(1)}, u32[]{:S(2)}, u32[]{:S(2)}) %collective-permute-start.17) | collective-permute-done | bytes 8224 | tf_op jit(solution)/shard_map/ppermute | solution.py:45
  160.5 2.1 collective-permute-start.19
  162.6 1.9 collective-permute-done.19
  164.5 1.8 collective-permute-start.20
  166.4 2.0 collective-permute-done.20
  168.4 59.7 %psum.7 = f32[8,4,128]{2,1,0:T(4,128)} all-reduce(f32[8,4,128]{2,1,0:T(4,128)S(1)} %broadcast_select_fusion.9), channel_id=1, replica_groups=mesh['groups'=2,'slab'=16] {'slab'}, use_global_device_ids=true, to_apply=%region_1.2 | all-reduce | flops 4096 | bytes 32768 | tf_op jit(solution)/shard_map/psum | solution.py:215
  228.1 0.6 fusion.446
  (223 shorter events, 25.7 us)
Async XLA Ops:
  0.6 32.1 %copy-start = (f32[8,4]{0,1:T(4,128)S(1)}, f32[8,4]{0,1:T(4,128)}, u32[]{:S(2)}) copy-start(f32[8,4]{0,1:T(4,128)} %param.25) | copy-start | bytes 388
  0.6 7.1 %copy-start.17 = (bf16[27,64,64]{2,1,0:T(8,128)(2,1)S(1)}, bf16[27,64,64]{2,1,0:T(8,128)(2,1)}, u32[]{:S(2)}) copy-start(bf16[27,64,64]{2,1,0:T(8,128)(2,1)} %param.19) | copy-start | bytes 663556
  0.7 5.6 %collective-permute-start.1 = (bf16[64,1,2048]{2,0,1:T(8,128)(2,1)}, bf16[64,1,2048]{2,0,1:T(8,128)(2,1)S(1)}, u32[]{:S(2)}, u32[]{:S(2)}) collective-permute-start(bf16[64,1,2048]{2,0,1:T(8,128)(2,1)} %param.18), channel_id=1, source_target_pairs={{1,0},{2,1},{3,2},{4,3},{5,4},{6,5},{7,6},{8,7},{9,8},{10,9},{11,1... | collective-permute-start | bytes 786440 | tf_op jit(solution)/shard_map/ppermute | solution.py:27
  2.1 4.4 %collective-permute-start = (bf16[64,1,2048]{2,0,1:T(8,128)(2,1)}, bf16[64,1,2048]{2,0,1:T(8,128)(2,1)S(1)}, u32[]{:S(2)}, u32[]{:S(2)}) collective-permute-start(bf16[64,1,2048]{2,0,1:T(8,128)(2,1)} %param.18), channel_id=1, source_target_pairs={{0,1},{1,2},{2,3},{3,4},{4,5},{5,6},{6,7},{7,8},{8,9},{9,10},{10,1... | collective-permute-start | bytes 786440 | tf_op jit(solution)/shard_map/ppermute | solution.py:24
  11.8 1.0 copy-start.15
  14.9 19.0 %copy-start.16 = (bf16[27,64,64]{2,1,0:T(8,128)(2,1)S(1)}, bf16[27,64,64]{2,1,0:T(8,128)(2,1)}, u32[]{:S(2)}) copy-start(bf16[27,64,64]{2,1,0:T(8,128)(2,1)} %param.20) | copy-start | bytes 663556
  15.2 18.2 %collective-permute-start.3 = (bf16[64,1,2048]{2,0,1:T(8,128)(2,1)S(1)}, bf16[64,1,2048]{2,0,1:T(8,128)(2,1)S(1)}, u32[]{:S(2)}, u32[]{:S(2)}) collective-permute-start(bf16[64,1,2048]{2,0,1:T(8,128)(2,1)S(1)} %bitcast.576), channel_id=1, source_target_pairs={{1,0},{2,1},{3,2},{4,3},{5,4},{6,5},{7,6},{8,7},{9,8},{10,9},{11,1... | collective-permute-start | bytes 786440 | tf_op jit(solution)/shard_map/ppermute | solution.py:27
  16.5 16.9 %collective-permute-start.2 = (bf16[64,1,2048]{2,0,1:T(8,128)(2,1)S(1)}, bf16[64,1,2048]{2,0,1:T(8,128)(2,1)S(1)}, u32[]{:S(2)}, u32[]{:S(2)}) collective-permute-start(bf16[64,1,2048]{2,0,1:T(8,128)(2,1)S(1)} %bitcast.577), channel_id=1, source_target_pairs={{0,1},{1,2},{2,3},{3,4},{4,5},{5,6},{6,7},{7,8},{8,9},{9,10},{10,1... | collective-permute-start | bytes 786440 | tf_op jit(solution)/shard_map/ppermute | solution.py:24
  25.7 34.2 %collective-permute-start.9 = (bf16[4,64,128]{2,1,0:T(8,128)(2,1)S(1)}, bf16[4,64,128]{2,1,0:T(8,128)(2,1)S(1)}, u32[]{:S(2)}, u32[]{:S(2)}) collective-permute-start(bf16[4,64,128]{2,1,0:T(8,128)(2,1)S(1)} %get-tuple-element.81), channel_id=1, source_target_pairs={{0,8},{1,9},{2,10},{3,11},{4,12},{5,13},{6,14},{7,15},{16,24},{17,... | collective-permute-start | bytes 196616 | tf_op jit(solution)/shard_map/ppermute | solution.py:45
  31.4 28.6 %collective-permute-start.10 = (bf16[4,64,128]{2,1,0:T(8,128)(2,1)S(1)}, bf16[4,64,128]{2,1,0:T(8,128)(2,1)S(1)}, u32[]{:S(2)}, u32[]{:S(2)}) collective-permute-start(bf16[4,64,128]{2,1,0:T(8,128)(2,1)S(1)} %get-tuple-element.82), channel_id=1, source_target_pairs={{8,0},{9,1},{10,2},{11,3},{12,4},{13,5},{14,6},{15,7},{24,16},{25,... | collective-permute-start | bytes 196616 | tf_op jit(solution)/shard_map/ppermute | solution.py:45
  40.4 0.9 copy-start.19
  40.7 5.9 %copy-start.18 = (s32[8,3]{0,1:T(4,128)S(1)}, s32[8,3]{0,1:T(4,128)}, u32[]{:S(2)}) copy-start(s32[8,3]{0,1:T(4,128)} %param.26) | copy-start | bytes 292
  40.7 16.0 %copy-start.21 = (s32[3]{0:T(128)S(1)}, s32[3]{0:T(128)}, u32[]{:S(2)}) copy-start(s32[3]{0:T(128)} %constant.246.clone.1) | copy-start | bytes 40
  40.7 21.6 %copy-start.2 = (f32[1,16,64,128]{3,2,1,0:T(8,128)S(1)}, f32[1,16,64,128]{3,2,1,0:T(8,128)}, u32[]{:S(2)}) copy-start(f32[1,16,64,128]{3,2,1,0:T(8,128)} %param.23) | copy-start | bytes 1572868
  41.6 5.0 %collective-permute-start.5 = (bf16[1,2048]{1,0:T(2,128)(2,1)S(1)}, bf16[1,2048]{1,0:T(2,128)(2,1)S(1)}, u32[]{:S(2)}, u32[]{:S(2)}) collective-permute-start(bf16[1,2048]{1,0:T(2,128)(2,1)S(1)} %convert_element_type.266), channel_id=1, source_target_pairs={{1,0},{2,1},{3,2},{4,3},{5,4},{6,5},{7,6},{8,7},{9,8},{10,9},{11,1... | collective-permute-start | bytes 12296 | tf_op jit(solution)/shard_map/ppermute | solution.py:27
  42.9 4.3 %collective-permute-start.4 = (bf16[1,2048]{1,0:T(2,128)(2,1)S(1)}, bf16[1,2048]{1,0:T(2,128)(2,1)S(1)}, u32[]{:S(2)}, u32[]{:S(2)}) collective-permute-start(bf16[1,2048]{1,0:T(2,128)(2,1)S(1)} %convert_element_type.266), channel_id=1, source_target_pairs={{0,1},{1,2},{2,3},{3,4},{4,5},{5,6},{6,7},{7,8},{8,9},{9,10},{10,1... | collective-permute-start | bytes 12296 | tf_op jit(solution)/shard_map/ppermute | solution.py:24
  47.4 6.8 %collective-permute-start.6 = (f32[1,2,2048]{2,1,0:T(2,128)S(1)}, f32[1,2,2048]{2,1,0:T(2,128)S(1)}, u32[]{:S(2)}, u32[]{:S(2)}) collective-permute-start(f32[1,2,2048]{2,1,0:T(2,128)S(1)} %pad_maximum_fusion.12), channel_id=1, source_target_pairs={{0,1},{1,0},{2,3},{3,2},{4,5},{5,4},{6,7},{7,6},{8,9},{9,8},{10,11... | collective-permute-start | bytes 49160 | tf_op jit(solution)/shard_map/ppermute | solution.py:35
  54.2 5.8 %collective-permute-start.7 = (f32[2,2,2048]{2,1,0:T(2,128)S(1)}, f32[2,2,2048]{2,1,0:T(2,128)S(1)}, u32[]{:S(2)}, u32[]{:S(2)}) collective-permute-start(f32[2,2,2048]{2,1,0:T(2,128)S(1)} %maximum_select_fusion.2), channel_id=1, source_target_pairs={{0,2},{1,3},{2,0},{3,1},{4,6},{5,7},{6,4},{7,5},{8,10},{9,11},{10,... | collective-permute-start | bytes 98312 | tf_op jit(solution)/shard_map/ppermute | solution.py:35
  60.0 5.3 %copy-start.11 = (f32[4,64,128]{2,1,0:T(8,128)}, f32[4,64,128]{2,1,0:T(8,128)S(1)}, u32[]{:S(2)}) copy-start(f32[4,64,128]{2,1,0:T(8,128)S(1)} %convert_element_type.271) | copy-start | bytes 393220
  60.1 4.5 %collective-permute-start.8 = (f32[4,2,2048]{2,1,0:T(2,128)S(1)}, f32[4,2,2048]{2,1,0:T(2,128)S(1)}, u32[]{:S(2)}, u32[]{:S(2)}) collective-permute-start(f32[4,2,2048]{2,1,0:T(2,128)S(1)} %maximum_select_fusion.1), channel_id=1, source_target_pairs={{0,4},{1,5},{2,6},{3,7},{4,0},{5,1},{6,2},{7,3},{8,12},{9,13},{10,... | collective-permute-start | bytes 196616 | tf_op jit(solution)/shard_map/ppermute | solution.py:35
  78.6 4.4 %copy-start.3 = (f32[16,64,128]{2,1,0:T(8,128)}, f32[16,64,128]{2,1,0:T(8,128)S(1)}, u32[]{:S(2)}) copy-start(f32[16,64,128]{2,1,0:T(8,128)S(1)} %copy.59) | copy-start | bytes 1572868
  85.7 7.1 %collective-permute-start.11 = (bf16[4,64,128]{2,1,0:T(8,128)(2,1)S(1)}, bf16[4,64,128]{2,1,0:T(8,128)(2,1)S(1)}, u32[]{:S(2)}, u32[]{:S(2)}) collective-permute-start(bf16[4,64,128]{2,1,0:T(8,128)(2,1)S(1)} %get-tuple-element.79), channel_id=1, source_target_pairs={{0,8},{1,9},{2,10},{3,11},{4,12},{5,13},{6,14},{7,15},{16,24},{17,... | collective-permute-start | bytes 196616 | tf_op jit(solution)/shard_map/ppermute | solution.py:45
  90.8 7.1 %collective-permute-start.12 = (bf16[4,64,128]{2,1,0:T(8,128)(2,1)S(1)}, bf16[4,64,128]{2,1,0:T(8,128)(2,1)S(1)}, u32[]{:S(2)}, u32[]{:S(2)}) collective-permute-start(bf16[4,64,128]{2,1,0:T(8,128)(2,1)S(1)} %get-tuple-element.80), channel_id=1, source_target_pairs={{8,0},{9,1},{10,2},{11,3},{12,4},{13,5},{14,6},{15,7},{24,16},{25,... | collective-permute-start | bytes 196616 | tf_op jit(solution)/shard_map/ppermute | solution.py:45
  97.9 0.7 copy-start.13
  106.1 5.3 %collective-permute-start.13 = (bf16[4,64,128]{2,1,0:T(8,128)(2,1)S(1)}, bf16[4,64,128]{2,1,0:T(8,128)(2,1)S(1)}, u32[]{:S(2)}, u32[]{:S(2)}) collective-permute-start(bf16[4,64,128]{2,1,0:T(8,128)(2,1)S(1)} %get-tuple-element.77), channel_id=1, source_target_pairs={{0,8},{1,9},{2,10},{3,11},{4,12},{5,13},{6,14},{7,15},{16,24},{17,... | collective-permute-start | bytes 196616 | tf_op jit(solution)/shard_map/ppermute | solution.py:45
  107.7 7.1 %collective-permute-start.14 = (bf16[4,64,128]{2,1,0:T(8,128)(2,1)S(1)}, bf16[4,64,128]{2,1,0:T(8,128)(2,1)S(1)}, u32[]{:S(2)}, u32[]{:S(2)}) collective-permute-start(bf16[4,64,128]{2,1,0:T(8,128)(2,1)S(1)} %get-tuple-element.78), channel_id=1, source_target_pairs={{8,0},{9,1},{10,2},{11,3},{12,4},{13,5},{14,6},{15,7},{24,16},{25,... | collective-permute-start | bytes 196616 | tf_op jit(solution)/shard_map/ppermute | solution.py:45
  114.8 0.7 copy-start.12
  120.1 7.1 %copy-start.5 = (f32[16,64,64,2]{2,0,1,3:T(8,128)S(1)}, f32[16,64,64,2]{2,0,1,3:T(8,128)}, u32[]{:S(2)}) copy-start(f32[16,64,64,2]{2,0,1,3:T(8,128)} %get-tuple-element.63) | copy-start | bytes 1572868
  123.0 11.6 %collective-permute-start.15 = (bf16[4,64,128]{2,1,0:T(8,128)(2,1)S(1)}, bf16[4,64,128]{2,1,0:T(8,128)(2,1)S(1)}, u32[]{:S(2)}, u32[]{:S(2)}) collective-permute-start(bf16[4,64,128]{2,1,0:T(8,128)(2,1)S(1)} %get-tuple-element.75), channel_id=1, source_target_pairs={{0,8},{1,9},{2,10},{3,11},{4,12},{5,13},{6,14},{7,15},{16,24},{17,... | collective-permute-start | bytes 196616 | tf_op jit(solution)/shard_map/ppermute | solution.py:45
  125.2 9.4 %collective-permute-start.16 = (bf16[4,64,128]{2,1,0:T(8,128)(2,1)S(1)}, bf16[4,64,128]{2,1,0:T(8,128)(2,1)S(1)}, u32[]{:S(2)}, u32[]{:S(2)}) collective-permute-start(bf16[4,64,128]{2,1,0:T(8,128)(2,1)S(1)} %get-tuple-element.76), channel_id=1, source_target_pairs={{8,0},{9,1},{10,2},{11,3},{12,4},{13,5},{14,6},{15,7},{24,16},{25,... | collective-permute-start | bytes 196616 | tf_op jit(solution)/shard_map/ppermute | solution.py:45
  133.1 2.1 copy-start.7
  133.1 2.1 copy-start.8
  133.1 2.1 copy-start.9
  134.6 1.0 copy-start.10
  134.6 1.4 copy-start.14
  136.0 3.4 %copy-start.4 = (f32[16,64,128]{2,1,0:T(8,128)S(1)}, f32[16,64,128]{2,1,0:T(8,128)}, u32[]{:S(2)}) copy-start(f32[16,64,128]{2,1,0:T(8,128)} %copy-done.3) | copy-start | bytes 1572868
  142.2 3.1 %copy-start.6 = (f32[16,64,128]{2,1,0:T(8,128)}, f32[16,64,128]{2,1,0:T(8,128)S(1)}, u32[]{:S(2)}) copy-start(f32[16,64,128]{2,1,0:T(8,128)S(1)} %scatter-add.19) | copy-start | bytes 1572868
  146.1 0.7 copy-start.22
  147.1 0.7 copy-start.20
  147.4 81.3 %copy-start.1 = (f32[8,4]{0,1:T(4,128)S(1)}, f32[8,4]{0,1:T(4,128)}, u32[]{:S(2)}) copy-start(f32[8,4]{0,1:T(4,128)} %param.25) | copy-start | bytes 388
  148.5 6.8 %collective-permute-start.18 = (f32[1,2048]{1,0:T(1,128)S(1)}, f32[1,2048]{1,0:T(1,128)S(1)}, u32[]{:S(2)}, u32[]{:S(2)}) collective-permute-start(f32[1,2048]{1,0:T(1,128)S(1)} %get-tuple-element.91), channel_id=1, source_target_pairs={{0,8},{1,9},{2,10},{3,11},{4,12},{5,13},{6,14},{7,15},{16,24},{17,... | collective-permute-start | bytes 24584 | tf_op jit(solution)/shard_map/ppermute | solution.py:45
  153.9 6.4 %collective-permute-start.17 = (f32[1,2048]{1,0:T(1,128)S(1)}, f32[1,2048]{1,0:T(1,128)S(1)}, u32[]{:S(2)}, u32[]{:S(2)}) collective-permute-start(f32[1,2048]{1,0:T(1,128)S(1)} %get-tuple-element.92), channel_id=1, source_target_pairs={{8,0},{9,1},{10,2},{11,3},{12,4},{13,5},{14,6},{15,7},{24,16},{25,... | collective-permute-start | bytes 24584 | tf_op jit(solution)/shard_map/ppermute | solution.py:45
  160.5 4.0 %collective-permute-start.19 = (f32[4,1,2048]{2,0,1:T(4,128)S(1)}, f32[4,1,2048]{2,0,1:T(4,128)S(1)}, u32[]{:S(2)}, u32[]{:S(2)}) collective-permute-start(f32[4,1,2048]{2,0,1:T(4,128)S(1)} %select_bitcast_fusion), channel_id=1, source_target_pairs={{0,4},{1,5},{2,6},{3,7},{4,0},{5,1},{6,2},{7,3},{8,12},{9,13},{10,... | collective-permute-start | bytes 98312 | tf_op jit(solution)/shard_map/ppermute | solution.py:35
  164.5 3.8 %collective-permute-start.20 = (f32[2,1,2048]{2,0,1:T(2,128)S(1)}, f32[2,1,2048]{2,0,1:T(2,128)S(1)}, u32[]{:S(2)}, u32[]{:S(2)}) collective-permute-start(f32[2,1,2048]{2,0,1:T(2,128)S(1)} %broadcast_select_fusion.4), channel_id=1, source_target_pairs={{0,2},{1,3},{2,0},{3,1},{4,6},{5,7},{6,4},{7,5},{8,10},{9,11},{10,... | collective-permute-start | bytes 49160 | tf_op jit(solution)/shard_map/ppermute | solution.py:35
  168.3 59.8 %collective-permute-start.21 = (f32[1,1,2048]{2,0,1:T(1,128)S(1)}, f32[1,1,2048]{2,0,1:T(1,128)S(1)}, u32[]{:S(2)}, u32[]{:S(2)}) collective-permute-start(f32[1,1,2048]{2,0,1:T(1,128)S(1)} %broadcast_select_fusion.5), channel_id=1, source_target_pairs={{0,1},{1,0},{2,3},{3,2},{4,5},{5,4},{6,7},{7,6},{8,9},{9,8},{10,11... | collective-permute-start | bytes 24584 | tf_op jit(solution)/shard_map/ppermute | solution.py:35
where the time goes:
time: 230 us; the launch traced here: 229 us
  blocking collectives  59.7 us (26%)
  starting transfers between devices  56.9 us (25%)
  local copies, waits for them, and re-layouts  31.1 us (14%)
  other arithmetic  28.9 us (13%)
  waiting for transfers between devices  20.4 us (9%)
  between operations  16.9 us (7%)
  matrix products  14.7 us (6%)
    psum x1, blocking collectives, body(): traces = lax.psum(own_traces, 'slab')  59.7 us
    ppermute x10, starting transfers between devices, from_behind(): lax.ppermute(value, axis, [(source, source + steps) for source in range(l...  26.7 us
    ppermute x3, starting transfers between devices, extended_2(): lax.ppermute(lax.slice_in_dim(block, block.shape[dim] - width, None, axis...  15.9 us
    dot_general x54, matrix products, conv_taps(): jnp.einsum('oi,izn->ozn', weight[tap_index], piece * column_valid, prefer...  14.4 us
    ppermute x10, waiting for transfers between devices, from_behind(): lax.ppermute(value, axis, [(source, source + steps) for source in range(l...  14.1 us
    add x4, other arithmetic, body(): advanced = 2.0 * current - previous + courant_sq * laplace_term  12.9 us
    ppermute x6, starting transfers between devices, from_partner(): return lax.ppermute(value, axis, pairs)  10.4 us
    gather x4, local copies, waits for them, and re-layouts, body(): advanced[station_depth, station[1], station[2]]  5.93 us
  transfers between devices with their start and end apart: 22, of which 9 were waited for; matrix products, arithmetic and copies ran while one was open for 10% of the time, Pallas kernels for 0%

commit v1 on v0

v1 whole, which is shorter than its diff:
```python
import functools

import jax
import jax.numpy as jnp
import numpy as np
from jax import lax
from jax.experimental import pallas as pl
from jax.experimental.pallas import tpu as pltpu
from jax.sharding import PartitionSpec as P

CH = 64
CY = 32
CX = 64
FY = 64
FX = 128
CELLS = CY * CX
SHOTS = 8
STEPS = 4
NREC = 128
PLANES = 16
REACH = 4
CUR_RIM = REACH * STEPS
PREV_RIM = CUR_RIM - REACH
RIM_PLANES = CUR_RIM + PREV_RIM
EXT = PLANES + 2 * CUR_RIM
PAD = 8
ROWS = FY + 2 * PAD

stencil_weights = (-205.0 / 72.0, 8.0 / 5.0, -1.0 / 5.0, 8.0 / 315.0, -1.0 / 560.0)
lowest_speed = 1.5
speed_range = 3.0
courant = 0.088
leak_slope = 0.2

VMEM = pl.BlockSpec(memory_space=pltpu.VMEM)
SMEM = pl.BlockSpec(memory_space=pltpu.SMEM)
PARAMS = pltpu.CompilerParams(vmem_limit_bytes=48 * 1024 * 1024)


def doubling_matrix(length):
    matrix = np.zeros((2 * length, length), np.float32)
    for k in range(length):
        matrix[2 * k, k] += 0.75
        matrix[2 * k, max(k - 1, 0)] += 0.25
        matrix[2 * k + 1, k] += 0.75
        matrix[2 * k + 1, min(k + 1, length - 1)] += 0.25
    return matrix


def plane_matrices():
    across = doubling_matrix(CX)
    down = doubling_matrix(CY)
    widen = np.zeros((128, 256), np.float32)
    widen[:64, :128] = across.T
    widen[64:, 128:] = across.T
    tall = np.concatenate([down[:, 0::2], down[:, 1::2]], axis=1)
    tall_twice = np.concatenate([tall, tall], axis=1)
    short_twice = np.concatenate([tall.T, tall.T], axis=1)
    narrow = widen.T
    return tuple(jnp.asarray(m, jnp.bfloat16) for m in (widen, tall_twice, short_twice, narrow))


def halves(value):
    high = value.astype(jnp.bfloat16)
    low = (value - high.astype(jnp.float32)).astype(jnp.bfloat16)
    return high, low


def leaky(value):
    return jnp.where(value > 0, value, leak_slope * value)


def conv(low_ref, mid_ref, high_ref, weight_ref, fields, packed):
    column = lax.broadcasted_iota(jnp.int32, (CH, CELLS), 1) % CX
    for depth, ref in enumerate((low_ref, mid_ref, high_ref)):
        plane = ref[...]
        wide = plane.astype(jnp.float32)
        left = jnp.where(column == 0, 0.0, pltpu.roll(wide, 1, 1)).astype(jnp.bfloat16)
        right = jnp.where(column == CX - 1, 0.0, pltpu.roll(wide, CELLS - 1, 1)).astype(jnp.bfloat16)
        for place, piece in enumerate((left, plane, right)):
            begin = (3 * depth + place) * CH
            fields[begin : begin + CH, :] = piece
    for depth in range(3):
        for row in range(3):
            for place in range(3):
                tap = 9 * depth + 3 * row + place
                begin = (3 * depth + place) * CH
                packed[row * CH : (row + 1) * CH, begin : begin + CH] = weight_ref[tap]
    products = jnp.dot(packed[...], fields[...], preferred_element_type=jnp.float32)
    cell = lax.broadcasted_iota(jnp.int32, (CH, CELLS), 1)
    above = jnp.where(cell < CX, 0.0, pltpu.roll(products[:CH], CX, 1))
    below = jnp.where(cell >= CELLS - CX, 0.0, pltpu.roll(products[2 * CH :], CELLS - CX, 1))
    return products[CH : 2 * CH] + above + below


def first_kernel(low_ref, mid_ref, high_ref, weight_ref, out_ref, fields, packed):
    out_ref[...] = leaky(conv(low_ref, mid_ref, high_ref, weight_ref, fields, packed)).astype(
        jnp.bfloat16
    )


def second_kernel(low_ref, mid_ref, high_ref, weight_ref, head_ref, out_ref, fields, packed):
    second = leaky(conv(low_ref, mid_ref, high_ref, weight_ref, fields, packed))
    logits = jnp.sum(second * head_ref[...], axis=0, keepdims=True)
    speed = lowest_speed + speed_range * jax.nn.sigmoid(logits)
    for j in range(16):
        out_ref[j : j + 1, :] = speed[:, 128 * j : 128 * (j + 1)].astype(jnp.bfloat16)


CONV_SCRATCH = [
    pltpu.VMEM((9 * CH, CELLS), jnp.bfloat16),
    pltpu.VMEM((3 * CH, 9 * CH), jnp.bfloat16),
]


def first_conv(low, mid, high, weight):
    return pl.pallas_call(
        first_kernel,
        out_shape=jax.ShapeDtypeStruct((CH, CELLS), jnp.bfloat16),
        in_specs=[VMEM] * 4,
        out_specs=VMEM,
        scratch_shapes=CONV_SCRATCH,
        compiler_params=PARAMS,
    )(low, mid, high, weight)


def second_conv(low, mid, high, weight, head):
    return pl.pallas_call(
        second_kernel,
        out_shape=jax.ShapeDtypeStruct((16, 128), jnp.bfloat16),
        in_specs=[VMEM] * 5,
        out_specs=VMEM,
        scratch_shapes=CONV_SCRATCH,
        compiler_params=PARAMS,
    )(low, mid, high, weight, head)


def laplace(field, plane, lane):
    middle = field[plane, PAD : PAD + FY, :]
    total = (3.0 * stencil_weights[0]) * middle
    for reach in range(1, REACH + 1):
        near = field[plane - reach, PAD : PAD + FY, :] + field[plane + reach, PAD : PAD + FY, :]
        near = near + field[plane, PAD - reach : PAD - reach + FY, :]
        near = near + field[plane, PAD + reach : PAD + reach + FY, :]
        near = near + jnp.where(lane < reach, 0.0, pltpu.roll(middle, reach, 1))
        near = near + jnp.where(lane >= FX - reach, 0.0, pltpu.roll(middle, FX - reach, 1))
        total = total + stencil_weights[reach] * near
    return total


def wave_kernel(
    info,
    pulses,
    stations,
    cur_ref,
    prev_ref,
    low_rim,
    high_rim,
    adjoint_ref,
    own_speed,
    low_speed,
    high_speed,
    pick_ref,
    widen_ref,
    tall_ref,
    short_ref,
    narrow_ref,
    final_ref,
    terms_ref,
    edges_ref,
    records_ref,
    field_a,
    field_b,
    factor,
    coarse,
    speed,
    total,
    rows,
):
    shot = info[0]
    has_low = info[1] == 1
    has_high = info[2] == 1
    lane = lax.broadcasted_iota(jnp.int32, (FY, FX), 1)

    def clear(plane, _):
        for field in (field_a, field_b):
            field[plane, :PAD, :] = jnp.zeros((PAD, FX), jnp.float32)
            field[plane, PAD + FY :, :] = jnp.zeros((PAD, FX), jnp.float32)
        return 0

    lax.fori_loop(0, EXT, clear, 0)
    inner = slice(PAD, PAD + FY)

    def load_own(plane, _):
        field_a[CUR_RIM + plane, inner, :] = cur_ref[plane]
        field_b[CUR_RIM + plane, inner, :] = prev_ref[plane]
        return 0

    lax.fori_loop(0, PLANES, load_own, 0)

    def load_rim(rim, at_cur, at_prev):
        def one(plane, _):
            field_a[at_cur + plane, inner, :] = rim[plane].astype(jnp.float32)
            return 0

        lax.fori_loop(0, CUR_RIM, one, 0)

        def two(plane, _):
            field_b[at_prev + plane, inner, :] = rim[CUR_RIM + plane].astype(jnp.float32)
            return 0

        lax.fori_loop(0, PREV_RIM, two, 0)

    def no_rim(at):
        def one(plane, _):
            for field in (field_a, field_b):
                field[at + plane, inner, :] = jnp.zeros((FY, FX), jnp.float32)
            return 0

        lax.fori_loop(0, REACH, one, 0)

    @pl.when(has_low)
    def _():
        load_rim(low_rim, 0, REACH)

    @pl.when(jnp.logical_not(has_low))
    def _():
        no_rim(CUR_RIM - REACH)

    @pl.when(has_high)
    def _():
        load_rim(high_rim, CUR_RIM + PLANES, CUR_RIM + PLANES)

    @pl.when(jnp.logical_not(has_high))
    def _():
        no_rim(CUR_RIM + PLANES)

    def widen_block(ref, at):
        block = ref[...].reshape(SHOTS * 16, 128)
        wide = jnp.dot(block, widen_ref[...], preferred_element_type=jnp.float32)
        for j in range(SHOTS):
            piece = wide[16 * j : 16 * (j + 1)]
            both = jnp.concatenate([piece[:, :128], piece[:, 128:]], axis=0)
            high, low = halves(both)
            stacked = jnp.concatenate([high, low], axis=0)
            coarse[at + (shot ^ j)] = jnp.dot(
                tall_ref[...], stacked, preferred_element_type=jnp.float32
            )

    widen_block(own_speed, SHOTS)

    @pl.when(has_low)
    def _():
        widen_block(low_speed, 0)

    @pl.when(jnp.logical_not(has_low))
    def _():
        coarse[SHOTS - 1] = coarse[SHOTS]

    @pl.when(has_high)
    def _():
        widen_block(high_speed, 2 * SHOTS)

    @pl.when(jnp.logical_not(has_high))
    def _():
        coarse[2 * SHOTS] = coarse[2 * SHOTS - 1]

    low_count = jnp.where(has_low, 1, 0)
    high_count = jnp.where(has_high, 1, 0)

    def refine(k, _):
        here = 0.75 * coarse[k]
        even = here + 0.25 * coarse[k - 1]
        odd = here + 0.25 * coarse[k + 1]
        speed[2 * k] = even
        speed[2 * k + 1] = odd
        factor[2 * k] = (courant * even) * (courant * even)
        factor[2 * k + 1] = (courant * odd) * (courant * odd)
        return 0

    lax.fori_loop(
        SHOTS - low_count * (PREV_RIM // 2),
        2 * SHOTS + high_count * (PREV_RIM // 2),
        refine,
        0,
    )

    source_plane = info[3] + CUR_RIM
    source_row = info[4] + PAD
    source_column = info[5]
    lane_row = lax.broadcasted_iota(jnp.int32, (1, FX), 1)

    for step in range(STEPS):
        now, other = (field_a, field_b) if step % 2 == 0 else (field_b, field_a)
        reach_out = CUR_RIM - REACH * (step + 1)

        def advance(plane, lap):
            other[plane, inner, :] = (
                2.0 * now[plane, inner, :] - other[plane, inner, :] + factor[plane] * lap
            )

        def rim_plane(plane, _):
            advance(plane, laplace(now, plane, lane))
            return 0

        def own_plane(plane, _):
            lap = laplace(now, plane + CUR_RIM, lane)
            term = adjoint_ref[step, plane].astype(jnp.float32) * lap
            if step == 0:
                total[plane] = term
            else:
                total[plane] = total[plane] + term
            advance(plane + CUR_RIM, lap)
            return 0

        first = CUR_RIM - low_count * reach_out
        last = CUR_RIM + PLANES + high_count * reach_out
        if reach_out > 0:
            lax.fori_loop(first, CUR_RIM, rim_plane, 0)
        lax.fori_loop(0, PLANES, own_plane, 0)
        if reach_out > 0:
            lax.fori_loop(CUR_RIM + PLANES, last, rim_plane, 0)

        @pl.when((source_plane >= first) & (source_plane < last))
        def _():
            cell = other[source_plane, pl.ds(source_row, 1), :]
            other[source_plane, pl.ds(source_row, 1), :] = cell + jnp.where(
                lane_row == source_column, pulses[step], 0.0
            )

        def collect(k, _):
            rows[pl.ds(k, 1), :] = other[stations[0, k], pl.ds(stations[1, k], 1), :]
            return 0

        lax.fori_loop(0, NREC, collect, 0, unroll=8)
        records_ref[step : step + 1, :] = jnp.sum(
            (rows[...] * pick_ref[...]).T, axis=0, keepdims=True
        )

    result = field_a if STEPS % 2 == 0 else field_b

    def store(plane, _):
        final_ref[plane] = result[CUR_RIM + plane, inner, :]
        return 0

    lax.fori_loop(0, PLANES, store, 0)

    def scale(plane, _):
        total[plane] = (2.0 * courant * courant) * speed[CUR_RIM + plane] * total[plane]
        return 0

    lax.fori_loop(0, PLANES, scale, 0)

    shrunk = []
    for k in range(-1, SHOTS + 1):
        value = 0.0
        for plane, weight in ((2 * k - 1, 0.25), (2 * k, 0.75), (2 * k + 1, 0.75), (2 * k + 2, 0.25)):
            if 0 <= plane < PLANES:
                value = value + weight * total[plane]
        high, low = halves(value)
        stacked = jnp.concatenate([high, low], axis=0)
        shrunk.append(jnp.dot(short_ref[...], stacked, preferred_element_type=jnp.float32))
    sides = [jnp.concatenate([z[:16], z[16:]], axis=1) for z in shrunk]
    high, low = halves(jnp.concatenate(sides, axis=0))
    narrow = narrow_ref[...]
    out = jnp.dot(high, narrow, preferred_element_type=jnp.float32) + jnp.dot(
        low, narrow, preferred_element_type=jnp.float32
    )
    below = out[:16]
    above = out[16 * (SHOTS + 1) :]
    for k in range(SHOTS):
        piece = out[16 * (k + 1) : 16 * (k + 2)]
        if k == 0:
            piece = piece + jnp.where(has_low, 0.0, below)
        if k == SHOTS - 1:
            piece = piece + jnp.where(has_high, 0.0, above)
        terms_ref[shot ^ k] = piece
    edges_ref[0] = jnp.where(has_low, below, 0.0)
    edges_ref[1] = jnp.where(has_high, above, 0.0)


def wave(*args):
    return pl.pallas_call(
        wave_kernel,
        out_shape=(
            jax.ShapeDtypeStruct((PLANES, FY, FX), jnp.float32),
            jax.ShapeDtypeStruct((SHOTS, 16, 128), jnp.float32),
            jax.ShapeDtypeStruct((2, 16, 128), jnp.float32),
            jax.ShapeDtypeStruct((STEPS, NREC), jnp.float32),
        ),
        in_specs=[SMEM] * 3 + [VMEM] * 13,
        out_specs=(VMEM,) * 4,
        scratch_shapes=[
            pltpu.VMEM((EXT, ROWS, FX), jnp.float32),
            pltpu.VMEM((EXT, ROWS, FX), jnp.float32),
            pltpu.VMEM((EXT, FY, FX), jnp.float32),
            pltpu.VMEM((3 * SHOTS, FY, FX), jnp.float32),
            pltpu.VMEM((EXT, FY, FX), jnp.float32),
            pltpu.VMEM((PLANES, FY, FX), jnp.float32),
            pltpu.VMEM((NREC, FX), jnp.float32),
        ],
        compiler_params=PARAMS,
    )(*args)


def finish_kernel(info, term_ref, records_ref, gradient_ref, traces_ref):
    shot = info[0]
    for j in range(16):
        gradient_ref[:, 128 * j : 128 * (j + 1)] = term_ref[j : j + 1, :]
    for j in range(SHOTS):
        traces_ref[shot ^ j] = records_ref[j]


def finish(info, term, records):
    return pl.pallas_call(
        finish_kernel,
        out_shape=(
            jax.ShapeDtypeStruct((1, CELLS), jnp.float32),
            jax.ShapeDtypeStruct((SHOTS, STEPS, NREC), jnp.float32),
        ),
        in_specs=[SMEM, VMEM, VMEM],
        out_specs=(VMEM, VMEM),
        compiler_params=PARAMS,
    )(info, term, records)


def shift(value, steps):
    count = lax.axis_size("slab")
    begin, end = max(0, -steps), min(count, count - steps)
    return lax.ppermute(value, "slab", [(source, source + steps) for source in range(begin, end)])


def partner(value, mask):
    count = lax.axis_size("slab")
    return lax.ppermute(value, "slab", [(source, source ^ mask) for source in range(count)])


def body(
    latent, conv1_weight, conv2_weight, head, p_prev, p_cur, adjoint, wavelet, sources, receivers
):
    position = lax.axis_index("slab")
    devices = lax.axis_size("slab")
    slabs = devices // SHOTS
    shot = position % SHOTS
    slab = position // SHOTS
    has_low = slab > 0
    has_high = slab < slabs - 1

    def exchange(to_low, to_high):
        if slabs == 2:
            got = partner(to_low if to_low is to_high else jnp.where(has_low, to_low, to_high), SHOTS)
            return got, got
        return shift(to_high, SHOTS), shift(to_low, -SHOTS)

    latent = latent.reshape(CH, CELLS)
    latent_low, latent_high = shift(latent, 1), shift(latent, -1)

    current = p_cur[0]
    previous = p_prev[0]
    rim_low, rim_high = exchange(
        jnp.concatenate([current, previous[:PREV_RIM]], axis=0).astype(jnp.bfloat16),
        jnp.concatenate([current, previous[PLANES - PREV_RIM :]], axis=0).astype(jnp.bfloat16),
    )

    hidden = first_conv(latent_low, latent, latent_high, conv1_weight)
    hidden_low, hidden_high = shift(hidden, 1), shift(hidden, -1)
    velocity = second_conv(
        hidden_low, hidden, hidden_high, conv2_weight, head.astype(jnp.float32)[:, None]
    )

    block = velocity[None]
    for bit in range(3):
        block = jnp.concatenate([block, partner(block, 1 << bit)], axis=0)
    speed_low, speed_high = exchange(block, block)

    source = lax.dynamic_index_in_dim(sources, shot, 0, keepdims=False)
    station = lax.dynamic_index_in_dim(receivers, shot, 0, keepdims=False)
    pulses = lax.dynamic_index_in_dim(wavelet, shot, 0, keepdims=False)
    offset = slab * PLANES
    info = jnp.stack(
        [
            shot,
            has_low.astype(jnp.int32),
            has_high.astype(jnp.int32),
            source[0] - offset,
            source[1],
            source[2],
        ]
    )
    depth = station[0] - offset
    inside = (depth >= 0) & (depth < PLANES)
    stations = jnp.stack([jnp.clip(depth, 0, PLANES - 1) + CUR_RIM, station[1] + PAD])
    pick = (
        (station[2][:, None] == jnp.arange(FX)[None, :]) & inside[:, None]
    ).astype(jnp.float32)
    final, terms, edges, record = wave(
        info,
        pulses,
        stations,
        current,
        previous,
        rim_low,
        rim_high,
        adjoint[:, 0],
        block,
        speed_low,
        speed_high,
        pick,
        *plane_matrices(),
    )

    if slabs == 2:
        message = jnp.concatenate([jnp.where(has_low, edges[0], edges[1]), record], axis=0)
        got = partner(message, SHOTS)
        edge_low = jnp.where(has_low, got[:16], 0.0)
        edge_high = jnp.where(has_high, got[:16], 0.0)
        record = record + got[16:]
    else:
        edge_low, edge_high = shift(edges[1], SHOTS), shift(edges[0], -SHOTS)
        mask = SHOTS
        while mask < devices:
            record = record + partner(record, mask)
            mask *= 2
    place = jnp.arange(SHOTS)[:, None, None]
    terms = terms + jnp.where(place == shot, edge_low, 0.0)
    terms = terms + jnp.where(place == shot ^ (SHOTS - 1), edge_high, 0.0)
    terms = terms.reshape(SHOTS * 16, 128)
    records = record
    for bit in reversed(range(3)):
        half = terms.shape[0] // 2
        size = records.shape[0]
        got = partner(jnp.concatenate([terms[half:], records], axis=0), 1 << bit)
        terms = terms[:half] + got[:half]
        records = jnp.concatenate([records, got[half:]], axis=0)
    order = [4 * (j & 1) + (j & 2) + (j >> 2) for j in range(SHOTS)]
    records = records.reshape(SHOTS, STEPS, NREC)
    records = jnp.stack([records[order.index(j)] for j in range(SHOTS)])
    gradient, traces = finish(info, terms, records)
    return (final[None], traces, gradient)


def solution(mesh):
    in_specs = (
        P(None, ("groups", "slab"), None),
        P(),
        P(),
        P(),
        P(("groups", "slab"), None, None, None),
        P(("groups", "slab"), None, None, None),
        P(None, ("groups", "slab"), None, None, None),
        P("groups", None),
        P("groups", None),
        P("groups", None, None),
    )
    out_specs = (
        P(("groups", "slab"), None, None, None),
        P("groups", None, None),
        P(("groups", "slab"), None),
    )
    return jax.shard_map(body, mesh=mesh, in_specs=in_specs, out_specs=out_specs, check_vma=False)
```

time: 230 us -> 89.4 us (0.39)
  blocking collectives: 59.7 us -> 0 us
  local copies, waits for them, and re-layouts: 31.1 us -> 5.54 us
  other arithmetic: 28.9 us -> 3.64 us
  Pallas kernels: 0 us -> 22.6 us
  between operations: 16.9 us -> 1.65 us
  matrix products: 14.7 us -> 0 us
  starting transfers between devices: 56.9 us -> 43.9 us
  waiting for transfers between devices: 20.4 us -> 11.6 us
    psum x1 -> x0, blocking collectives: 59.7 us -> none  [body(): traces = lax.psum(own_traces, 'slab')]
    pallas_call x0 -> x4, Pallas kernels: none -> 22.6 us  [the longest x1 17.9 us: wave(): pl.pallas_call(wave_kernel, out_shape=(jax.ShapeDtypeStruct((PLANES, FY,...]
    add x9 -> x4, other arithmetic: 14.8 us -> 0.1 us  [the longest x1 0.09 us: body(): terms = terms + jnp.where(place == shot ^ SHOTS - 1, edge_high, 0.0)]
    dot_general x55 -> x0, matrix products: 14.7 us -> none  [the longest x54 14.4 us: conv_taps(): jnp.einsum('oi,izn->ozn', weight[tap_index], piece * column_valid, prefer...]
    ppermute x22 -> x13, starting transfers between devices: 56.9 us -> 43.9 us  [the longest x9 36.5 us: partner(): lax.ppermute(value, 'slab', [(source, source ^ mask) for source in range(...]
    ppermute x22 -> x13, waiting for transfers between devices: 20.4 us -> 11.6 us  [the longest x9 11.5 us: partner(): lax.ppermute(value, 'slab', [(source, source ^ mask) for source in range(...]
    mul x4 -> x0, local copies, waits for them, and re-layouts: 6.2 us -> none  [the longest x3 5.89 us: body(): fine_gradient = 2.0 * courant * courant * fine_speed * correlation]
    gather x4 -> x0, local copies, waits for them, and re-layouts: 5.93 us -> none  [body(): advanced[station_depth, station[1], station[2]]]
  transfers between devices with their start and end apart: 22 -> 13, of which waited for: 9 -> 9; matrix products, arithmetic and copies ran while one was open for 10% -> 7% of each run, Pallas kernels for 0% -> 4%
where the time goes in v1:
time: 89.4 us; the launch traced here: 88.9 us
  starting transfers between devices  43.9 us (49%)
  Pallas kernels  22.6 us (25%)
  waiting for transfers between devices  11.6 us (13%)
  local copies, waits for them, and re-layouts  5.54 us (6%)
  other arithmetic  3.64 us (4%)
  between operations  1.65 us (2%)
    ppermute x9, starting transfers between devices, partner(): lax.ppermute(value, 'slab', [(source, source ^ mask) for source in range(...  36.5 us
    pallas_call x1, Pallas kernels, wave(): pl.pallas_call(wave_kernel, out_shape=(jax.ShapeDtypeStruct((PLANES, FY,...  17.9 us
    ppermute x9, waiting for transfers between devices, partner(): lax.ppermute(value, 'slab', [(source, source ^ mask) for source in range(...  11.5 us
    ppermute x4, starting transfers between devices, shift(): lax.ppermute(value, 'slab', [(source, source + steps) for source in range...  7.42 us
    unnamed x34, local copies, waits for them, and re-layouts  2.59 us
    pallas_call x1, Pallas kernels, second_conv(): pl.pallas_call(second_kernel, out_shape=jax.ShapeDtypeStruct((16, 128), j...  2.24 us
  transfers between devices with their start and end apart: 13, of which 9 were waited for; matrix products, arithmetic and copies ran while one was open for 7% of the time, Pallas kernels for 4%

profile of v1, /device:TPU:0, one launch (start us, length us, event | category | flops | bytes accessed | tf_op | source)
XLA Modules:
  0.0 88.9 jit_solution(2977011720089171066)
XLA Ops:
  0.6 0.0 copy-start
  0.6 0.0 copy-start.1
  0.7 2.5 %collective-permute-start.1 = (bf16[64,2048]{1,0:T(8,128)(2,1)}, bf16[64,2048]{1,0:T(8,128)(2,1)S(1)}, u32[]{:S(2)}, u32[]{:S(2)}) collective-permute-start(bf16[64,2048]{1,0:T(8,128)(2,1)} %bitcast.65), channel_id=1, source_target_pairs={{0,1},{1,2},{2,3},{3,4},{4,5},{5,6},{6,7},{7,8},{8,9},{9,10},{10,1... | collective-permute-start | bytes 786440 | tf_op jit(solution)/shard_map/ppermute | solution.py:430
  3.2 1.3 %collective-permute-start.2 = (bf16[64,2048]{1,0:T(8,128)(2,1)}, bf16[64,2048]{1,0:T(8,128)(2,1)S(1)}, u32[]{:S(2)}, u32[]{:S(2)}) collective-permute-start(bf16[64,2048]{1,0:T(8,128)(2,1)} %bitcast.66), channel_id=1, source_target_pairs={{1,0},{2,1},{3,2},{4,3},{5,4},{6,5},{7,6},{8,7},{9,8},{10,9},{11,1... | collective-permute-start | bytes 786440 | tf_op jit(solution)/shard_map/ppermute | solution.py:430
  4.5 1.1 %convert.16 = bf16[1,16,64,128]{3,2,1,0:T(8,128)(2,1)S(1)} convert(f32[1,16,64,128]{3,2,1,0:T(8,128)} %param.18) | non-fusion elementwise | flops 131072 | bytes 786432 | tf_op jit(solution)/shard_map/convert.10
  5.6 0.0 copy-done.1
  5.7 0.0 copy-start.4
  5.7 0.0 copy-start.6
  5.7 0.8 fusion
  6.5 6.8 %collective-permute-start = (bf16[28,64,128]{2,1,0:T(8,128)(2,1)}, bf16[28,64,128]{2,1,0:T(8,128)(2,1)S(1)}, u32[]{:S(2)}, u32[]{:S(2)}) collective-permute-start(bf16[28,64,128]{2,1,0:T(8,128)(2,1)} %fusion), channel_id=1, source_target_pairs={{0,8},{1,9},{2,10},{3,11},{4,12},{5,13},{6,14},{7,15},{8,0},{9,1},... | collective-permute-start | bytes 1376264 | tf_op jit(solution)/shard_map/ppermute | solution.py:435
  13.4 0.0 collective-permute-done.1.low_ref
  13.4 0.0 collective-permute-done.2.high_ref
  13.4 0.0 copy-done.4
  13.4 0.0 copy-done.6
  13.4 0.0 copy-start.12
  13.4 0.0 copy-start.10
  13.4 0.0 copy-start.11
  13.4 1.3 %shard_map.157.mid_ref = bf16[64,2048]{1,0:T(8,128)(2,1)S(1)} custom-call(bf16[64,2048]{1,0:T(8,128)(2,1)S(1)} %collective-permute-done.1.low_ref, bf16[64,2048]{1,0:T(8,128)(2,1)S(1)} %bitcast.67, bf16[64,2048]{1,0:T(8,128)(2,1)S(1)} %collective-permute-done.2.high_ref, bf16[27,64,64]{2,1,0:T(8,128)(2,1)S(1)} %copy-done.4), custom_call_target="tpu_custom_call" | custom-call | tf_op jit(solution)/shard_map/pallas_call | solution.py:117
  14.7 0.0 copy-start.3
  14.7 2.3 %collective-permute-start.3 = (bf16[64,2048]{1,0:T(8,128)(2,1)S(1)}, bf16[64,2048]{1,0:T(8,128)(2,1)S(1)}, u32[]{:S(2)}, u32[]{:S(2)}) collective-permute-start(bf16[64,2048]{1,0:T(8,128)(2,1)S(1)} %shard_map.157.mid_ref), channel_id=1, source_target_pairs={{0,1},{1,2},{2,3},{3,4},{4,5},{5,6},{6,7},{7,8},{8,9},{9,10},{10,1... | collective-permute-start | bytes 786440 | tf_op jit(solution)/shard_map/ppermute | solution.py:430
  17.1 1.3 %collective-permute-start.4 = (bf16[64,2048]{1,0:T(8,128)(2,1)S(1)}, bf16[64,2048]{1,0:T(8,128)(2,1)}, u32[]{:S(2)}, u32[]{:S(2)}) collective-permute-start(bf16[64,2048]{1,0:T(8,128)(2,1)S(1)} %shard_map.157.mid_ref), channel_id=1, source_target_pairs={{1,0},{2,1},{3,2},{4,3},{5,4},{6,5},{7,6},{8,7},{9,8},{10,9},{11,1... | collective-permute-start | bytes 786440 | tf_op jit(solution)/shard_map/ppermute | solution.py:430
  18.4 0.0 copy-done.13
  18.4 0.7 copy.17.head_ref
  19.1 0.7 and_bitcast_fusion
  19.8 0.7 fusion.3
  20.5 0.0 collective-permute-done.3.low_ref
  20.5 0.1 collective-permute-done.4.high_ref
  20.6 0.0 copy-done.5
  20.6 0.8 copy-done.7
  21.4 2.2 %shard_map.158 = bf16[16,128]{1,0:T(8,128)(2,1)S(1)} custom-call(bf16[64,2048]{1,0:T(8,128)(2,1)S(1)} %collective-permute-done.3.low_ref, bf16[64,2048]{1,0:T(8,128)(2,1)S(1)} %shard_map.157.mid_ref, bf16[64,2048]{1,0:T(8,128)(2,1)} %collective-permute-done.4.high_ref, bf16[27,64,64]{2,1,0:T(8,128)(2,1)S(1)} %copy-done.5, f32[64,1]{1,0:T(8,128)S(1)} %copy-done.7), custom_call_target="tpu_custom_call" | custom-call | tf_op jit(solution)/shard_map/pallas_call | solution.py:128
  23.7 6.1 %collective-permute-start.5 = (bf16[1,16,128]{2,1,0:T(8,128)(2,1)S(1)}, bf16[1,16,128]{2,1,0:T(8,128)(2,1)S(1)}, u32[]{:S(2)}, u32[]{:S(2)}) collective-permute-start(bf16[1,16,128]{2,1,0:T(8,128)(2,1)S(1)} %bitcast.68), channel_id=1, source_target_pairs={{0,1},{1,0},{2,3},{3,2},{4,5},{5,4},{6,7},{7,6},{8,9},{9,8},{10,11... | collective-permute-start | bytes 12296 | tf_op jit(solution)/shard_map/ppermute | solution.py:435
  29.8 0.1 fusion.2.pick_ref
  29.9 0.7 collective-permute-done.5
  30.6 10.6 %collective-permute-start.6 = (bf16[2,16,128]{2,1,0:T(8,128)(2,1)S(1)}, bf16[2,16,128]{2,1,0:T(8,128)(2,1)S(1)}, u32[]{:S(2)}, u32[]{:S(2)}) collective-permute-start(bf16[2,16,128]{2,1,0:T(8,128)(2,1)S(1)} %pad_maximum_fusion.8), channel_id=1, source_target_pairs={{0,2},{1,3},{2,0},{3,1},{4,6},{5,7},{6,4},{7,5},{8,10},{9,11},{10,... | collective-permute-start | bytes 24584 | tf_op jit(solution)/shard_map/ppermute | solution.py:435
  41.3 0.0 copy-done.12
  41.3 0.1 constant_dynamic-slice_fusion.3
  41.4 1.6 %collective-permute-done.6 = bf16[2,16,128]{2,1,0:T(8,128)(2,1)S(1)} collective-permute-done((bf16[2,16,128]{2,1,0:T(8,128)(2,1)S(1)}, bf16[2,16,128]{2,1,0:T(8,128)(2,1)S(1)}, u32[]{:S(2)}, u32[]{:S(2)}) %collective-permute-start.6) | collective-permute-done | bytes 8224 | tf_op jit(solution)/shard_map/ppermute | solution.py:435
  42.9 4.6 %collective-permute-start.7 = (bf16[4,16,128]{2,1,0:T(8,128)(2,1)S(1)}, bf16[4,16,128]{2,1,0:T(8,128)(2,1)S(1)}, u32[]{:S(2)}, u32[]{:S(2)}) collective-permute-start(bf16[4,16,128]{2,1,0:T(8,128)(2,1)S(1)} %pad_maximum_fusion.5), channel_id=1, source_target_pairs={{0,4},{1,5},{2,6},{3,7},{4,0},{5,1},{6,2},{7,3},{8,12},{9,13},{10,... | collective-permute-start | bytes 49160 | tf_op jit(solution)/shard_map/ppermute | solution.py:435
  47.5 0.6 fusion.8
  48.1 1.1 %collective-permute-done.7 = bf16[4,16,128]{2,1,0:T(8,128)(2,1)S(1)} collective-permute-done((bf16[4,16,128]{2,1,0:T(8,128)(2,1)S(1)}, bf16[4,16,128]{2,1,0:T(8,128)(2,1)S(1)}, u32[]{:S(2)}, u32[]{:S(2)}) %collective-permute-start.7) | collective-permute-done | bytes 16416 | tf_op jit(solution)/shard_map/ppermute | solution.py:435
  49.2 2.0 %collective-permute-start.8 = (bf16[8,16,128]{2,1,0:T(8,128)(2,1)S(1)}, bf16[8,16,128]{2,1,0:T(8,128)(2,1)S(1)}, u32[]{:S(2)}, u32[]{:S(2)}) collective-permute-start(bf16[8,16,128]{2,1,0:T(8,128)(2,1)S(1)} %pad_maximum_fusion.3.own_speed), channel_id=1, source_target_pairs={{0,8},{1,9},{2,10},{3,11},{4,12},{5,13},{6,14},{7,15},{8,0},{9,1},... | collective-permute-start | bytes 98312 | tf_op jit(solution)/shard_map/ppermute | solution.py:435
  51.9 0.0 copy-done
  51.9 0.2 dynamic-slice_reduce_fusion.pulses
  52.1 1.3 %stack.35.info = s32[6]{0:T(128)S(1)} concatenate(s32[1]{0:T(128)} %bitcast, s32[1]{0:T(128)} %bitcast.1, s32[1]{0:T(128)} %bitcast.2, s32[1]{0:T(128)} %bitcast.4, s32[1]{0:T(128)} %bitcast.5, s32[1]{0:T(128)} %bitcast.6), dimensions={0} | concatenate | bytes 48 | tf_op jit(solution)/shard_map/stack | solution.py:480
  53.4 0.0 collective-permute-done.low_rim.high_rim
  53.4 0.6 collective-permute-done.8.low_speed.high_speed
  54.1 0.0 copy-done.10
  54.1 0.0 copy-done.11
  54.1 0.0 copy-done.3
  54.1 0.0 copy-done.2
  54.1 0.0 copy-start.8
  54.1 0.8 copy-done.8
  54.9 0.8 copy-done.9
  55.8 17.9 %shard_map.159 = (f32[16,64,128]{2,1,0:T(8,128)}, f32[8,16,128]{2,1,0:T(8,128)S(1)}, f32[2,16,128]{2,1,0:T(8,128)S(1)}, f32[4,128]{1,0:T(4,128)S(1)}) custom-call(s32[6]{0:T(128)S(1)} %stack.35.info, f32[4]{0:T(128)S(1)} %dynamic-slice_reduce_fusion.pulses, s32[2,128]{1,0:T(2,128)S(1)} %pad_add_fusion.stations, f32[16,64,128]{2,1,0:T(8,128)S(1)} %bitcast.62, ...), custom_call_target="tpu_custom_call" | custom-call | tf_op jit(solution)/shard_map/pallas_call | solution.py:383
  73.7 2.0 %collective-permute-start.9 = (f32[20,128]{1,0:T(8,128)S(1)}, f32[20,128]{1,0:T(8,128)S(1)}, u32[]{:S(2)}, u32[]{:S(2)}) collective-permute-start(f32[20,128]{1,0:T(8,128)S(1)} %pad_maximum_fusion.7), channel_id=1, source_target_pairs={{0,8},{1,9},{2,10},{3,11},{4,12},{5,13},{6,14},{7,15},{8,0},{9,1},... | collective-permute-start | bytes 30728 | tf_op jit(solution)/shard_map/ppermute | solution.py:435
  75.7 2.6 %collective-permute-done.9 = f32[20,128]{1,0:T(8,128)S(1)} collective-permute-done((f32[20,128]{1,0:T(8,128)S(1)}, f32[20,128]{1,0:T(8,128)S(1)}, u32[]{:S(2)}, u32[]{:S(2)}) %collective-permute-start.9) | collective-permute-done | bytes 10272 | tf_op jit(solution)/shard_map/ppermute | solution.py:435
  78.3 0.1 select_add_fusion
  78.5 2.1 %collective-permute-start.10 = (f32[68,128]{1,0:T(8,128)S(1)}, f32[68,128]{1,0:T(8,128)S(1)}, u32[]{:S(2)}, u32[]{:S(2)}) collective-permute-start(f32[68,128]{1,0:T(8,128)S(1)} %pad_maximum_fusion.2), channel_id=1, source_target_pairs={{0,4},{1,5},{2,6},{3,7},{4,0},{5,1},{6,2},{7,3},{8,12},{9,13},{10,... | collective-permute-start | bytes 104456 | tf_op jit(solution)/shard_map/ppermute | solution.py:435
  80.6 1.9 %collective-permute-done.10 = f32[68,128]{1,0:T(8,128)S(1)} collective-permute-done((f32[68,128]{1,0:T(8,128)S(1)}, f32[68,128]{1,0:T(8,128)S(1)}, u32[]{:S(2)}, u32[]{:S(2)}) %collective-permute-start.10) | collective-permute-done | bytes 34848 | tf_op jit(solution)/shard_map/ppermute | solution.py:435
  82.5 2.1 %collective-permute-start.11 = (f32[40,128]{1,0:T(8,128)S(1)}, f32[40,128]{1,0:T(8,128)S(1)}, u32[]{:S(2)}, u32[]{:S(2)}) collective-permute-start(f32[40,128]{1,0:T(8,128)S(1)} %pad_maximum_fusion.4), channel_id=1, source_target_pairs={{0,2},{1,3},{2,0},{3,1},{4,6},{5,7},{6,4},{7,5},{8,10},{9,11},{10,... | collective-permute-start | bytes 61448 | tf_op jit(solution)/shard_map/ppermute | solution.py:435
  84.6 1.8 %collective-permute-done.11 = f32[40,128]{1,0:T(8,128)S(1)} collective-permute-done((f32[40,128]{1,0:T(8,128)S(1)}, f32[40,128]{1,0:T(8,128)S(1)}, u32[]{:S(2)}, u32[]{:S(2)}) %collective-permute-start.11) | collective-permute-done | bytes 20512 | tf_op jit(solution)/shard_map/ppermute | solution.py:435
  86.4 0.1 collective-permute-start.12
  86.5 1.2 %collective-permute-done.12 = f32[32,128]{1,0:T(8,128)S(1)} collective-permute-done((f32[32,128]{1,0:T(8,128)S(1)}, f32[32,128]{1,0:T(8,128)S(1)}, u32[]{:S(2)}, u32[]{:S(2)}) %collective-permute-start.12) | collective-permute-done | bytes 16416 | tf_op jit(solution)/shard_map/ppermute | solution.py:435
  87.7 1.2 %shard_map.160 = (f32[1,2048]{1,0:T(1,128)}, f32[8,4,128]{2,1,0:T(4,128)}) custom-call(s32[6]{0:T(128)S(1)} %stack.35.info, f32[16,128]{1,0:T(8,128)S(1)} %slice_add_fusion.2.term_ref, f32[8,4,128]{2,1,0:T(4,128)S(1)} %constant_dynamic-update-slice_fusion.records_ref), custom_call_target="tpu_custom_call" | custom-call | tf_op jit(solution)/shard_map/pallas_call | solution.py:415
  (35 shorter events, 0.3 us)
Async XLA Ops:
  0.6 51.3 %copy-start = (f32[8,4]{0,1:T(4,128)S(1)}, f32[8,4]{0,1:T(4,128)}, u32[]{:S(2)}) copy-start(f32[8,4]{0,1:T(4,128)} %param.21) | copy-start | bytes 388
  0.6 4.9 %copy-start.1 = (f32[1,16,64,128]{3,2,1,0:T(8,128)S(1)}, f32[1,16,64,128]{3,2,1,0:T(8,128)}, u32[]{:S(2)}) copy-start(f32[1,16,64,128]{3,2,1,0:T(8,128)} %param.19) | copy-start | bytes 1572868
  0.7 12.7 %collective-permute-start.1 = (bf16[64,2048]{1,0:T(8,128)(2,1)}, bf16[64,2048]{1,0:T(8,128)(2,1)S(1)}, u32[]{:S(2)}, u32[]{:S(2)}) collective-permute-start(bf16[64,2048]{1,0:T(8,128)(2,1)} %bitcast.65), channel_id=1, source_target_pairs={{0,1},{1,2},{2,3},{3,4},{4,5},{5,6},{6,7},{7,8},{8,9},{9,10},{10,1... | collective-permute-start | bytes 786440 | tf_op jit(solution)/shard_map/ppermute | solution.py:430
  3.2 10.2 %collective-permute-start.2 = (bf16[64,2048]{1,0:T(8,128)(2,1)}, bf16[64,2048]{1,0:T(8,128)(2,1)S(1)}, u32[]{:S(2)}, u32[]{:S(2)}) collective-permute-start(bf16[64,2048]{1,0:T(8,128)(2,1)} %bitcast.66), channel_id=1, source_target_pairs={{1,0},{2,1},{3,2},{4,3},{5,4},{6,5},{7,6},{8,7},{9,8},{10,9},{11,1... | collective-permute-start | bytes 786440 | tf_op jit(solution)/shard_map/ppermute | solution.py:430
  5.7 7.7 %copy-start.4 = (bf16[27,64,64]{2,1,0:T(8,128)(2,1)S(1)}, bf16[27,64,64]{2,1,0:T(8,128)(2,1)}, u32[]{:S(2)}) copy-start(bf16[27,64,64]{2,1,0:T(8,128)(2,1)} %weight_ref.2) | copy-start | bytes 663556
  5.7 7.7 %copy-start.6 = (bf16[64,1,2048]{2,0,1:T(8,128)(2,1)S(1)}, bf16[64,1,2048]{2,0,1:T(8,128)(2,1)}, u32[]{:S(2)}) copy-start(bf16[64,1,2048]{2,0,1:T(8,128)(2,1)} %param.14) | copy-start | bytes 786436
  6.5 11.8 %copy-start.13 = (bf16[64]{0:T(256)(128)(2,1)S(1)}, bf16[64]{0:T(256)(128)(2,1)}, u32[]{:S(2)}) copy-start(bf16[64]{0:T(256)(128)(2,1)} %param.17) | copy-start | bytes 388
  6.5 14.1 %copy-start.5 = (bf16[27,64,64]{2,1,0:T(8,128)(2,1)S(1)}, bf16[27,64,64]{2,1,0:T(8,128)(2,1)}, u32[]{:S(2)}) copy-start(bf16[27,64,64]{2,1,0:T(8,128)(2,1)} %weight_ref.3) | copy-start | bytes 663556
  6.5 46.9 %collective-permute-start = (bf16[28,64,128]{2,1,0:T(8,128)(2,1)}, bf16[28,64,128]{2,1,0:T(8,128)(2,1)S(1)}, u32[]{:S(2)}, u32[]{:S(2)}) collective-permute-start(bf16[28,64,128]{2,1,0:T(8,128)(2,1)} %fusion), channel_id=1, source_target_pairs={{0,8},{1,9},{2,10},{3,11},{4,12},{5,13},{6,14},{7,15},{8,0},{9,1},... | collective-permute-start | bytes 1376264 | tf_op jit(solution)/shard_map/ppermute | solution.py:435
  13.4 27.9 %copy-start.12 = (s32[8,3]{0,1:T(4,128)S(1)}, s32[8,3]{0,1:T(4,128)}, u32[]{:S(2)}) copy-start(s32[8,3]{0,1:T(4,128)} %param.22) | copy-start | bytes 292
  13.4 40.6 %copy-start.10 = (bf16[64,64]{1,0:T(8,128)(2,1)S(1)}, bf16[64,64]{1,0:T(8,128)(2,1)}, u32[]{:S(2)}) copy-start(bf16[64,64]{1,0:T(8,128)(2,1)} %constant.63.clone.tall_ref) | copy-start | bytes 24580
  13.4 40.6 %copy-start.11 = (bf16[32,128]{1,0:T(8,128)(2,1)S(1)}, bf16[32,128]{1,0:T(8,128)(2,1)}, u32[]{:S(2)}) copy-start(bf16[32,128]{1,0:T(8,128)(2,1)} %constant.64.clone.short_ref) | copy-start | bytes 24580
  14.7 39.4 %copy-start.3 = (bf16[4,1,16,64,128]{4,3,2,1,0:T(8,128)(2,1)S(1)}, bf16[4,1,16,64,128]{4,3,2,1,0:T(8,128)(2,1)}, u32[]{:S(2)}) copy-start(bf16[4,1,16,64,128]{4,3,2,1,0:T(8,128)(2,1)} %param.20) | copy-start | bytes 3145732
  14.7 5.8 %collective-permute-start.3 = (bf16[64,2048]{1,0:T(8,128)(2,1)S(1)}, bf16[64,2048]{1,0:T(8,128)(2,1)S(1)}, u32[]{:S(2)}, u32[]{:S(2)}) collective-permute-start(bf16[64,2048]{1,0:T(8,128)(2,1)S(1)} %shard_map.157.mid_ref), channel_id=1, source_target_pairs={{0,1},{1,2},{2,3},{3,4},{4,5},{5,6},{6,7},{7,8},{8,9},{9,10},{10,1... | collective-permute-start | bytes 786440 | tf_op jit(solution)/shard_map/ppermute | solution.py:430
  17.1 3.6 %collective-permute-start.4 = (bf16[64,2048]{1,0:T(8,128)(2,1)S(1)}, bf16[64,2048]{1,0:T(8,128)(2,1)}, u32[]{:S(2)}, u32[]{:S(2)}) collective-permute-start(bf16[64,2048]{1,0:T(8,128)(2,1)S(1)} %shard_map.157.mid_ref), channel_id=1, source_target_pairs={{1,0},{2,1},{3,2},{4,3},{5,4},{6,5},{7,6},{8,7},{9,8},{10,9},{11,1... | collective-permute-start | bytes 786440 | tf_op jit(solution)/shard_map/ppermute | solution.py:430
  20.5 33.6 %copy-start.2 = (f32[1,16,64,128]{3,2,1,0:T(8,128)S(1)}, f32[1,16,64,128]{3,2,1,0:T(8,128)}, u32[]{:S(2)}) copy-start(f32[1,16,64,128]{3,2,1,0:T(8,128)} %param.18) | copy-start | bytes 1572868
  20.6 0.8 copy-start.7
  23.7 7.0 %collective-permute-start.5 = (bf16[1,16,128]{2,1,0:T(8,128)(2,1)S(1)}, bf16[1,16,128]{2,1,0:T(8,128)(2,1)S(1)}, u32[]{:S(2)}, u32[]{:S(2)}) collective-permute-start(bf16[1,16,128]{2,1,0:T(8,128)(2,1)S(1)} %bitcast.68), channel_id=1, source_target_pairs={{0,1},{1,0},{2,3},{3,2},{4,5},{5,4},{6,7},{7,6},{8,9},{9,8},{10,11... | collective-permute-start | bytes 12296 | tf_op jit(solution)/shard_map/ppermute | solution.py:435
  30.6 12.3 %collective-permute-start.6 = (bf16[2,16,128]{2,1,0:T(8,128)(2,1)S(1)}, bf16[2,16,128]{2,1,0:T(8,128)(2,1)S(1)}, u32[]{:S(2)}, u32[]{:S(2)}) collective-permute-start(bf16[2,16,128]{2,1,0:T(8,128)(2,1)S(1)} %pad_maximum_fusion.8), channel_id=1, source_target_pairs={{0,2},{1,3},{2,0},{3,1},{4,6},{5,7},{6,4},{7,5},{8,10},{9,11},{10,... | collective-permute-start | bytes 24584 | tf_op jit(solution)/shard_map/ppermute | solution.py:435
  42.9 6.3 %collective-permute-start.7 = (bf16[4,16,128]{2,1,0:T(8,128)(2,1)S(1)}, bf16[4,16,128]{2,1,0:T(8,128)(2,1)S(1)}, u32[]{:S(2)}, u32[]{:S(2)}) collective-permute-start(bf16[4,16,128]{2,1,0:T(8,128)(2,1)S(1)} %pad_maximum_fusion.5), channel_id=1, source_target_pairs={{0,4},{1,5},{2,6},{3,7},{4,0},{5,1},{6,2},{7,3},{8,12},{9,13},{10,... | collective-permute-start | bytes 49160 | tf_op jit(solution)/shard_map/ppermute | solution.py:435
  49.2 4.8 %collective-permute-start.8 = (bf16[8,16,128]{2,1,0:T(8,128)(2,1)S(1)}, bf16[8,16,128]{2,1,0:T(8,128)(2,1)S(1)}, u32[]{:S(2)}, u32[]{:S(2)}) collective-permute-start(bf16[8,16,128]{2,1,0:T(8,128)(2,1)S(1)} %pad_maximum_fusion.3.own_speed), channel_id=1, source_target_pairs={{0,8},{1,9},{2,10},{3,11},{4,12},{5,13},{6,14},{7,15},{8,0},{9,1},... | collective-permute-start | bytes 98312 | tf_op jit(solution)/shard_map/ppermute | solution.py:435
  54.1 0.8 copy-start.8
  54.9 0.8 copy-start.9
  73.7 4.7 %collective-permute-start.9 = (f32[20,128]{1,0:T(8,128)S(1)}, f32[20,128]{1,0:T(8,128)S(1)}, u32[]{:S(2)}, u32[]{:S(2)}) collective-permute-start(f32[20,128]{1,0:T(8,128)S(1)} %pad_maximum_fusion.7), channel_id=1, source_target_pairs={{0,8},{1,9},{2,10},{3,11},{4,12},{5,13},{6,14},{7,15},{8,0},{9,1},... | collective-permute-start | bytes 30728 | tf_op jit(solution)/shard_map/ppermute | solution.py:435
  78.5 4.0 %collective-permute-start.10 = (f32[68,128]{1,0:T(8,128)S(1)}, f32[68,128]{1,0:T(8,128)S(1)}, u32[]{:S(2)}, u32[]{:S(2)}) collective-permute-start(f32[68,128]{1,0:T(8,128)S(1)} %pad_maximum_fusion.2), channel_id=1, source_target_pairs={{0,4},{1,5},{2,6},{3,7},{4,0},{5,1},{6,2},{7,3},{8,12},{9,13},{10,... | collective-permute-start | bytes 104456 | tf_op jit(solution)/shard_map/ppermute | solution.py:435
  82.5 3.9 %collective-permute-start.11 = (f32[40,128]{1,0:T(8,128)S(1)}, f32[40,128]{1,0:T(8,128)S(1)}, u32[]{:S(2)}, u32[]{:S(2)}) collective-permute-start(f32[40,128]{1,0:T(8,128)S(1)} %pad_maximum_fusion.4), channel_id=1, source_target_pairs={{0,2},{1,3},{2,0},{3,1},{4,6},{5,7},{6,4},{7,5},{8,10},{9,11},{10,... | collective-permute-start | bytes 61448 | tf_op jit(solution)/shard_map/ppermute | solution.py:435
  86.4 1.2 %collective-permute-start.12 = (f32[32,128]{1,0:T(8,128)S(1)}, f32[32,128]{1,0:T(8,128)S(1)}, u32[]{:S(2)}, u32[]{:S(2)}) collective-permute-start(f32[32,128]{1,0:T(8,128)S(1)} %pad_maximum_fusion.6), channel_id=1, source_target_pairs={{0,1},{1,0},{2,3},{3,2},{4,5},{5,4},{6,7},{7,6},{8,9},{9,8},{10,11... | collective-permute-start | bytes 49160 | tf_op jit(solution)/shard_map/ppermute | solution.py:435

commit v2 on v1

v2 whole, which is shorter than its diff:
```python
import functools

import jax
import jax.numpy as jnp
import numpy as np
from jax import lax
from jax.experimental import pallas as pl
from jax.experimental.pallas import tpu as pltpu
from jax.sharding import PartitionSpec as P

CH = 64
CY = 32
CX = 64
FY = 64
FX = 128
CELLS = CY * CX
SHOTS = 8
STEPS = 4
NREC = 128
PLANES = 16
REACH = 4
CUR_RIM = REACH * STEPS
PREV_RIM = CUR_RIM - REACH
RIM_PLANES = CUR_RIM + PREV_RIM
PARTS = (0, 20, RIM_PLANES)
EXT = PLANES + 2 * CUR_RIM
PAD = 8
ROWS = FY + 2 * PAD
CHUNK = 4

stencil_weights = (-205.0 / 72.0, 8.0 / 5.0, -1.0 / 5.0, 8.0 / 315.0, -1.0 / 560.0)
lowest_speed = 1.5
speed_range = 3.0
courant = 0.088
leak_slope = 0.2

VMEM = pl.BlockSpec(memory_space=pltpu.VMEM)
ANY = pl.BlockSpec(memory_space=pl.ANY)
SMEM = pl.BlockSpec(memory_space=pltpu.SMEM)
PARAMS = pltpu.CompilerParams(vmem_limit_bytes=24 * 1024 * 1024)


def doubling_matrix(length):
    matrix = np.zeros((2 * length, length), np.float32)
    for k in range(length):
        matrix[2 * k, k] += 0.75
        matrix[2 * k, max(k - 1, 0)] += 0.25
        matrix[2 * k + 1, k] += 0.75
        matrix[2 * k + 1, min(k + 1, length - 1)] += 0.25
    return matrix


def plane_matrices():
    across = doubling_matrix(CX)
    down = doubling_matrix(CY)
    widen = np.zeros((128, 256), np.float32)
    widen[:64, :128] = across.T
    widen[64:, 128:] = across.T
    tall = np.concatenate([down[:, 0::2], down[:, 1::2]], axis=1)
    tall_twice = np.concatenate([tall, tall], axis=1)
    short_twice = np.concatenate([tall.T, tall.T], axis=1)
    narrow = widen.T
    return tuple(jnp.asarray(m, jnp.bfloat16) for m in (widen, tall_twice, short_twice, narrow))


def halves(value):
    high = value.astype(jnp.bfloat16)
    low = (value - high.astype(jnp.float32)).astype(jnp.bfloat16)
    return high, low


def leaky(value):
    return jnp.where(value > 0, value, leak_slope * value)


def conv(near_ref, mid_ref, far_ref, weight_ref, fields, packed):
    odd = lax.axis_index("slab") % 2
    depths = (2 - 2 * odd, 1, 2 * odd)
    column = lax.broadcasted_iota(jnp.int32, (CH, CELLS), 1) % CX
    for part, ref in enumerate((near_ref, mid_ref, far_ref)):
        plane = ref[...]
        wide = plane.astype(jnp.float32)
        left = jnp.where(column == 0, 0.0, pltpu.roll(wide, 1, 1)).astype(jnp.bfloat16)
        right = jnp.where(column == CX - 1, 0.0, pltpu.roll(wide, CELLS - 1, 1)).astype(jnp.bfloat16)
        for place, piece in enumerate((left, plane, right)):
            begin = (3 * part + place) * CH
            fields[begin : begin + CH, :] = piece
    for part, depth in enumerate(depths):
        for row in range(3):
            for place in range(3):
                begin = (3 * part + place) * CH
                packed[row * CH : (row + 1) * CH, begin : begin + CH] = weight_ref[
                    9 * depth + 3 * row + place
                ]
    products = jnp.dot(packed[...], fields[...], preferred_element_type=jnp.float32)
    cell = lax.broadcasted_iota(jnp.int32, (CH, CELLS), 1)
    above = jnp.where(cell < CX, 0.0, pltpu.roll(products[:CH], CX, 1))
    below = jnp.where(cell >= CELLS - CX, 0.0, pltpu.roll(products[2 * CH :], CELLS - CX, 1))
    return products[CH : 2 * CH] + above + below


def to_column(row):
    count = row.shape[1]
    here = lax.broadcasted_iota(jnp.int32, (count, count), 0)
    there = lax.broadcasted_iota(jnp.int32, (count, count), 1)
    return jnp.sum(jnp.where(here == there, row, 0), axis=1, keepdims=True)


def first_kernel(near_ref, mid_ref, far_ref, weight_ref, low_part, high_part, out_ref, fields, packed):
    out_ref[...] = leaky(conv(near_ref, mid_ref, far_ref, weight_ref, fields, packed)).astype(
        jnp.bfloat16
    )


def second_kernel(near_ref, mid_ref, far_ref, weight_ref, head_ref, low_part, high_part, out_ref, fields, packed):
    second = leaky(conv(near_ref, mid_ref, far_ref, weight_ref, fields, packed))
    head = to_column(head_ref[...].astype(jnp.float32))
    logits = jnp.sum(second * head, axis=0, keepdims=True)
    speed = lowest_speed + speed_range * jax.nn.sigmoid(logits)
    for j in range(16):
        out_ref[j : j + 1, :] = speed[:, 128 * j : 128 * (j + 1)].astype(jnp.bfloat16)


CONV_SCRATCH = [
    pltpu.VMEM((9 * CH, CELLS), jnp.bfloat16),
    pltpu.VMEM((3 * CH, 9 * CH), jnp.bfloat16),
]


def first_conv(near, mid, far, weight, low_part, high_part):
    return pl.pallas_call(
        first_kernel,
        out_shape=jax.ShapeDtypeStruct((CH, CELLS), jnp.bfloat16),
        in_specs=[VMEM] * 4 + [ANY] * 2,
        out_specs=VMEM,
        scratch_shapes=CONV_SCRATCH,
        compiler_params=PARAMS,
    )(near, mid, far, weight, low_part, high_part)


def second_conv(near, mid, far, weight, head, low_part, high_part):
    return pl.pallas_call(
        second_kernel,
        out_shape=jax.ShapeDtypeStruct((16, 128), jnp.bfloat16),
        in_specs=[VMEM] * 5 + [ANY] * 2,
        out_specs=VMEM,
        scratch_shapes=CONV_SCRATCH,
        compiler_params=PARAMS,
    )(near, mid, far, weight, head, low_part, high_part)


def band_matrix():
    band = np.zeros((FX, FX), np.float64)
    for reach, weight in enumerate(stencil_weights):
        for at in range(FX):
            if reach == 0:
                band[at, at] = 3.0 * weight
            elif at + reach < FX:
                band[at, at + reach] = band[at + reach, at] = weight
    high = band.astype(jnp.bfloat16)
    low = (band - high.astype(np.float64)).astype(jnp.bfloat16)
    return jnp.asarray(np.concatenate([high, high, low], axis=0))


INNER = slice(PAD, PAD + FY)


def laplace(field, first, band, use):
    planes = field[pl.ds(first, CHUNK), INNER, :].reshape(CHUNK * FY, FX)
    high, low = halves(planes)
    across = jnp.dot(
        jnp.concatenate([high, low, high], axis=1), band, preferred_element_type=jnp.float32
    )
    for row in range(0, FY, 8):
        column = [
            field[first + k - REACH, PAD + row : PAD + row + 8, :]
            for k in range(CHUNK + 2 * REACH)
        ]
        for k in range(CHUNK):
            total = across[k * FY + row : k * FY + row + 8]
            for reach in range(1, REACH + 1):
                near = column[k + REACH - reach] + column[k + REACH + reach]
                begin = PAD + row - reach
                near = near + field[first + k, begin : begin + 8, :]
                begin = PAD + row + reach
                near = near + field[first + k, begin : begin + 8, :]
                total = total + stencil_weights[reach] * near
            use(k, slice(row, row + 8), column[k + REACH], total)


def slab_place():
    slab = lax.axis_index("slab") // SHOTS
    slabs = lax.axis_size("slab") // SHOTS
    return slab, slab > 0, slab < slabs - 1


def clear_rows(field, first, last):
    def one(plane, _):
        field[plane, :PAD, :] = jnp.zeros((PAD, FX), jnp.float32)
        field[plane, PAD + FY :, :] = jnp.zeros((PAD, FX), jnp.float32)
        return 0

    lax.fori_loop(first, last, one, 0)


def clear_beyond(field, has_low, has_high):
    for inside, begin in ((has_low, CUR_RIM - REACH), (has_high, CUR_RIM + PLANES)):

        @pl.when(jnp.logical_not(inside))
        def _():
            for plane in range(begin, begin + REACH):
                field[plane, INNER, :] = jnp.zeros((FY, FX), jnp.float32)


def prepare_kernel(
    cur_ref,
    prev_ref,
    low_0,
    low_1,
    high_0,
    high_1,
    adjoint_ref,
    stations_ref,
    band_ref,
    cur_out,
    base_out,
    laplace_out,
    total_out,
    pick_out,
    field,
):
    slab, has_low, has_high = slab_place()
    band = band_ref[...]
    clear_rows(field, 0, EXT)
    clear_beyond(field, has_low, has_high)

    def load_own(plane, _):
        value = cur_ref[plane]
        field[CUR_RIM + plane, INNER, :] = value
        cur_out[CUR_RIM + plane] = value
        base_out[CUR_RIM + plane] = 2.0 * value - prev_ref[plane]
        return 0

    lax.fori_loop(0, PLANES, load_own, 0)

    def load_rim(parts, at_cur, at_prev):
        for ref, begin, end in zip(parts, PARTS[:-1], PARTS[1:]):

            def one(plane, _):
                value = ref[plane - begin].astype(jnp.float32)
                field[at_cur + plane - PREV_RIM, INNER, :] = value
                cur_out[at_cur + plane - PREV_RIM] = value
                return 0

            lax.fori_loop(max(begin, PREV_RIM), end, one, 0)
        for ref, begin, end in zip(parts, PARTS[:-1], PARTS[1:]):

            def two(plane, _):
                value = ref[plane - begin].astype(jnp.float32)
                base_out[at_prev + plane] = 2.0 * field[at_prev + plane, INNER, :] - value
                return 0

            lax.fori_loop(begin, min(end, PREV_RIM), two, 0)

    @pl.when(has_low)
    def _():
        load_rim((low_0, low_1), 0, REACH)

    @pl.when(has_high)
    def _():
        load_rim((high_0, high_1), CUR_RIM + PLANES, CUR_RIM + PLANES)

    def rim_planes(chunk, _):
        def use(k, rows, centre, lap):
            laplace_out[chunk * CHUNK + k, rows, :] = lap

        laplace(field, chunk * CHUNK, band, use)
        return 0

    def own_planes(chunk, _):
        def use(k, rows, centre, lap):
            laplace_out[CUR_RIM + chunk * CHUNK + k, rows, :] = lap
            weight = adjoint_ref[chunk * CHUNK + k, rows, :].astype(jnp.float32)
            total_out[chunk * CHUNK + k, rows, :] = weight * lap

        laplace(field, CUR_RIM + chunk * CHUNK, band, use)
        return 0

    first, last = stretch(has_low, has_high, PREV_RIM)
    lax.fori_loop(first // CHUNK, CUR_RIM // CHUNK, rim_planes, 0)
    lax.fori_loop(0, PLANES // CHUNK, own_planes, 0)
    lax.fori_loop((CUR_RIM + PLANES) // CHUNK, last // CHUNK, rim_planes, 0)

    shot = lax.axis_index("slab") % SHOTS
    depth = stations_ref[0, pl.ds(shot, 1), :] - slab * PLANES
    column = jnp.where((depth >= 0) & (depth < PLANES), stations_ref[2, pl.ds(shot, 1), :], -1)
    lane = lax.broadcasted_iota(jnp.int32, (NREC, FX), 1)
    pick_out[...] = jnp.where(to_column(column) == lane, 1.0, 0.0)


def stretch(has_low, has_high, reach_out):
    first = CUR_RIM - jnp.where(has_low, reach_out, 0)
    last = CUR_RIM + PLANES + jnp.where(has_high, reach_out, 0)
    return first, last


def prepare(*args):
    ext = jax.ShapeDtypeStruct((EXT, FY, FX), jnp.float32)
    return pl.pallas_call(
        prepare_kernel,
        out_shape=(
            ext,
            ext,
            ext,
            jax.ShapeDtypeStruct((PLANES, FY, FX), jnp.float32),
            jax.ShapeDtypeStruct((NREC, FX), jnp.float32),
        ),
        in_specs=[VMEM] * 9,
        out_specs=(VMEM,) * 5,
        scratch_shapes=[pltpu.VMEM((EXT, ROWS, FX), jnp.float32)],
        compiler_params=PARAMS,
    )(*args)


def wave_kernel(
    pulses,
    sources,
    stations,
    cur_ref,
    base_ref,
    laplace_ref,
    total_ref,
    pick_ref,
    adjoint_ref,
    own_speed,
    low_speed,
    high_speed,
    widen_ref,
    tall_ref,
    short_ref,
    narrow_ref,
    band_ref,
    final_ref,
    terms_ref,
    edges_ref,
    records_ref,
    field_a,
    field_b,
    factor,
    coarse,
    speed,
    total,
    rows_ref,
):
    shot = lax.axis_index("slab") % SHOTS
    slab, has_low, has_high = slab_place()
    band = band_ref[...]
    clear_rows(field_a, REACH, EXT - REACH)
    clear_rows(field_b, REACH, EXT - REACH)
    clear_beyond(field_a, has_low, has_high)
    clear_beyond(field_b, has_low, has_high)

    def widen_block(ref, at):
        block = ref[...].reshape(SHOTS * 16, 128)
        wide = jnp.dot(block, widen_ref[...], preferred_element_type=jnp.float32)
        for j in range(SHOTS):
            piece = wide[16 * j : 16 * (j + 1)]
            both = jnp.concatenate([piece[:, :128], piece[:, 128:]], axis=0)
            high, low = halves(both)
            stacked = jnp.concatenate([high, low], axis=0)
            coarse[at + (shot ^ j)] = jnp.dot(
                tall_ref[...], stacked, preferred_element_type=jnp.float32
            )

    widen_block(own_speed, SHOTS)

    @pl.when(has_low)
    def _():
        widen_block(low_speed, 0)

    @pl.when(jnp.logical_not(has_low))
    def _():
        coarse[SHOTS - 1] = coarse[SHOTS]

    @pl.when(has_high)
    def _():
        widen_block(high_speed, 2 * SHOTS)

    @pl.when(jnp.logical_not(has_high))
    def _():
        coarse[2 * SHOTS] = coarse[2 * SHOTS - 1]

    def refine(k, _):
        here = 0.75 * coarse[k]
        for plane, there in ((2 * k, coarse[k - 1]), (2 * k + 1, coarse[k + 1])):
            value = here + 0.25 * there
            square = (courant * value) * (courant * value)
            speed[plane] = value
            factor[plane] = square
            field_b[plane, INNER, :] = base_ref[plane] + square * laplace_ref[plane]
        return 0

    first, last = stretch(has_low, has_high, PREV_RIM)
    lax.fori_loop(first // 2, last // 2, refine, 0)

    source_plane = sources[0, shot] - slab * PLANES + CUR_RIM
    source_row = sources[1, shot]
    lane_row = lax.broadcasted_iota(jnp.int32, (1, FX), 1)

    def inject(field, pad, at, step, first, last):
        @pl.when((source_plane >= first) & (source_plane < last))
        def _():
            place = (source_plane - at, pl.ds(source_row + pad, 1), slice(None))
            field[place] = field[place] + jnp.where(
                lane_row == sources[2, shot], pulses[step, shot], 0.0
            )

    def collect(field, pad, at, step, k):
        depth = jnp.clip(stations[0, shot, k] - slab * PLANES, 0, PLANES - 1)
        rows_ref[step, pl.ds(k, 1), :] = field[
            depth + at, pl.ds(stations[1, shot, k] + pad, 1), :
        ]

    inject(field_b, PAD, 0, 0, first, last)

    for step in range(1, STEPS):
        now, before, out = (
            (field_b, cur_ref, field_a),
            (field_a, field_b, field_b),
            (field_b, field_a, final_ref),
        )[step - 1]
        reach_out = CUR_RIM - REACH * (step + 1)
        before_pad = 0 if before is cur_ref else PAD
        out_pad, out_at = (0, CUR_RIM) if out is final_ref else (PAD, 0)

        def advance(plane, rows, centre, lap):
            back = before[plane, rows.start + before_pad : rows.stop + before_pad, :]
            out[plane - out_at, rows.start + out_pad : rows.stop + out_pad, :] = (
                2.0 * centre - back + factor[plane, rows, :] * lap
            )

        def rim_planes(chunk, _):
            def use(k, rows, centre, lap):
                advance(chunk * CHUNK + k, rows, centre, lap)

            laplace(now, chunk * CHUNK, band, use)
            return 0

        def own_planes(chunk, _):
            begin = chunk * CHUNK

            def use(k, rows, centre, lap):
                weight = adjoint_ref[step, begin + k, rows, :].astype(jnp.float32)
                so_far = total_ref if step == 1 else total
                total[begin + k, rows, :] = so_far[begin + k, rows, :] + weight * lap
                advance(CUR_RIM + begin + k, rows, centre, lap)

            laplace(now, CUR_RIM + begin, band, use)
            share = NREC * CHUNK // PLANES
            for k in range(share):
                collect(now, PAD, CUR_RIM, step - 1, chunk * share + k)
            return 0

        first, last = stretch(has_low, has_high, reach_out)
        if reach_out > 0:
            lax.fori_loop(first // CHUNK, CUR_RIM // CHUNK, rim_planes, 0)
        lax.fori_loop(0, PLANES // CHUNK, own_planes, 0)
        if reach_out > 0:
            lax.fori_loop((CUR_RIM + PLANES) // CHUNK, last // CHUNK, rim_planes, 0)
        inject(out, out_pad, out_at, step, first, last)

    def collect_last(k, _):
        collect(final_ref, 0, 0, STEPS - 1, k)
        return 0

    lax.fori_loop(0, NREC, collect_last, 0, unroll=16)
    for step in range(STEPS):
        records_ref[step : step + 1, :] = jnp.sum(
            (rows_ref[step] * pick_ref[...]).T, axis=0, keepdims=True
        )

    def scale(plane, _):
        total[plane] = (2.0 * courant * courant) * speed[CUR_RIM + plane] * total[plane]
        return 0

    lax.fori_loop(0, PLANES, scale, 0)

    shrunk = []
    for k in range(-1, SHOTS + 1):
        value = 0.0
        for plane, weight in ((2 * k - 1, 0.25), (2 * k, 0.75), (2 * k + 1, 0.75), (2 * k + 2, 0.25)):
            if 0 <= plane < PLANES:
                value = value + weight * total[plane]
        high, low = halves(value)
        stacked = jnp.concatenate([high, low], axis=0)
        shrunk.append(jnp.dot(short_ref[...], stacked, preferred_element_type=jnp.float32))
    sides = [jnp.concatenate([z[:16], z[16:]], axis=1) for z in shrunk]
    high, low = halves(jnp.concatenate(sides, axis=0))
    narrow = narrow_ref[...]
    out = jnp.dot(high, narrow, preferred_element_type=jnp.float32) + jnp.dot(
        low, narrow, preferred_element_type=jnp.float32
    )
    below = out[:16]
    above = out[16 * (SHOTS + 1) :]
    for k in range(SHOTS):
        piece = out[16 * (k + 1) : 16 * (k + 2)]
        if k == 0:
            piece = piece + jnp.where(has_low, 0.0, below)
        if k == SHOTS - 1:
            piece = piece + jnp.where(has_high, 0.0, above)
        terms_ref[shot ^ k] = piece
    edges_ref[0] = jnp.where(has_low, below, 0.0)
    edges_ref[1] = jnp.where(has_high, above, 0.0)


def wave(*args):
    return pl.pallas_call(
        wave_kernel,
        out_shape=(
            jax.ShapeDtypeStruct((PLANES, FY, FX), jnp.float32),
            jax.ShapeDtypeStruct((SHOTS, 16, 128), jnp.float32),
            jax.ShapeDtypeStruct((2, 16, 128), jnp.float32),
            jax.ShapeDtypeStruct((STEPS, NREC), jnp.float32),
        ),
        in_specs=[SMEM] * 3 + [VMEM] * 14,
        out_specs=(VMEM,) * 4,
        scratch_shapes=[
            pltpu.VMEM((EXT, ROWS, FX), jnp.float32),
            pltpu.VMEM((EXT, ROWS, FX), jnp.float32),
            pltpu.VMEM((EXT, FY, FX), jnp.float32),
            pltpu.VMEM((3 * SHOTS, FY, FX), jnp.float32),
            pltpu.VMEM((EXT, FY, FX), jnp.float32),
            pltpu.VMEM((PLANES, FY, FX), jnp.float32),
            pltpu.VMEM((STEPS, NREC, FX), jnp.float32),
        ],
        compiler_params=PARAMS,
    )(*args)


def finish_kernel(term_ref, records_ref, gradient_ref, traces_ref):
    shot = lax.axis_index("slab") % SHOTS
    for j in range(16):
        gradient_ref[:, 128 * j : 128 * (j + 1)] = term_ref[j : j + 1, :]
    for j in range(SHOTS):
        traces_ref[shot ^ j] = records_ref[j]


def finish(term, records):
    return pl.pallas_call(
        finish_kernel,
        out_shape=(
            jax.ShapeDtypeStruct((1, CELLS), jnp.float32),
            jax.ShapeDtypeStruct((SHOTS, STEPS, NREC), jnp.float32),
        ),
        in_specs=[VMEM, VMEM],
        out_specs=(VMEM, VMEM),
        compiler_params=PARAMS,
    )(term, records)


def shift(value, steps):
    count = lax.axis_size("slab")
    begin, end = max(0, -steps), min(count, count - steps)
    return lax.ppermute(value, "slab", [(source, source + steps) for source in range(begin, end)])


def across_chips(value):
    count = lax.axis_size("slab")
    pairs = [(i, i + 1) for i in range(1, count - 1, 2)]
    return lax.ppermute(value, "slab", pairs + [(b, a) for a, b in pairs])


def partner(value, mask):
    count = lax.axis_size("slab")
    return lax.ppermute(value, "slab", [(source, source ^ mask) for source in range(count)])


def body(
    latent, conv1_weight, conv2_weight, head, p_prev, p_cur, adjoint, wavelet, sources, receivers
):
    position = lax.axis_index("slab")
    devices = lax.axis_size("slab")
    slabs = devices // SHOTS
    shot = position % SHOTS
    slab = position // SHOTS
    has_low = slab > 0
    has_high = slab < slabs - 1

    def exchange(to_low, to_high):
        if slabs == 2:
            got = partner(to_low if to_low is to_high else jnp.where(has_low, to_low, to_high), SHOTS)
            return got, got
        return shift(to_high, SHOTS), shift(to_low, -SHOTS)

    latent = latent.reshape(CH, CELLS)
    latent_far, latent_near = across_chips(latent), partner(latent, 1)
    current = p_cur[0]
    previous = p_prev[0]
    to_low = jnp.concatenate([previous[:PREV_RIM], current], axis=0).astype(jnp.bfloat16)
    to_high = jnp.concatenate([previous[PLANES - PREV_RIM :], current], axis=0).astype(jnp.bfloat16)
    to_low = [to_low[begin:end] for begin, end in zip(PARTS[:-1], PARTS[1:])]
    to_high = [to_high[begin:end] for begin, end in zip(PARTS[:-1], PARTS[1:])]
    low_0, high_0 = exchange(to_low[0], to_high[0])

    hidden = first_conv(latent_near, latent, latent_far, conv1_weight, latent_near, latent_near)
    hidden_far, hidden_near = across_chips(hidden), partner(hidden, 1)
    velocity = second_conv(
        hidden_near, hidden, hidden_far, conv2_weight, head[None], low_0, high_0
    )
    late = to_low[1], to_high[1]
    late, velocity_tied = lax.optimization_barrier((late, hidden_far))
    low_1, high_1 = exchange(*late)

    block = velocity[None]
    for bit in range(3):
        block = jnp.concatenate([block, partner(block, 1 << bit)], axis=0)
    block, low_1, high_1 = lax.optimization_barrier((block, low_1, high_1))
    speed_low, speed_high = exchange(block, block)

    stations = jnp.transpose(receivers, (1, 0, 2))
    adjoint = adjoint[:, 0]
    band = band_matrix()
    prepared = prepare(
        current,
        previous,
        low_0,
        low_1,
        high_0,
        high_1,
        adjoint[0],
        stations,
        band,
    )
    final, terms, edges, record = wave(
        wavelet.T,
        sources.T,
        stations,
        *prepared,
        adjoint,
        block,
        speed_low,
        speed_high,
        *plane_matrices(),
        band,
    )

    if slabs == 2:
        message = jnp.concatenate([jnp.where(has_low, edges[0], edges[1]), record], axis=0)
        got = partner(message, SHOTS)
        edge_low = jnp.where(has_low, got[:16], 0.0)
        edge_high = jnp.where(has_high, got[:16], 0.0)
        record = record + got[16:]
    else:
        edge_low, edge_high = shift(edges[1], SHOTS), shift(edges[0], -SHOTS)
        mask = SHOTS
        while mask < devices:
            record = record + partner(record, mask)
            mask *= 2
    place = jnp.arange(SHOTS)[:, None, None]
    terms = terms + jnp.where(place == shot, edge_low, 0.0)
    terms = terms + jnp.where(place == shot ^ (SHOTS - 1), edge_high, 0.0)
    terms = terms.reshape(SHOTS * 16, 128)
    records = record
    for bit in reversed(range(3)):
        half = terms.shape[0] // 2
        size = records.shape[0]
        got = partner(jnp.concatenate([terms[half:], records], axis=0), 1 << bit)
        terms = terms[:half] + got[:half]
        records = jnp.concatenate([records, got[half:]], axis=0)
    order = [4 * (j & 1) + (j & 2) + (j >> 2) for j in range(SHOTS)]
    records = records.reshape(SHOTS, STEPS, NREC)
    records = jnp.stack([records[order.index(j)] for j in range(SHOTS)])
    gradient, traces = finish(terms, records)
    return (final[None], traces, gradient)


def solution(mesh):
    in_specs = (
        P(None, ("groups", "slab"), None),
        P(),
        P(),
        P(),
        P(("groups", "slab"), None, None, None),
        P(("groups", "slab"), None, None, None),
        P(None, ("groups", "slab"), None, None, None),
        P("groups", None),
        P("groups", None),
        P("groups", None, None),
    )
    out_specs = (
        P(("groups", "slab"), None, None, None),
        P("groups", None, None),
        P(("groups", "slab"), None),
    )
    return jax.shard_map(body, mesh=mesh, in_specs=in_specs, out_specs=out_specs, check_vma=False)
```

time: 89.4 us -> 69.1 us (0.77)
  starting transfers between devices: 43.9 us -> 21.8 us
  waiting for transfers between devices: 11.6 us -> 29.8 us
  Pallas kernels: 22.6 us -> 13.6 us
  local copies, waits for them, and re-layouts: 5.54 us -> 0.26 us
  other arithmetic: 3.64 us -> 2.38 us
    ppermute x9 -> x12, waiting for transfers between devices: 11.5 us -> 29.8 us  [partner(): lax.ppermute(value, 'slab', [(source, source ^ mask) for source in range(...]
    ppermute x9 -> x12, starting transfers between devices: 36.5 us -> 20.3 us  [partner(): lax.ppermute(value, 'slab', [(source, source ^ mask) for source in range(...]
    pallas_call x1, Pallas kernels: 17.9 us -> 8.08 us  [wave(): pl.pallas_call(wave_kernel, out_shape=(jax.ShapeDtypeStruct((PLANES, FY,...]
    ppermute x4 -> x2, starting transfers between devices: 7.42 us -> 1.47 us  [across_chips(): return lax.ppermute(value, 'slab', pairs + [(b, a) for a, b in pairs])]
    unnamed x34 -> x36, local copies, waits for them, and re-layouts: 2.59 us -> 0.14 us
    pallas_call x0 -> x1, Pallas kernels: none -> 2.32 us  [prepare(): pl.pallas_call(prepare_kernel, out_shape=(ext, ext, ext, jax.ShapeDtypeSt...]
    another operation x1 -> x0, local copies, waits for them, and re-layouts: 1.33 us -> none  [body(): jnp.stack([shot, has_low.astype(jnp.int32), has_high.astype(jnp.int32), s...]
    another operation x3 -> x2, other arithmetic: 1.13 us -> 2.16 us
  transfers between devices with their start and end apart: 13 -> 14, of which waited for: 9 -> 9; matrix products, arithmetic and copies ran while one was open for 7% -> 3% of each run, Pallas kernels for 4% -> 5%
where the time goes in v2:
time: 69.1 us; the launch traced here: 68.9 us
  waiting for transfers between devices  29.8 us (43%)
  starting transfers between devices  21.8 us (32%)
  Pallas kernels  13.6 us (20%)
  other arithmetic  2.38 us (3%)
  between operations  1.03 us (1%)
    ppermute x12, waiting for transfers between devices, partner(): lax.ppermute(value, 'slab', [(source, source ^ mask) for source in range(...  29.8 us
    ppermute x12, starting transfers between devices, partner(): lax.ppermute(value, 'slab', [(source, source ^ mask) for source in range(...  20.3 us
    pallas_call x1, Pallas kernels, wave(): pl.pallas_call(wave_kernel, out_shape=(jax.ShapeDtypeStruct((PLANES, FY,...  8.08 us
    pallas_call x1, Pallas kernels, prepare(): pl.pallas_call(prepare_kernel, out_shape=(ext, ext, ext, jax.ShapeDtypeSt...  2.32 us
    another operation x2, other arithmetic  2.16 us
    ppermute x2, starting transfers between devices, across_chips(): return lax.ppermute(value, 'slab', pairs + [(b, a) for a, b in pairs])  1.47 us
  transfers between devices with their start and end apart: 14, of which 9 were waited for; matrix products, arithmetic and copies ran while one was open for 3% of the time, Pallas kernels for 5%

profile of v2, /device:TPU:0, one launch (start us, length us, event | category | flops | bytes accessed | tf_op | source)
XLA Modules:
  0.0 68.9 jit_solution(9204738450650862681)
XLA Ops:
  0.6 0.0 copy-start.4
  0.6 0.0 copy-start.6
  0.6 0.5 collective-permute-start.1
  1.2 0.7 collective-permute-start.2
  1.8 1.1 %convert.12 = bf16[1,16,64,128]{3,2,1,0:T(8,128)(2,1)S(1)} convert(f32[1,16,64,128]{3,2,1,0:T(8,128)} %param.19) | non-fusion elementwise | flops 131072 | bytes 786432 | tf_op jit(solution)/shard_map/convert.7
  2.9 1.1 %bitcast_convert_fusion = bf16[16,64,128]{2,1,0:T(8,128)(2,1)S(1)} fusion(f32[1,16,64,128]{3,2,1,0:T(8,128)} %param.20), kind=kLoop, calls=%fused_computation.38 | loop fusion | flops 131072 | bytes 786432 | tf_op jit(solution)/shard_map/convert.5
  4.0 0.1 slice_bitcast_fusion.2
  4.1 0.0 copy-start.3
  4.1 0.0 copy-start.14
  4.2 6.4 %collective-permute-start = (bf16[20,64,128]{2,1,0:T(8,128)(2,1)S(1)}, bf16[20,64,128]{2,1,0:T(8,128)(2,1)S(1)}, u32[]{:S(2)}, u32[]{:S(2)}) collective-permute-start(bf16[20,64,128]{2,1,0:T(8,128)(2,1)S(1)} %fusion), channel_id=1, source_target_pairs={{0,8},{1,9},{2,10},{3,11},{4,12},{5,13},{6,14},{7,15},{8,0},{9,1},... | collective-permute-start | bytes 983048 | tf_op jit(solution)/shard_map/ppermute | solution.py:575
  10.6 0.0 collective-permute-done.1.near_ref.low_part.high_part
  10.6 0.0 collective-permute-done.2.far_ref
  10.6 0.0 copy-done.4
  10.6 0.0 copy-done.6
  10.6 1.2 %shard_map.166.mid_ref = bf16[64,2048]{1,0:T(8,128)(2,1)S(1)} custom-call(bf16[64,2048]{1,0:T(8,128)(2,1)S(1)} %collective-permute-done.1.near_ref.low_part.high_part, bf16[64,2048]{1,0:T(8,128)(2,1)S(1)} %bitcast.55, bf16[64,2048]{1,0:T(8,128)(2,1)S(1)} %collective-permute-done.2.far_ref, bf16[27,64,64]{2,1,0:T(8,128)(2,1)S(1)} %copy-done.4, ...), custom_call_target="tpu_custom_call" | custom-call | tf_op jit(solution)/shard_map/pallas_call | solution.py:131
  11.8 0.0 copy-start.2
  11.9 0.0 copy-start
  11.9 0.0 copy-start.1
  11.9 0.0 copy-start.5
  11.9 0.0 copy-start.9
  11.9 0.8 %collective-permute-start.4 = (bf16[64,2048]{1,0:T(8,128)(2,1)S(1)}, bf16[64,2048]{1,0:T(8,128)(2,1)S(1)}, u32[]{:S(2)}, u32[]{:S(2)}) collective-permute-start(bf16[64,2048]{1,0:T(8,128)(2,1)S(1)} %shard_map.166.mid_ref), channel_id=1, source_target_pairs={{1,2},{3,4},{5,6},{7,8},{9,10},{11,12},{13,14},{2,1},{4,3},{6,5},{... | collective-permute-start | bytes 786440 | tf_op jit(solution)/shard_map/ppermute | solution.py:570
  12.7 5.3 %collective-permute-start.3 = (bf16[64,2048]{1,0:T(8,128)(2,1)S(1)}, bf16[64,2048]{1,0:T(8,128)(2,1)S(1)}, u32[]{:S(2)}, u32[]{:S(2)}) collective-permute-start(bf16[64,2048]{1,0:T(8,128)(2,1)S(1)} %shard_map.166.mid_ref), channel_id=1, source_target_pairs={{0,1},{1,0},{2,3},{3,2},{4,5},{5,4},{6,7},{7,6},{8,9},{9,8},{10,11... | collective-permute-start | bytes 786440 | tf_op jit(solution)/shard_map/ppermute | solution.py:575
  18.1 8.8 %collective-permute-done.low_part.high_part.low_0.high_0 = bf16[20,64,128]{2,1,0:T(8,128)(2,1)S(1)} collective-permute-done((bf16[20,64,128]{2,1,0:T(8,128)(2,1)S(1)}, bf16[20,64,128]{2,1,0:T(8,128)(2,1)S(1)}, u32[]{:S(2)}, u32[]{:S(2)}) %collective-permute-start) | collective-permute-done | bytes 327712 | tf_op jit(solution)/shard_map/ppermute | solution.py:575
  26.9 0.0 collective-permute-done.4.far_ref
  26.9 0.0 collective-permute-done.3.near_ref
  26.9 0.0 copy-done.3
  26.9 0.0 copy-done.14
  26.9 1.3 %shard_map.167 = bf16[16,128]{1,0:T(8,128)(2,1)S(1)} custom-call(bf16[64,2048]{1,0:T(8,128)(2,1)S(1)} %collective-permute-done.3.near_ref, bf16[64,2048]{1,0:T(8,128)(2,1)S(1)} %shard_map.166.mid_ref, bf16[64,2048]{1,0:T(8,128)(2,1)S(1)} %collective-permute-done.4.far_ref, bf16[27,64,64]{2,1,0:T(8,128)(2,1)S(1)} %copy-done.3, bf16[1,64]{1,0:T(2,128)(2,1)S(1)} %bitcast.64, ...), custom_call_target="tpu_custom_call" | custom-call | tf_op jit(solution)/shard_map/pallas_call | solution.py:142
  28.3 0.1 collective-permute-start.5
  28.4 1.1 %collective-permute-done.5 = bf16[1,16,128]{2,1,0:T(8,128)(2,1)S(1)} collective-permute-done((bf16[1,16,128]{2,1,0:T(8,128)(2,1)S(1)}, bf16[1,16,128]{2,1,0:T(8,128)(2,1)S(1)}, u32[]{:S(2)}, u32[]{:S(2)}) %collective-permute-start.5) | collective-permute-done | bytes 4128 | tf_op jit(solution)/shard_map/ppermute | solution.py:575
  29.5 0.0 copy-start.10
  29.5 0.0 copy-start.11
  29.5 0.0 copy-start.12
  29.5 0.0 copy-start.13
  29.5 2.1 %collective-permute-start.6 = (bf16[2,16,128]{2,1,0:T(8,128)(2,1)S(1)}, bf16[2,16,128]{2,1,0:T(8,128)(2,1)S(1)}, u32[]{:S(2)}, u32[]{:S(2)}) collective-permute-start(bf16[2,16,128]{2,1,0:T(8,128)(2,1)S(1)} %pad_maximum_fusion.8), channel_id=1, source_target_pairs={{0,2},{1,3},{2,0},{3,1},{4,6},{5,7},{6,4},{7,5},{8,10},{9,11},{10,... | collective-permute-start | bytes 24584 | tf_op jit(solution)/shard_map/ppermute | solution.py:575
  31.6 1.9 %collective-permute-start.8 = (bf16[8,64,128]{2,1,0:T(8,128)(2,1)S(1)}, bf16[8,64,128]{2,1,0:T(8,128)(2,1)S(1)}, u32[]{:S(2)}, u32[]{:S(2)}) collective-permute-start(bf16[8,64,128]{2,1,0:T(8,128)(2,1)S(1)} %broadcast_select_fusion), channel_id=1, source_target_pairs={{0,8},{1,9},{2,10},{3,11},{4,12},{5,13},{6,14},{7,15},{8,0},{9,1},... | collective-permute-start | bytes 393224 | tf_op jit(solution)/shard_map/ppermute | solution.py:575
  33.5 0.0 collective-permute-done.6
  33.5 2.0 %collective-permute-start.7 = (bf16[4,16,128]{2,1,0:T(8,128)(2,1)S(1)}, bf16[4,16,128]{2,1,0:T(8,128)(2,1)S(1)}, u32[]{:S(2)}, u32[]{:S(2)}) collective-permute-start(bf16[4,16,128]{2,1,0:T(8,128)(2,1)S(1)} %pad_maximum_fusion.5), channel_id=1, source_target_pairs={{0,4},{1,5},{2,6},{3,7},{4,0},{5,1},{6,2},{7,3},{8,12},{9,13},{10,... | collective-permute-start | bytes 49160 | tf_op jit(solution)/shard_map/ppermute | solution.py:575
  35.5 1.9 %collective-permute-done.7 = bf16[4,16,128]{2,1,0:T(8,128)(2,1)S(1)} collective-permute-done((bf16[4,16,128]{2,1,0:T(8,128)(2,1)S(1)}, bf16[4,16,128]{2,1,0:T(8,128)(2,1)S(1)}, u32[]{:S(2)}, u32[]{:S(2)}) %collective-permute-start.7) | collective-permute-done | bytes 16416 | tf_op jit(solution)/shard_map/ppermute | solution.py:575
  37.4 3.5 %collective-permute-done.8.low_1.high_1 = bf16[8,64,128]{2,1,0:T(8,128)(2,1)S(1)} collective-permute-done((bf16[8,64,128]{2,1,0:T(8,128)(2,1)S(1)}, bf16[8,64,128]{2,1,0:T(8,128)(2,1)S(1)}, u32[]{:S(2)}, u32[]{:S(2)}) %collective-permute-start.8) | collective-permute-done | bytes 131104 | tf_op jit(solution)/shard_map/ppermute | solution.py:575
  40.9 0.0 collective-permute-start.9
  40.9 0.0 copy-done.2
  40.9 0.0 copy-done
  40.9 0.0 copy-done.1
  40.9 0.0 copy-done.5
  40.9 0.0 copy-done.9
  41.0 2.3 %shard_map.168 = (f32[48,64,128]{2,1,0:T(8,128)S(1)}, f32[48,64,128]{2,1,0:T(8,128)S(1)}, f32[48,64,128]{2,1,0:T(8,128)S(1)}, f32[16,64,128]{2,1,0:T(8,128)S(1)}, f32[128,128]{1,0:T(8,128)S(1)}) custom-call(f32[16,64,128]{2,1,0:T(8,128)S(1)} %bitcast.50, f32[16,64,128]{2,1,0:T(8,128)S(1)} %bitcast.51, ...), custom_call_target="tpu_custom_call" | custom-call | tf_op jit(solution)/shard_map/pallas_call | solution.py:309
  43.3 2.8 %collective-permute-done.9.low_speed.high_speed = bf16[8,16,128]{2,1,0:T(8,128)(2,1)S(1)} collective-permute-done((bf16[8,16,128]{2,1,0:T(8,128)(2,1)S(1)}, bf16[8,16,128]{2,1,0:T(8,128)(2,1)S(1)}, u32[]{:S(2)}, u32[]{:S(2)}) %collective-permute-start.9) | collective-permute-done | bytes 32800 | tf_op jit(solution)/shard_map/ppermute | solution.py:575
  46.0 0.0 copy-done.7
  46.0 0.0 copy-done.8
  46.0 0.0 copy-done.10
  46.1 0.0 copy-done.11
  46.1 0.0 copy-done.12
  46.1 8.1 %shard_map.169 = (f32[16,64,128]{2,1,0:T(8,128)}, f32[8,16,128]{2,1,0:T(8,128)S(1)}, f32[2,16,128]{2,1,0:T(8,128)S(1)}, f32[4,128]{1,0:T(4,128)S(1)}) custom-call(f32[4,8]{1,0:T(4,128)S(1)} %bitcast.62, s32[3,8]{1,0:T(4,128)S(1)} %bitcast.63, s32[3,8,128]{2,1,0:T(8,128)S(1)} %bitcast.61, f32[48,64,128]{2,1,0:T(8,128)S(1)} %get-tuple-element.23.cur_ref, ...), custom_call_target="tpu_custom_call" | custom-call | tf_op jit(solution)/shard_map/pallas_call | solution.py:517
  54.2 0.3 collective-permute-start.10
  54.4 4.4 %collective-permute-done.10 = f32[20,128]{1,0:T(8,128)S(1)} collective-permute-done((f32[20,128]{1,0:T(8,128)S(1)}, f32[20,128]{1,0:T(8,128)S(1)}, u32[]{:S(2)}, u32[]{:S(2)}) %collective-permute-start.10) | collective-permute-done | bytes 10272 | tf_op jit(solution)/shard_map/ppermute | solution.py:575
  58.8 0.1 select_add_fusion
  59.0 0.9 %collective-permute-start.11 = (f32[68,128]{1,0:T(8,128)S(1)}, f32[68,128]{1,0:T(8,128)S(1)}, u32[]{:S(2)}, u32[]{:S(2)}) collective-permute-start(f32[68,128]{1,0:T(8,128)S(1)} %pad_maximum_fusion.2), channel_id=1, source_target_pairs={{0,4},{1,5},{2,6},{3,7},{4,0},{5,1},{6,2},{7,3},{8,12},{9,13},{10,... | collective-permute-start | bytes 104456 | tf_op jit(solution)/shard_map/ppermute | solution.py:575
  59.9 3.1 %collective-permute-done.11 = f32[68,128]{1,0:T(8,128)S(1)} collective-permute-done((f32[68,128]{1,0:T(8,128)S(1)}, f32[68,128]{1,0:T(8,128)S(1)}, u32[]{:S(2)}, u32[]{:S(2)}) %collective-permute-start.11) | collective-permute-done | bytes 34848 | tf_op jit(solution)/shard_map/ppermute | solution.py:575
  63.0 0.9 %collective-permute-start.12 = (f32[40,128]{1,0:T(8,128)S(1)}, f32[40,128]{1,0:T(8,128)S(1)}, u32[]{:S(2)}, u32[]{:S(2)}) collective-permute-start(f32[40,128]{1,0:T(8,128)S(1)} %pad_maximum_fusion.4), channel_id=1, source_target_pairs={{0,2},{1,3},{2,0},{3,1},{4,6},{5,7},{6,4},{7,5},{8,10},{9,11},{10,... | collective-permute-start | bytes 61448 | tf_op jit(solution)/shard_map/ppermute | solution.py:575
  63.9 3.0 %collective-permute-done.12 = f32[40,128]{1,0:T(8,128)S(1)} collective-permute-done((f32[40,128]{1,0:T(8,128)S(1)}, f32[40,128]{1,0:T(8,128)S(1)}, u32[]{:S(2)}, u32[]{:S(2)}) %collective-permute-start.12) | collective-permute-done | bytes 20512 | tf_op jit(solution)/shard_map/ppermute | solution.py:575
  66.9 0.1 collective-permute-start.13
  67.0 1.2 %collective-permute-done.13 = f32[32,128]{1,0:T(8,128)S(1)} collective-permute-done((f32[32,128]{1,0:T(8,128)S(1)}, f32[32,128]{1,0:T(8,128)S(1)}, u32[]{:S(2)}, u32[]{:S(2)}) %collective-permute-start.13) | collective-permute-done | bytes 16416 | tf_op jit(solution)/shard_map/ppermute | solution.py:575
  68.2 0.6 shard_map.170
  (33 shorter events, 0.2 us)
Async XLA Ops:
  0.6 10.0 %copy-start.4 = (bf16[27,64,64]{2,1,0:T(8,128)(2,1)S(1)}, bf16[27,64,64]{2,1,0:T(8,128)(2,1)}, u32[]{:S(2)}) copy-start(bf16[27,64,64]{2,1,0:T(8,128)(2,1)} %weight_ref.2) | copy-start | bytes 663556
  0.6 10.0 %copy-start.6 = (bf16[64,1,2048]{2,0,1:T(8,128)(2,1)S(1)}, bf16[64,1,2048]{2,0,1:T(8,128)(2,1)}, u32[]{:S(2)}) copy-start(bf16[64,1,2048]{2,0,1:T(8,128)(2,1)} %param.15) | copy-start | bytes 786436
  0.6 9.9 %collective-permute-start.1 = (bf16[64,2048]{1,0:T(8,128)(2,1)}, bf16[64,2048]{1,0:T(8,128)(2,1)S(1)}, u32[]{:S(2)}, u32[]{:S(2)}) collective-permute-start(bf16[64,2048]{1,0:T(8,128)(2,1)} %bitcast.53), channel_id=1, source_target_pairs={{0,1},{1,0},{2,3},{3,2},{4,5},{5,4},{6,7},{7,6},{8,9},{9,8},{10,11... | collective-permute-start | bytes 786440 | tf_op jit(solution)/shard_map/ppermute | solution.py:575
  1.2 9.4 %collective-permute-start.2 = (bf16[64,2048]{1,0:T(8,128)(2,1)}, bf16[64,2048]{1,0:T(8,128)(2,1)S(1)}, u32[]{:S(2)}, u32[]{:S(2)}) collective-permute-start(bf16[64,2048]{1,0:T(8,128)(2,1)} %bitcast.54), channel_id=1, source_target_pairs={{1,2},{3,4},{5,6},{7,8},{9,10},{11,12},{13,14},{2,1},{4,3},{6,5},{... | collective-permute-start | bytes 786440 | tf_op jit(solution)/shard_map/ppermute | solution.py:570
  4.1 22.8 %copy-start.3 = (bf16[27,64,64]{2,1,0:T(8,128)(2,1)S(1)}, bf16[27,64,64]{2,1,0:T(8,128)(2,1)}, u32[]{:S(2)}) copy-start(bf16[27,64,64]{2,1,0:T(8,128)(2,1)} %weight_ref.3) | copy-start | bytes 663556
  4.1 22.8 %copy-start.14 = (bf16[64]{0:T(256)(128)(2,1)S(1)}, bf16[64]{0:T(256)(128)(2,1)}, u32[]{:S(2)}) copy-start(bf16[64]{0:T(256)(128)(2,1)} %param.18) | copy-start | bytes 388
  4.2 22.7 %collective-permute-start = (bf16[20,64,128]{2,1,0:T(8,128)(2,1)S(1)}, bf16[20,64,128]{2,1,0:T(8,128)(2,1)S(1)}, u32[]{:S(2)}, u32[]{:S(2)}) collective-permute-start(bf16[20,64,128]{2,1,0:T(8,128)(2,1)S(1)} %fusion), channel_id=1, source_target_pairs={{0,8},{1,9},{2,10},{3,11},{4,12},{5,13},{6,14},{7,15},{8,0},{9,1},... | collective-permute-start | bytes 983048 | tf_op jit(solution)/shard_map/ppermute | solution.py:575
  11.8 29.0 %copy-start.2 = (bf16[4,1,16,64,128]{4,3,2,1,0:T(8,128)(2,1)S(1)}, bf16[4,1,16,64,128]{4,3,2,1,0:T(8,128)(2,1)}, u32[]{:S(2)}) copy-start(bf16[4,1,16,64,128]{4,3,2,1,0:T(8,128)(2,1)} %param.21) | copy-start | bytes 3145732
  11.9 29.1 %copy-start = (f32[1,16,64,128]{3,2,1,0:T(8,128)S(1)}, f32[1,16,64,128]{3,2,1,0:T(8,128)}, u32[]{:S(2)}) copy-start(f32[1,16,64,128]{3,2,1,0:T(8,128)} %param.20) | copy-start | bytes 1572868
  11.9 29.1 %copy-start.1 = (f32[1,16,64,128]{3,2,1,0:T(8,128)S(1)}, f32[1,16,64,128]{3,2,1,0:T(8,128)}, u32[]{:S(2)}) copy-start(f32[1,16,64,128]{3,2,1,0:T(8,128)} %param.19) | copy-start | bytes 1572868
  11.9 29.1 %copy-start.5 = (bf16[384,128]{1,0:T(8,128)(2,1)S(1)}, bf16[384,128]{1,0:T(8,128)(2,1)}, u32[]{:S(2)}) copy-start(bf16[384,128]{1,0:T(8,128)(2,1)} %constant.45.clone.band_ref) | copy-start | bytes 294916
  11.9 29.1 %copy-start.9 = (s32[8,3,128]{2,0,1:T(8,128)S(1)}, s32[8,3,128]{2,0,1:T(8,128)}, u32[]{:S(2)}) copy-start(s32[8,3,128]{2,0,1:T(8,128)} %param.24) | copy-start | bytes 36868
  11.9 15.0 %collective-permute-start.4 = (bf16[64,2048]{1,0:T(8,128)(2,1)S(1)}, bf16[64,2048]{1,0:T(8,128)(2,1)S(1)}, u32[]{:S(2)}, u32[]{:S(2)}) collective-permute-start(bf16[64,2048]{1,0:T(8,128)(2,1)S(1)} %shard_map.166.mid_ref), channel_id=1, source_target_pairs={{1,2},{3,4},{5,6},{7,8},{9,10},{11,12},{13,14},{2,1},{4,3},{6,5},{... | collective-permute-start | bytes 786440 | tf_op jit(solution)/shard_map/ppermute | solution.py:570
  12.7 14.2 %collective-permute-start.3 = (bf16[64,2048]{1,0:T(8,128)(2,1)S(1)}, bf16[64,2048]{1,0:T(8,128)(2,1)S(1)}, u32[]{:S(2)}, u32[]{:S(2)}) collective-permute-start(bf16[64,2048]{1,0:T(8,128)(2,1)S(1)} %shard_map.166.mid_ref), channel_id=1, source_target_pairs={{0,1},{1,0},{2,3},{3,2},{4,5},{5,4},{6,7},{7,6},{8,9},{9,8},{10,11... | collective-permute-start | bytes 786440 | tf_op jit(solution)/shard_map/ppermute | solution.py:575
  28.3 1.2 %collective-permute-start.5 = (bf16[1,16,128]{2,1,0:T(8,128)(2,1)S(1)}, bf16[1,16,128]{2,1,0:T(8,128)(2,1)S(1)}, u32[]{:S(2)}, u32[]{:S(2)}) collective-permute-start(bf16[1,16,128]{2,1,0:T(8,128)(2,1)S(1)} %bitcast.56), channel_id=1, source_target_pairs={{0,1},{1,0},{2,3},{3,2},{4,5},{5,4},{6,7},{7,6},{8,9},{9,8},{10,11... | collective-permute-start | bytes 12296 | tf_op jit(solution)/shard_map/ppermute | solution.py:575
  29.5 16.6 %copy-start.7 = (bf16[128,256]{1,0:T(8,128)(2,1)S(1)}, bf16[128,256]{1,0:T(8,128)(2,1)}, u32[]{:S(2)}) copy-start(bf16[128,256]{1,0:T(8,128)(2,1)} %constant.46.clone.widen_ref) | copy-start | bytes 196612
  29.5 16.6 %copy-start.8 = (bf16[256,128]{1,0:T(8,128)(2,1)S(1)}, bf16[256,128]{1,0:T(8,128)(2,1)}, u32[]{:S(2)}) copy-start(bf16[256,128]{1,0:T(8,128)(2,1)} %constant.49.clone.narrow_ref) | copy-start | bytes 196612
  29.5 16.6 %copy-start.10 = (bf16[64,64]{1,0:T(8,128)(2,1)S(1)}, bf16[64,64]{1,0:T(8,128)(2,1)}, u32[]{:S(2)}) copy-start(bf16[64,64]{1,0:T(8,128)(2,1)} %constant.47.clone.tall_ref) | copy-start | bytes 24580
  29.5 16.5 %copy-start.11 = (bf16[32,128]{1,0:T(8,128)(2,1)S(1)}, bf16[32,128]{1,0:T(8,128)(2,1)}, u32[]{:S(2)}) copy-start(bf16[32,128]{1,0:T(8,128)(2,1)} %constant.48.clone.short_ref) | copy-start | bytes 24580
  29.5 16.5 %copy-start.12 = (f32[8,4]{0,1:T(4,128)S(1)}, f32[8,4]{0,1:T(4,128)}, u32[]{:S(2)}) copy-start(f32[8,4]{0,1:T(4,128)} %param.22) | copy-start | bytes 388
  29.5 16.5 %copy-start.13 = (s32[8,3]{0,1:T(4,128)S(1)}, s32[8,3]{0,1:T(4,128)}, u32[]{:S(2)}) copy-start(s32[8,3]{0,1:T(4,128)} %param.23) | copy-start | bytes 292
  29.5 3.9 %collective-permute-start.6 = (bf16[2,16,128]{2,1,0:T(8,128)(2,1)S(1)}, bf16[2,16,128]{2,1,0:T(8,128)(2,1)S(1)}, u32[]{:S(2)}, u32[]{:S(2)}) collective-permute-start(bf16[2,16,128]{2,1,0:T(8,128)(2,1)S(1)} %pad_maximum_fusion.8), channel_id=1, source_target_pairs={{0,2},{1,3},{2,0},{3,1},{4,6},{5,7},{6,4},{7,5},{8,10},{9,11},{10,... | collective-permute-start | bytes 24584 | tf_op jit(solution)/shard_map/ppermute | solution.py:575
  31.6 9.2 %collective-permute-start.8 = (bf16[8,64,128]{2,1,0:T(8,128)(2,1)S(1)}, bf16[8,64,128]{2,1,0:T(8,128)(2,1)S(1)}, u32[]{:S(2)}, u32[]{:S(2)}) collective-permute-start(bf16[8,64,128]{2,1,0:T(8,128)(2,1)S(1)} %broadcast_select_fusion), channel_id=1, source_target_pairs={{0,8},{1,9},{2,10},{3,11},{4,12},{5,13},{6,14},{7,15},{8,0},{9,1},... | collective-permute-start | bytes 393224 | tf_op jit(solution)/shard_map/ppermute | solution.py:575
  33.5 3.9 %collective-permute-start.7 = (bf16[4,16,128]{2,1,0:T(8,128)(2,1)S(1)}, bf16[4,16,128]{2,1,0:T(8,128)(2,1)S(1)}, u32[]{:S(2)}, u32[]{:S(2)}) collective-permute-start(bf16[4,16,128]{2,1,0:T(8,128)(2,1)S(1)} %pad_maximum_fusion.5), channel_id=1, source_target_pairs={{0,4},{1,5},{2,6},{3,7},{4,0},{5,1},{6,2},{7,3},{8,12},{9,13},{10,... | collective-permute-start | bytes 49160 | tf_op jit(solution)/shard_map/ppermute | solution.py:575
  40.9 5.2 %collective-permute-start.9 = (bf16[8,16,128]{2,1,0:T(8,128)(2,1)S(1)}, bf16[8,16,128]{2,1,0:T(8,128)(2,1)S(1)}, u32[]{:S(2)}, u32[]{:S(2)}) collective-permute-start(bf16[8,16,128]{2,1,0:T(8,128)(2,1)S(1)} %pad_maximum_fusion.3.own_speed), channel_id=1, source_target_pairs={{0,8},{1,9},{2,10},{3,11},{4,12},{5,13},{6,14},{7,15},{8,0},{9,1},... | collective-permute-start | bytes 98312 | tf_op jit(solution)/shard_map/ppermute | solution.py:575
  54.2 4.7 %collective-permute-start.10 = (f32[20,128]{1,0:T(8,128)S(1)}, f32[20,128]{1,0:T(8,128)S(1)}, u32[]{:S(2)}, u32[]{:S(2)}) collective-permute-start(f32[20,128]{1,0:T(8,128)S(1)} %pad_maximum_fusion.7), channel_id=1, source_target_pairs={{0,8},{1,9},{2,10},{3,11},{4,12},{5,13},{6,14},{7,15},{8,0},{9,1},... | collective-permute-start | bytes 30728 | tf_op jit(solution)/shard_map/ppermute | solution.py:575
  59.0 4.0 %collective-permute-start.11 = (f32[68,128]{1,0:T(8,128)S(1)}, f32[68,128]{1,0:T(8,128)S(1)}, u32[]{:S(2)}, u32[]{:S(2)}) collective-permute-start(f32[68,128]{1,0:T(8,128)S(1)} %pad_maximum_fusion.2), channel_id=1, source_target_pairs={{0,4},{1,5},{2,6},{3,7},{4,0},{5,1},{6,2},{7,3},{8,12},{9,13},{10,... | collective-permute-start | bytes 104456 | tf_op jit(solution)/shard_map/ppermute | solution.py:575
  63.0 3.8 %collective-permute-start.12 = (f32[40,128]{1,0:T(8,128)S(1)}, f32[40,128]{1,0:T(8,128)S(1)}, u32[]{:S(2)}, u32[]{:S(2)}) collective-permute-start(f32[40,128]{1,0:T(8,128)S(1)} %pad_maximum_fusion.4), channel_id=1, source_target_pairs={{0,2},{1,3},{2,0},{3,1},{4,6},{5,7},{6,4},{7,5},{8,10},{9,11},{10,... | collective-permute-start | bytes 61448 | tf_op jit(solution)/shard_map/ppermute | solution.py:575
  66.9 1.2 %collective-permute-start.13 = (f32[32,128]{1,0:T(8,128)S(1)}, f32[32,128]{1,0:T(8,128)S(1)}, u32[]{:S(2)}, u32[]{:S(2)}) collective-permute-start(f32[32,128]{1,0:T(8,128)S(1)} %pad_maximum_fusion.6), channel_id=1, source_target_pairs={{0,1},{1,0},{2,3},{3,2},{4,5},{5,4},{6,7},{7,6},{8,9},{9,8},{10,11... | collective-permute-start | bytes 49160 | tf_op jit(solution)/shard_map/ppermute | solution.py:575

commit v3 on v2

v3 whole, which is shorter than its diff:
```python
import functools

import jax
import jax.numpy as jnp
import numpy as np
from jax import lax
from jax.experimental import pallas as pl
from jax.experimental.pallas import tpu as pltpu
from jax.sharding import PartitionSpec as P

CH = 64
CY = 32
CX = 64
FY = 64
FX = 128
CELLS = CY * CX
SHOTS = 8
STEPS = 4
NREC = 128
PLANES = 16
REACH = 4
CUR_RIM = REACH * STEPS
PREV_RIM = CUR_RIM - REACH
RIM_PLANES = CUR_RIM + PREV_RIM
PARTS = (0, RIM_PLANES)
EXT = PLANES + 2 * CUR_RIM
PAD = 8
ROWS = FY + 2 * PAD
CHUNK = 4

stencil_weights = (-205.0 / 72.0, 8.0 / 5.0, -1.0 / 5.0, 8.0 / 315.0, -1.0 / 560.0)
lowest_speed = 1.5
speed_range = 3.0
courant = 0.088
leak_slope = 0.2

VMEM = pl.BlockSpec(memory_space=pltpu.VMEM)
ANY = pl.BlockSpec(memory_space=pl.ANY)
PARAMS = pltpu.CompilerParams(vmem_limit_bytes=24 * 1024 * 1024)


def doubling_matrix(length):
    matrix = np.zeros((2 * length, length), np.float32)
    for k in range(length):
        matrix[2 * k, k] += 0.75
        matrix[2 * k, max(k - 1, 0)] += 0.25
        matrix[2 * k + 1, k] += 0.75
        matrix[2 * k + 1, min(k + 1, length - 1)] += 0.25
    return matrix


def plane_matrices():
    across = doubling_matrix(CX)
    down = doubling_matrix(CY)
    widen = np.zeros((128, 256), np.float32)
    widen[:64, :128] = across.T
    widen[64:, 128:] = across.T
    tall = np.concatenate([down[:, 0::2], down[:, 1::2]], axis=1)
    tall_twice = np.concatenate([tall, tall], axis=1)
    short_twice = np.concatenate([tall.T, tall.T], axis=1)
    narrow = widen.T
    return tuple(jnp.asarray(m, jnp.bfloat16) for m in (widen, tall_twice, short_twice, narrow))


def halves(value):
    high = value.astype(jnp.bfloat16)
    low = (value - high.astype(jnp.float32)).astype(jnp.bfloat16)
    return high, low


def leaky(value):
    return jnp.where(value > 0, value, leak_slope * value)


def at_boundary():
    place = lax.axis_index("slab")
    rank = place % SHOTS
    last = lax.axis_size("slab") - 1
    return ((rank == 0) & (place > 0)) | ((rank == SHOTS - 1) & (place < last))


def conv(near, mid, far, weight_ref, fields, packed):
    odd = lax.axis_index("slab") % 2
    depths = (2 - 2 * odd, 1, 2 * odd)
    column = lax.broadcasted_iota(jnp.int32, (CH, CELLS), 1) % CX
    for part, plane in enumerate((near, mid, far)):
        wide = plane.astype(jnp.float32)
        left = jnp.where(column == 0, 0.0, pltpu.roll(wide, 1, 1)).astype(jnp.bfloat16)
        right = jnp.where(column == CX - 1, 0.0, pltpu.roll(wide, CELLS - 1, 1)).astype(jnp.bfloat16)
        for place, piece in enumerate((left, plane, right)):
            begin = (3 * part + place) * CH
            fields[begin : begin + CH, :] = piece
    for part, depth in enumerate(depths):
        for row in range(3):
            for place in range(3):
                begin = (3 * part + place) * CH
                packed[row * CH : (row + 1) * CH, begin : begin + CH] = weight_ref[
                    9 * depth + 3 * row + place
                ]
    products = jnp.dot(packed[...], fields[...], preferred_element_type=jnp.float32)
    cell = lax.broadcasted_iota(jnp.int32, (CH, CELLS), 1)
    above = jnp.where(cell < CX, 0.0, pltpu.roll(products[:CH], CX, 1))
    below = jnp.where(cell >= CELLS - CX, 0.0, pltpu.roll(products[2 * CH :], CELLS - CX, 1))
    return products[CH : 2 * CH] + above + below


def to_column(row):
    count = row.shape[1]
    here = lax.broadcasted_iota(jnp.int32, (count, count), 0)
    there = lax.broadcasted_iota(jnp.int32, (count, count), 1)
    return jnp.sum(jnp.where(here == there, row, 0), axis=1, keepdims=True)


def first_kernel(
    near_ref, mid_ref, far_ref, extra_ref, weight_ref, out_ref, beyond_ref, fields, packed
):
    near, mid, far = near_ref[...], mid_ref[...], far_ref[...]
    hidden = leaky(conv(near, mid, far, weight_ref, fields, packed))
    out_ref[...] = hidden.astype(jnp.bfloat16)

    @pl.when(at_boundary())
    def _():
        hidden = leaky(conv(mid, far, extra_ref[...], weight_ref, fields, packed))
        beyond_ref[...] = hidden.astype(jnp.bfloat16)


def second_kernel(
    near_ref, mid_ref, far_ref, beyond_ref, weight_ref, head_ref, out_ref, fields, packed
):
    far = jnp.where(at_boundary(), beyond_ref[...], far_ref[...])
    second = leaky(conv(near_ref[...], mid_ref[...], far, weight_ref, fields, packed))
    head = to_column(head_ref[...].astype(jnp.float32))
    logits = jnp.sum(second * head, axis=0, keepdims=True)
    speed = lowest_speed + speed_range * jax.nn.sigmoid(logits)
    for j in range(16):
        out_ref[j : j + 1, :] = speed[:, 128 * j : 128 * (j + 1)].astype(jnp.bfloat16)


CONV_SCRATCH = [
    pltpu.VMEM((9 * CH, CELLS), jnp.bfloat16),
    pltpu.VMEM((3 * CH, 9 * CH), jnp.bfloat16),
]


def first_conv(near, mid, far, extra, weight):
    plane = jax.ShapeDtypeStruct((CH, CELLS), jnp.bfloat16)
    return pl.pallas_call(
        first_kernel,
        out_shape=(plane, plane),
        in_specs=[VMEM] * 5,
        out_specs=(VMEM, VMEM),
        scratch_shapes=CONV_SCRATCH,
        compiler_params=PARAMS,
    )(near, mid, far, extra, weight)


def second_conv(near, mid, far, beyond, weight, head):
    return pl.pallas_call(
        second_kernel,
        out_shape=jax.ShapeDtypeStruct((16, 128), jnp.bfloat16),
        in_specs=[VMEM] * 6,
        out_specs=VMEM,
        scratch_shapes=CONV_SCRATCH,
        compiler_params=PARAMS,
    )(near, mid, far, beyond, weight, head)


def band_matrix():
    band = np.zeros((FX, FX), np.float64)
    for reach, weight in enumerate(stencil_weights):
        for at in range(FX):
            if reach == 0:
                band[at, at] = 3.0 * weight
            elif at + reach < FX:
                band[at, at + reach] = band[at + reach, at] = weight
    high = band.astype(jnp.bfloat16)
    low = (band - high.astype(np.float64)).astype(jnp.bfloat16)
    return jnp.asarray(np.block([[high, low], [high, np.zeros_like(low)]]))


INNER = slice(PAD, PAD + FY)


def laplace(field, first, band, use):
    planes = field[pl.ds(first, CHUNK), INNER, :].reshape(CHUNK * FY, FX)
    high, low = halves(planes)
    across = jnp.dot(
        jnp.concatenate([high, low], axis=1), band, preferred_element_type=jnp.float32
    )
    for row in range(0, FY, 8):
        column = [
            field[first + k - REACH, PAD + row : PAD + row + 8, :]
            for k in range(CHUNK + 2 * REACH)
        ]
        for k in range(CHUNK):
            begin = k * FY + row
            total = across[begin : begin + 8, :FX] + across[begin : begin + 8, FX:]
            for reach in range(1, REACH + 1):
                near = column[k + REACH - reach] + column[k + REACH + reach]
                begin = PAD + row - reach
                near = near + field[first + k, begin : begin + 8, :]
                begin = PAD + row + reach
                near = near + field[first + k, begin : begin + 8, :]
                total = total + stencil_weights[reach] * near
            use(k, slice(row, row + 8), column[k + REACH], total)


def slab_place():
    slab = lax.axis_index("slab") // SHOTS
    slabs = lax.axis_size("slab") // SHOTS
    return slab, slab > 0, slab < slabs - 1


def over_rims(has_low, has_high, planes, size, use):
    count = planes // size
    below, above = CUR_RIM // size - count, (CUR_RIM + PLANES) // size
    if lax.axis_size("slab") == 2 * SHOTS:
        for k in range(count):
            use(jnp.where(has_low, below, above) + k)
        return
    for inside, begin in ((has_low, below), (has_high, above)):

        @pl.when(inside)
        def _():
            for k in range(count):
                use(begin + k)


def clear_rows(field, first, last):
    def one(plane, _):
        field[plane, :PAD, :] = jnp.zeros((PAD, FX), jnp.float32)
        field[plane, PAD + FY :, :] = jnp.zeros((PAD, FX), jnp.float32)
        return 0

    lax.fori_loop(first, last, one, 0, unroll=8)


def clear_beyond(field, has_low, has_high):
    for inside, begin in ((has_low, CUR_RIM - REACH), (has_high, CUR_RIM + PLANES)):

        @pl.when(jnp.logical_not(inside))
        def _():
            for plane in range(begin, begin + REACH):
                field[plane, INNER, :] = jnp.zeros((FY, FX), jnp.float32)


def plan_kernel(stations_ref, sources_ref, pulses_ref, plan_out, pick_out, pulses_out):
    slab, _, _ = slab_place()
    shot = lax.axis_index("slab") % SHOTS
    depth = stations_ref[0, pl.ds(shot, 1), :] - slab * PLANES
    inside = (depth >= 0) & (depth < PLANES)
    column = jnp.where(inside, stations_ref[2, pl.ds(shot, 1), :], -1)
    lane = lax.broadcasted_iota(jnp.int32, (NREC, FX), 1)
    pick_out[...] = jnp.where(to_column(column) == lane, 1.0, 0.0)
    plan_out[:1, :] = (
        (jnp.clip(depth, 0, PLANES - 1) + CUR_RIM) * ROWS + PAD + stations_ref[1, pl.ds(shot, 1), :]
    )
    mine = lax.broadcasted_iota(jnp.int32, (1, SHOTS), 1) == shot
    source = jnp.sum(jnp.where(mine, sources_ref[...], 0), axis=1, keepdims=True)
    plan_out[1:2, :] = jnp.broadcast_to(source[:1] - slab * PLANES + CUR_RIM, (1, FX))
    plan_out[2:3, :] = jnp.broadcast_to(source[1:2] + PAD, (1, FX))
    plan_out[3:4, :] = jnp.broadcast_to(source[2:], (1, FX))
    pulse = jnp.sum(jnp.where(mine, pulses_ref[...], 0.0), axis=1, keepdims=True)
    pulses_out[...] = jnp.broadcast_to(pulse, (STEPS, FX))


def plan_wave(stations, sources, pulses):
    return pl.pallas_call(
        plan_kernel,
        out_shape=(
            jax.ShapeDtypeStruct((4, NREC), jnp.int32),
            jax.ShapeDtypeStruct((NREC, FX), jnp.float32),
            jax.ShapeDtypeStruct((STEPS, FX), jnp.float32),
        ),
        in_specs=[VMEM] * 3,
        out_specs=(VMEM,) * 3,
        compiler_params=PARAMS,
    )(stations, sources, pulses)


def stretch(has_low, has_high, reach_out):
    first = CUR_RIM - jnp.where(has_low, reach_out, 0)
    last = CUR_RIM + PLANES + jnp.where(has_high, reach_out, 0)
    return first, last


def wave_kernel(
    plan,
    pick_ref,
    pulses_ref,
    cur_ref,
    prev_ref,
    low_0,
    high_0,
    adjoint_ref,
    speeds_ref,
    widen_ref,
    tall_ref,
    short_ref,
    narrow_ref,
    band_ref,
    final_out,
    terms_ref,
    copied,
    field_a,
    field_b,
    factor,
    coarse,
    speed,
    total,
    rows_ref,
):
    slab, has_low, has_high = slab_place()
    band = band_ref[...]
    for field in (field_a, field_b):
        clear_rows(field, 0, EXT)
        clear_beyond(field, has_low, has_high)

    for plane in range(PLANES):
        value = cur_ref[plane]
        field_a[CUR_RIM + plane, INNER, :] = value
        field_b[CUR_RIM + plane, INNER, :] = 2.0 * value - prev_ref[plane]

    def load_rim(parts, at_cur, at_prev):
        def rim(plane):
            for ref, begin, end in zip(parts, PARTS[:-1], PARTS[1:]):
                if begin <= plane < end:
                    return ref[plane - begin].astype(jnp.float32)

        for plane in range(CUR_RIM):
            field_a[at_cur + plane, INNER, :] = rim(PREV_RIM + plane)
        for plane in range(PREV_RIM):
            field_b[at_prev + plane, INNER, :] = 2.0 * field_a[
                at_prev + plane, INNER, :
            ] - rim(plane)

    @pl.when(has_low)
    def _():
        load_rim((low_0,), 0, REACH)

    @pl.when(has_high)
    def _():
        load_rim((high_0,), CUR_RIM + PLANES, CUR_RIM + PLANES)

    def widen_block(slab, at):
        block = speeds_ref[pl.ds(slab * SHOTS, SHOTS)].reshape(SHOTS * 16, 128)
        wide = jnp.dot(block, widen_ref[...], preferred_element_type=jnp.float32)
        for k in range(SHOTS):
            piece = wide[16 * k : 16 * (k + 1)]
            both = jnp.concatenate([piece[:, :128], piece[:, 128:]], axis=0)
            high, low = halves(both)
            stacked = jnp.concatenate([high, low], axis=0)
            coarse[at + k] = jnp.dot(
                tall_ref[...], stacked, preferred_element_type=jnp.float32
            )

    widen_block(slab, SHOTS)

    @pl.when(has_low)
    def _():
        widen_block(slab - 1, 0)

    @pl.when(jnp.logical_not(has_low))
    def _():
        coarse[SHOTS - 1] = coarse[SHOTS]

    @pl.when(has_high)
    def _():
        widen_block(slab + 1, 2 * SHOTS)

    @pl.when(jnp.logical_not(has_high))
    def _():
        coarse[2 * SHOTS] = coarse[2 * SHOTS - 1]

    def refine(k):
        here = 0.75 * coarse[k]
        for plane, there in ((2 * k, coarse[k - 1]), (2 * k + 1, coarse[k + 1])):
            value = here + 0.25 * there
            speed[plane] = value
            factor[plane] = (courant * value) * (courant * value)

    for k in range(CUR_RIM // 2, (CUR_RIM + PLANES) // 2):
        refine(k)
    over_rims(has_low, has_high, PREV_RIM, 2, refine)

    source_plane, source_row = plan[1, 0], plan[2, 0]
    lane_row = lax.broadcasted_iota(jnp.int32, (1, FX), 1)

    def inject(field, step, first, last):
        @pl.when((source_plane >= first) & (source_plane < last))
        def _():
            place = (source_plane, pl.ds(source_row, 1), slice(None))
            field[place] = field[place] + jnp.where(
                lane_row == plan[3, 0], pulses_ref[step : step + 1, :], 0.0
            )

    def collect(field, step, k):
        rows_ref[step, pl.ds(k, 1), :] = field.reshape(EXT * ROWS, FX)[pl.ds(plan[0, k], 1), :]

    for step in range(STEPS):
        now, out = (field_a, field_b) if step % 2 == 0 else (field_b, field_a)
        reach_out = CUR_RIM - REACH * (step + 1)

        def advance(plane, rows, centre, lap):
            here = (plane, slice(rows.start + PAD, rows.stop + PAD), slice(None))
            carried = out[here] if step == 0 else 2.0 * centre - out[here]
            out[here] = carried + factor[plane, rows, :] * lap

        def rim_planes(chunk):
            def use(k, rows, centre, lap):
                advance(chunk * CHUNK + k, rows, centre, lap)

            laplace(now, chunk * CHUNK, band, use)

        def own_planes(chunk):
            begin = chunk * CHUNK

            def use(k, rows, centre, lap):
                term = adjoint_ref[step, begin + k, rows, :].astype(jnp.float32) * lap
                if step > 0:
                    term = total[begin + k, rows, :] + term
                total[begin + k, rows, :] = term
                advance(CUR_RIM + begin + k, rows, centre, lap)

            laplace(now, CUR_RIM + begin, band, use)
            share = NREC * CHUNK // PLANES if step > 0 else 0
            for k in range(share):
                collect(now, step - 1, chunk * share + k)

        first, last = stretch(has_low, has_high, reach_out)
        for chunk in range(PLANES // CHUNK):
            own_planes(chunk)
        if reach_out > 0:
            over_rims(has_low, has_high, reach_out, CHUNK, rim_planes)
        inject(out, step, first, last)

    store = pltpu.make_async_copy(
        field_a.at[pl.ds(CUR_RIM, PLANES), pl.ds(PAD, FY), :], final_out, copied
    )
    store.start()
    for k in range(NREC):
        collect(field_a, STEPS - 1, k)
    record = jnp.concatenate(
        [
            jnp.sum((rows_ref[step] * pick_ref[...]).T, axis=0, keepdims=True)
            for step in range(STEPS)
        ]
        + [jnp.zeros((16 - STEPS, FX), jnp.float32)],
        axis=0,
    ).astype(jnp.bfloat16)

    for plane in range(PLANES):
        total[plane] = (2.0 * courant * courant) * speed[CUR_RIM + plane] * total[plane]

    shrunk = []
    for k in range(-1, SHOTS + 1):
        value = 0.0
        for plane, weight in ((2 * k - 1, 0.25), (2 * k, 0.75), (2 * k + 1, 0.75), (2 * k + 2, 0.25)):
            if 0 <= plane < PLANES:
                value = value + weight * total[plane]
        high, low = halves(value)
        stacked = jnp.concatenate([high, low], axis=0)
        shrunk.append(jnp.dot(short_ref[...], stacked, preferred_element_type=jnp.float32))
    sides = [jnp.concatenate([z[:16], z[16:]], axis=1) for z in shrunk]
    high, low = halves(jnp.concatenate(sides, axis=0))
    narrow = narrow_ref[...]
    out = jnp.dot(high, narrow, preferred_element_type=jnp.float32) + jnp.dot(
        low, narrow, preferred_element_type=jnp.float32
    )
    below = out[:16]
    above = out[16 * (SHOTS + 1) :]

    def no_term(position, _):
        terms_ref[position, :16, :] = jnp.zeros((16, 128), jnp.bfloat16)
        terms_ref[position, 16:, :] = record
        return 0

    lax.fori_loop(0, terms_ref.shape[0], no_term, 0, unroll=8)
    for k in range(SHOTS):
        piece = out[16 * (k + 1) : 16 * (k + 2)]
        if k == 0:
            piece = piece + jnp.where(has_low, 0.0, below)
        if k == SHOTS - 1:
            piece = piece + jnp.where(has_high, 0.0, above)
        terms_ref[slab * SHOTS + k, :16, :] = piece.astype(jnp.bfloat16)

    @pl.when(has_low)
    def _():
        terms_ref[slab * SHOTS - 1, :16, :] = below.astype(jnp.bfloat16)

    @pl.when(has_high)
    def _():
        terms_ref[slab * SHOTS + SHOTS, :16, :] = above.astype(jnp.bfloat16)

    store.wait()


def wave(*args):
    devices = lax.axis_size("slab")
    return pl.pallas_call(
        wave_kernel,
        out_shape=(
            jax.ShapeDtypeStruct((PLANES, FY, FX), jnp.float32),
            jax.ShapeDtypeStruct((devices, 32, 128), jnp.bfloat16),
        ),
        in_specs=[pl.BlockSpec(memory_space=pltpu.SMEM)] + [VMEM] * 13,
        out_specs=(ANY, VMEM),
        scratch_shapes=[
            pltpu.SemaphoreType.DMA,
            pltpu.VMEM((EXT, ROWS, FX), jnp.float32),
            pltpu.VMEM((EXT, ROWS, FX), jnp.float32),
            pltpu.VMEM((EXT, FY, FX), jnp.float32),
            pltpu.VMEM((3 * SHOTS, FY, FX), jnp.float32),
            pltpu.VMEM((EXT, FY, FX), jnp.float32),
            pltpu.VMEM((PLANES, FY, FX), jnp.float32),
            pltpu.VMEM((STEPS, NREC, FX), jnp.float32),
        ],
        compiler_params=PARAMS,
    )(*args)


def finish_kernel(terms_ref, gradient_ref, traces_ref):
    devices = terms_ref.shape[0]
    term = terms_ref[0, :16, :].astype(jnp.float32)
    for position in range(1, devices):
        term = term + terms_ref[position, :16, :].astype(jnp.float32)
    for j in range(16):
        gradient_ref[:, 128 * j : 128 * (j + 1)] = term[j : j + 1, :]
    for shot in range(SHOTS):
        record = terms_ref[shot, 16:, :].astype(jnp.float32)
        for position in range(shot + SHOTS, devices, SHOTS):
            record = record + terms_ref[position, 16:, :].astype(jnp.float32)
        traces_ref[shot] = record[:STEPS]


def finish(terms):
    return pl.pallas_call(
        finish_kernel,
        out_shape=(
            jax.ShapeDtypeStruct((1, CELLS), jnp.float32),
            jax.ShapeDtypeStruct((SHOTS, STEPS, NREC), jnp.float32),
        ),
        in_specs=[VMEM],
        out_specs=(VMEM, VMEM),
        compiler_params=PARAMS,
    )(terms)


def shift(value, steps):
    count = lax.axis_size("slab")
    begin, end = max(0, -steps), min(count, count - steps)
    return lax.ppermute(value, "slab", [(source, source + steps) for source in range(begin, end)])


def across_chips(value, boundaries):
    count = lax.axis_size("slab")
    pairs = [(i, i + 1) for i in range(1, count - 1, 2) if boundaries or (i + 1) % SHOTS > 0]
    return lax.ppermute(value, "slab", pairs + [(b, a) for a, b in pairs])


def past_boundary(value):
    pairs = []
    for first in range(SHOTS, lax.axis_size("slab"), SHOTS):
        pairs += [(first + 1, first - 1), (first - 2, first)]
    return lax.ppermute(value, "slab", pairs)


def partner(value, mask):
    count = lax.axis_size("slab")
    return lax.ppermute(value, "slab", [(source, source ^ mask) for source in range(count)])


def body(
    latent, conv1_weight, conv2_weight, head, p_prev, p_cur, adjoint, wavelet, sources, receivers
):
    position = lax.axis_index("slab")
    devices = lax.axis_size("slab")
    slabs = devices // SHOTS
    shot = position % SHOTS
    slab = position // SHOTS
    has_low = slab > 0
    has_high = slab < slabs - 1

    def exchange(to_low, to_high):
        if slabs == 2:
            got = partner(to_low if to_low is to_high else jnp.where(has_low, to_low, to_high), SHOTS)
            return got, got
        return shift(to_high, SHOTS), shift(to_low, -SHOTS)

    latent = latent.reshape(CH, CELLS)
    latent_far, latent_near = across_chips(latent, True), partner(latent, 1)
    latent_extra = past_boundary(latent)
    current = p_cur[0]
    previous = p_prev[0]
    to_low = jnp.concatenate([previous[:PREV_RIM], current], axis=0).astype(jnp.bfloat16)
    to_high = jnp.concatenate([previous[PLANES - PREV_RIM :], current], axis=0).astype(jnp.bfloat16)
    to_low = [to_low[begin:end] for begin, end in zip(PARTS[:-1], PARTS[1:])]
    to_high = [to_high[begin:end] for begin, end in zip(PARTS[:-1], PARTS[1:])]
    to_low, to_high, _ = lax.optimization_barrier(
        (to_low[0], to_high[0], (latent_far, latent_near, latent_extra))
    )
    low_0, high_0 = exchange(to_low, to_high)

    hidden, beyond = first_conv(latent_near, latent, latent_far, latent_extra, conv1_weight)
    hidden_far, hidden_near = across_chips(hidden, False), partner(hidden, 1)
    velocity = second_conv(hidden_near, hidden, hidden_far, beyond, conv2_weight, head[None])
    speeds = lax.all_to_all(
        jnp.broadcast_to(velocity[None], (devices,) + velocity.shape), "slab", 0, 0
    )

    adjoint = adjoint[:, 0]
    plan, pick, pulses = plan_wave(
        jnp.transpose(receivers, (1, 0, 2)), sources.T, wavelet.T
    )
    final, terms = wave(
        plan,
        pick,
        pulses,
        current,
        previous,
        low_0,
        high_0,
        adjoint,
        speeds,
        *plane_matrices(),
        band_matrix(),
    )

    gradient, traces = finish(lax.all_to_all(terms, "slab", 0, 0))
    return (final[None], traces, gradient)


def solution(mesh):
    in_specs = (
        P(None, ("groups", "slab"), None),
        P(),
        P(),
        P(),
        P(("groups", "slab"), None, None, None),
        P(("groups", "slab"), None, None, None),
        P(None, ("groups", "slab"), None, None, None),
        P("groups", None),
        P("groups", None),
        P("groups", None, None),
    )
    out_specs = (
        P(("groups", "slab"), None, None, None),
        P("groups", None, None),
        P(("groups", "slab"), None),
    )
    return jax.shard_map(body, mesh=mesh, in_specs=in_specs, out_specs=out_specs, check_vma=False)
```

time: 69.1 us -> 60.5 us (0.88)
  waiting for transfers between devices: 29.8 us -> 7.89 us
  blocking collectives: 0 us -> 10.5 us
  starting transfers between devices: 21.8 us -> 28.5 us
  Pallas kernels: 13.6 us -> 10.4 us
  other arithmetic: 2.38 us -> 1.24 us
    ppermute x12 -> x3, waiting for transfers between devices: 29.8 us -> 1.16 us  [partner(): lax.ppermute(value, 'slab', [(source, source ^ mask) for source in range(...]
    all_to_all x0 -> x1, blocking collectives: none -> 10.5 us  [body(): gradient, traces = finish(lax.all_to_all(terms, 'slab', 0, 0))]
    all_to_all x0 -> x1, starting transfers between devices: none -> 8.74 us  [body(): lax.all_to_all(jnp.broadcast_to(velocity[None], (devices,) + velocity.sha...]
    all_to_all x0 -> x1, waiting for transfers between devices: none -> 6.72 us  [body(): lax.all_to_all(jnp.broadcast_to(velocity[None], (devices,) + velocity.sha...]
    ppermute x12 -> x3, starting transfers between devices: 20.3 us -> 17.4 us  [partner(): lax.ppermute(value, 'slab', [(source, source ^ mask) for source in range(...]
    pallas_call x2, Pallas kernels: 3.55 us -> 1.59 us  [the longest x1 1.46 us: first_conv(): pl.pallas_call(first_kernel, out_shape=(plane, plane), in_specs=[VMEM] *...]
    pallas_call x1, Pallas kernels: 8.08 us -> 6.81 us  [wave(): pl.pallas_call(wave_kernel, out_shape=(jax.ShapeDtypeStruct((PLANES, FY,...]
    another operation x2, other arithmetic: 2.16 us -> 1.12 us
  transfers between devices with their start and end apart: 14 -> 7, of which waited for: 9 -> 2; matrix products, arithmetic and copies ran while one was open for 3% -> 3% of each run, Pallas kernels for 5% -> 5%
where the time goes in v3:
time: 60.5 us; the launch traced here: 60.2 us
  starting transfers between devices  28.5 us (47%)
  blocking collectives  10.5 us (17%)
  Pallas kernels  10.4 us (17%)
  waiting for transfers between devices  7.89 us (13%)
  other arithmetic  1.24 us (2%)
  between operations  0.95 us (2%)
  local copies, waits for them, and re-layouts  0.79 us (1%)
    ppermute x3, starting transfers between devices, partner(): lax.ppermute(value, 'slab', [(source, source ^ mask) for source in range(...  17.4 us
    all_to_all x1, blocking collectives, body(): gradient, traces = finish(lax.all_to_all(terms, 'slab', 0, 0))  10.5 us
    all_to_all x1, starting transfers between devices, body(): lax.all_to_all(jnp.broadcast_to(velocity[None], (devices,) + velocity.sha...  8.74 us
    pallas_call x1, Pallas kernels, wave(): pl.pallas_call(wave_kernel, out_shape=(jax.ShapeDtypeStruct((PLANES, FY,...  6.81 us
    all_to_all x1, waiting for transfers between devices, body(): lax.all_to_all(jnp.broadcast_to(velocity[None], (devices,) + velocity.sha...  6.72 us
    ppermute x2, starting transfers between devices, across_chips(): return lax.ppermute(value, 'slab', pairs + [(b, a) for a, b in pairs])  1.47 us
    pallas_call x1, Pallas kernels, first_conv(): pl.pallas_call(first_kernel, out_shape=(plane, plane), in_specs=[VMEM] *...  1.46 us
    pallas_call x1, Pallas kernels, second_conv(): pl.pallas_call(second_kernel, out_shape=jax.ShapeDtypeStruct((16, 128), j...  1.34 us
  transfers between devices with their start and end apart: 7, of which 2 were waited for; matrix products, arithmetic and copies ran while one was open for 3% of the time, Pallas kernels for 5%

profile of v3, /device:TPU:0, one launch (start us, length us, event | category | flops | bytes accessed | tf_op | source)
XLA Modules:
  0.0 60.2 jit_solution(8689191153225913091)
XLA Ops:
  0.6 0.0 copy-start
  0.6 0.8 %collective-permute-start.2 = (bf16[64,2048]{1,0:T(8,128)(2,1)}, bf16[64,2048]{1,0:T(8,128)(2,1)S(1)}, u32[]{:S(2)}, u32[]{:S(2)}) collective-permute-start(bf16[64,2048]{1,0:T(8,128)(2,1)} %bitcast.17), channel_id=1, source_target_pairs={{9,7},{6,8},{25,23},{22,24}} | collective-permute-start | bytes 786440 | tf_op jit(solution)/shard_map/ppermute | solution.py:565
  1.5 0.5 collective-permute-start.1
  2.0 0.7 %collective-permute-start = (bf16[64,2048]{1,0:T(8,128)(2,1)}, bf16[64,2048]{1,0:T(8,128)(2,1)S(1)}, u32[]{:S(2)}, u32[]{:S(2)}) collective-permute-start(bf16[64,2048]{1,0:T(8,128)(2,1)} %bitcast.19), channel_id=1, source_target_pairs={{1,2},{3,4},{5,6},{7,8},{9,10},{11,12},{13,14},{2,1},{4,3},{6,5},{... | collective-permute-start | bytes 786440 | tf_op jit(solution)/shard_map/ppermute | solution.py:558
  2.7 1.1 %convert.12 = bf16[1,16,64,128]{3,2,1,0:T(8,128)(2,1)S(1)} convert(f32[1,16,64,128]{3,2,1,0:T(8,128)} %param.19) | non-fusion elementwise | flops 131072 | bytes 786432 | tf_op jit(solution)/shard_map/convert.7
  3.8 0.0 copy-done
  3.8 0.1 slice_bitcast_fusion
  3.9 0.1 pad_maximum_fusion
  4.0 0.0 collective-permute-done.2.extra_ref
  4.0 0.0 collective-permute-done.1.near_ref
  4.0 0.0 collective-permute-done.far_ref
  4.0 0.0 copy-start.3
  4.0 0.0 copy-start.5
  4.0 0.1 broadcast_select_fusion
  4.1 0.0 copy-start.4
  4.1 13.1 %collective-permute-start.3 = (bf16[28,64,128]{2,1,0:T(8,128)(2,1)S(1)}, bf16[28,64,128]{2,1,0:T(8,128)(2,1)S(1)}, u32[]{:S(2)}, u32[]{:S(2)}) collective-permute-start(bf16[28,64,128]{2,1,0:T(8,128)(2,1)S(1)} %broadcast_select_fusion), channel_id=1, source_target_pairs={{0,8},{1,9},{2,10},{3,11},{4,12},{5,13},{6,14},{7,15},{8,0},{9,1},... | collective-permute-start | bytes 1376264 | tf_op jit(solution)/shard_map/ppermute | solution.py:570
  17.2 0.0 copy-done.3
  17.2 0.0 copy-done.5
  17.2 0.0 copy-start.14
  17.2 0.0 copy-start.13
  17.2 0.0 copy-start.7
  17.3 0.0 copy-start.8
  17.3 0.0 copy-start.11
  17.3 1.5 %shard_map.167 = (bf16[64,2048]{1,0:T(8,128)(2,1)S(1)}, bf16[64,2048]{1,0:T(8,128)(2,1)S(1)}) custom-call(bf16[64,2048]{1,0:T(8,128)(2,1)S(1)} %collective-permute-done.1.near_ref, bf16[64,2048]{1,0:T(8,128)(2,1)S(1)} %bitcast.20, bf16[64,2048]{1,0:T(8,128)(2,1)S(1)} %collective-permute-done.far_ref, bf16[64,2048]{1,0:T(8,128)(2,1)S(1)} %collective-permute-done.2.extra_ref, ...), custom_call_target="tpu_custom_call" | custom-call | tf_op jit(solution)/shard_map/pallas_call | solution.py:147
  18.8 0.0 copy-start.2
  18.8 0.8 %collective-permute-start.5 = (bf16[64,2048]{1,0:T(8,128)(2,1)S(1)}, bf16[64,2048]{1,0:T(8,128)(2,1)S(1)}, u32[]{:S(2)}, u32[]{:S(2)}) collective-permute-start(bf16[64,2048]{1,0:T(8,128)(2,1)S(1)} %get-tuple-element.19.mid_ref), channel_id=1, source_target_pairs={{1,2},{3,4},{5,6},{9,10},{11,12},{13,14},{2,1},{4,3},{6,5},{10,9},... | collective-permute-start | bytes 786440 | tf_op jit(solution)/shard_map/ppermute | solution.py:558
  19.6 3.8 %collective-permute-start.4 = (bf16[64,2048]{1,0:T(8,128)(2,1)S(1)}, bf16[64,2048]{1,0:T(8,128)(2,1)S(1)}, u32[]{:S(2)}, u32[]{:S(2)}) collective-permute-start(bf16[64,2048]{1,0:T(8,128)(2,1)S(1)} %get-tuple-element.19.mid_ref), channel_id=1, source_target_pairs={{0,1},{1,0},{2,3},{3,2},{4,5},{5,4},{6,7},{7,6},{8,9},{9,8},{10,11... | collective-permute-start | bytes 786440 | tf_op jit(solution)/shard_map/ppermute | solution.py:570
  23.4 0.0 collective-permute-done.5.far_ref
  23.4 1.2 %collective-permute-done.4.near_ref = bf16[64,2048]{1,0:T(8,128)(2,1)S(1)} collective-permute-done((bf16[64,2048]{1,0:T(8,128)(2,1)S(1)}, bf16[64,2048]{1,0:T(8,128)(2,1)S(1)}, u32[]{:S(2)}, u32[]{:S(2)}) %collective-permute-start.4) | collective-permute-done | bytes 262176 | tf_op jit(solution)/shard_map/ppermute | solution.py:570
  24.5 0.0 copy-done.4
  24.5 0.0 copy-done.14
  24.5 0.0 copy-start.10
  24.5 0.0 copy-start.12
  24.5 0.0 copy-start.1
  24.5 1.3 %shard_map.168 = bf16[16,128]{1,0:T(8,128)(2,1)S(1)} custom-call(bf16[64,2048]{1,0:T(8,128)(2,1)S(1)} %collective-permute-done.4.near_ref, bf16[64,2048]{1,0:T(8,128)(2,1)S(1)} %get-tuple-element.19.mid_ref, bf16[64,2048]{1,0:T(8,128)(2,1)S(1)} %collective-permute-done.5.far_ref, bf16[64,2048]{1,0:T(8,128)(2,1)S(1)} %get-tuple-element.20.beyond_ref, ...), custom_call_target="tpu_custom_call" | custom-call | tf_op jit(solution)/shard_map/pallas_call | solution.py:158
  25.9 0.0 copy-start.6
  25.9 0.6 %broadcast_in_dim.13 = bf16[16,16,128]{2,1,0:T(8,128)(2,1)} broadcast(bf16[16,128]{1,0:T(8,128)(2,1)S(1)} %shard_map.168), dimensions={1,2} | broadcast | bytes 69632 | tf_op jit(solution)/shard_map/broadcast_in_dim | solution.py:608
  26.5 8.7 %all-to-all-start = ((bf16[16,16,128]{2,1,0:T(8,128)(2,1)}), bf16[16,16,128]{2,1,0:T(8,128)(2,1)S(1)}, u32[]{:S(2)}, u32[]{:S(2)}) async-start(bf16[16,16,128]{2,1,0:T(8,128)(2,1)} %broadcast_in_dim.13), calls=%async_computation | async-start | bytes 131072 | tf_op jit(solution)/shard_map/all_to_all | solution.py:607
  35.3 0.0 copy-start.9
  35.3 0.0 copy-done.13
  35.3 0.0 copy-done.10
  35.3 0.0 copy-done.12
  35.3 0.1 shard_map.166
  35.5 6.7 %all-to-all-done.speeds_ref = bf16[16,16,128]{2,1,0:T(8,128)(2,1)S(1)} async-done(((bf16[16,16,128]{2,1,0:T(8,128)(2,1)}), bf16[16,16,128]{2,1,0:T(8,128)(2,1)S(1)}, u32[]{:S(2)}, u32[]{:S(2)}) %all-to-all-start) | async-done | bytes 65568 | tf_op jit(solution)/shard_map/all_to_all | solution.py:607
  42.2 0.0 collective-permute-done.3.low_0.high_0
  42.2 0.0 copy-done.7
  42.2 0.0 copy-done.8
  42.2 0.0 copy-done.11
  42.2 0.0 copy-done.2
  42.2 0.0 copy-done.1
  42.2 0.0 copy-done.6
  42.2 0.0 copy-done.9
  42.2 6.8 %shard_map.169 = (f32[16,64,128]{2,1,0:T(8,128)}, bf16[16,32,128]{2,1,0:T(8,128)(2,1)S(1)}) custom-call(s32[4,128]{1,0:T(4,128)S(1)} %get-tuple-element.14.plan, f32[128,128]{1,0:T(8,128)S(1)} %get-tuple-element.15.pick_ref, f32[4,128]{1,0:T(4,128)S(1)} %get-tuple-element.16.pulses_ref, f32[16,64,128]{2,1,0:T(8,128)S(1)} %bitcast.14, ...), custom_call_target="tpu_custom_call" | custom-call | tf_op jit(solution)/shard_map/pallas_call | solution.py:500
  49.1 10.5 %all_to_all.10.terms_ref = bf16[16,32,128]{2,1,0:T(8,128)(2,1)S(1)} all-to-all(bf16[16,32,128]{2,1,0:T(8,128)(2,1)S(1)} %get-tuple-element.22), channel_id=1, replica_groups=mesh['groups'=2,'slab'=16] {'slab'}, dimensions={0} | all-to-all | bytes 262144 | tf_op jit(solution)/shard_map/all_to_all | solution.py:629
  59.6 0.6 %shard_map.170 = (f32[1,2048]{1,0:T(1,128)}, f32[8,4,128]{2,1,0:T(4,128)}) custom-call(bf16[16,32,128]{2,1,0:T(8,128)(2,1)S(1)} %all_to_all.10.terms_ref), custom_call_target="tpu_custom_call" | custom-call | tf_op jit(solution)/shard_map/pallas_call | solution.py:537
  (1 shorter events, 0.0 us)
Async XLA Ops:
  0.6 3.1 %copy-start = (f32[1,16,64,128]{3,2,1,0:T(8,128)S(1)}, f32[1,16,64,128]{3,2,1,0:T(8,128)}, u32[]{:S(2)}) copy-start(f32[1,16,64,128]{3,2,1,0:T(8,128)} %param.20) | copy-start | bytes 1572868
  0.6 3.3 %collective-permute-start.2 = (bf16[64,2048]{1,0:T(8,128)(2,1)}, bf16[64,2048]{1,0:T(8,128)(2,1)S(1)}, u32[]{:S(2)}, u32[]{:S(2)}) collective-permute-start(bf16[64,2048]{1,0:T(8,128)(2,1)} %bitcast.17), channel_id=1, source_target_pairs={{9,7},{6,8},{25,23},{22,24}} | collective-permute-start | bytes 786440 | tf_op jit(solution)/shard_map/ppermute | solution.py:565
  1.5 2.5 %collective-permute-start.1 = (bf16[64,2048]{1,0:T(8,128)(2,1)}, bf16[64,2048]{1,0:T(8,128)(2,1)S(1)}, u32[]{:S(2)}, u32[]{:S(2)}) collective-permute-start(bf16[64,2048]{1,0:T(8,128)(2,1)} %bitcast.18), channel_id=1, source_target_pairs={{0,1},{1,0},{2,3},{3,2},{4,5},{5,4},{6,7},{7,6},{8,9},{9,8},{10,11... | collective-permute-start | bytes 786440 | tf_op jit(solution)/shard_map/ppermute | solution.py:570
  2.0 2.0 %collective-permute-start = (bf16[64,2048]{1,0:T(8,128)(2,1)}, bf16[64,2048]{1,0:T(8,128)(2,1)S(1)}, u32[]{:S(2)}, u32[]{:S(2)}) collective-permute-start(bf16[64,2048]{1,0:T(8,128)(2,1)} %bitcast.19), channel_id=1, source_target_pairs={{1,2},{3,4},{5,6},{7,8},{9,10},{11,12},{13,14},{2,1},{4,3},{6,5},{... | collective-permute-start | bytes 786440 | tf_op jit(solution)/shard_map/ppermute | solution.py:558
  4.0 13.2 %copy-start.3 = (bf16[27,64,64]{2,1,0:T(8,128)(2,1)S(1)}, bf16[27,64,64]{2,1,0:T(8,128)(2,1)}, u32[]{:S(2)}) copy-start(bf16[27,64,64]{2,1,0:T(8,128)(2,1)} %weight_ref.2) | copy-start | bytes 663556
  4.0 13.2 %copy-start.5 = (bf16[64,1,2048]{2,0,1:T(8,128)(2,1)S(1)}, bf16[64,1,2048]{2,0,1:T(8,128)(2,1)}, u32[]{:S(2)}) copy-start(bf16[64,1,2048]{2,0,1:T(8,128)(2,1)} %param.15) | copy-start | bytes 786436
  4.1 20.4 %copy-start.4 = (bf16[27,64,64]{2,1,0:T(8,128)(2,1)S(1)}, bf16[27,64,64]{2,1,0:T(8,128)(2,1)}, u32[]{:S(2)}) copy-start(bf16[27,64,64]{2,1,0:T(8,128)(2,1)} %weight_ref.3) | copy-start | bytes 663556
  4.1 38.1 %collective-permute-start.3 = (bf16[28,64,128]{2,1,0:T(8,128)(2,1)S(1)}, bf16[28,64,128]{2,1,0:T(8,128)(2,1)S(1)}, u32[]{:S(2)}, u32[]{:S(2)}) collective-permute-start(bf16[28,64,128]{2,1,0:T(8,128)(2,1)S(1)} %broadcast_select_fusion), channel_id=1, source_target_pairs={{0,8},{1,9},{2,10},{3,11},{4,12},{5,13},{6,14},{7,15},{8,0},{9,1},... | collective-permute-start | bytes 1376264 | tf_op jit(solution)/shard_map/ppermute | solution.py:570
  17.2 7.3 %copy-start.14 = (bf16[64]{0:T(256)(128)(2,1)S(1)}, bf16[64]{0:T(256)(128)(2,1)}, u32[]{:S(2)}) copy-start(bf16[64]{0:T(256)(128)(2,1)} %param.18) | copy-start | bytes 388
  17.2 18.1 %copy-start.13 = (f32[8,4]{0,1:T(4,128)S(1)}, f32[8,4]{0,1:T(4,128)}, u32[]{:S(2)}) copy-start(f32[8,4]{0,1:T(4,128)} %param.22) | copy-start | bytes 388
  17.2 24.9 %copy-start.7 = (bf16[256,128]{1,0:T(8,128)(2,1)S(1)}, bf16[256,128]{1,0:T(8,128)(2,1)}, u32[]{:S(2)}) copy-start(bf16[256,128]{1,0:T(8,128)(2,1)} %constant.34.clone.narrow_ref) | copy-start | bytes 196612
  17.3 24.9 %copy-start.8 = (bf16[128,256]{1,0:T(8,128)(2,1)S(1)}, bf16[128,256]{1,0:T(8,128)(2,1)}, u32[]{:S(2)}) copy-start(bf16[128,256]{1,0:T(8,128)(2,1)} %constant.31.clone.widen_ref) | copy-start | bytes 196612
  17.3 24.9 %copy-start.11 = (bf16[32,128]{1,0:T(8,128)(2,1)S(1)}, bf16[32,128]{1,0:T(8,128)(2,1)}, u32[]{:S(2)}) copy-start(bf16[32,128]{1,0:T(8,128)(2,1)} %constant.33.clone.short_ref) | copy-start | bytes 24580
  18.8 23.4 %copy-start.2 = (bf16[4,1,16,64,128]{4,3,2,1,0:T(8,128)(2,1)S(1)}, bf16[4,1,16,64,128]{4,3,2,1,0:T(8,128)(2,1)}, u32[]{:S(2)}) copy-start(bf16[4,1,16,64,128]{4,3,2,1,0:T(8,128)(2,1)} %param.21) | copy-start | bytes 3145732
  18.8 4.6 %collective-permute-start.5 = (bf16[64,2048]{1,0:T(8,128)(2,1)S(1)}, bf16[64,2048]{1,0:T(8,128)(2,1)S(1)}, u32[]{:S(2)}, u32[]{:S(2)}) collective-permute-start(bf16[64,2048]{1,0:T(8,128)(2,1)S(1)} %get-tuple-element.19.mid_ref), channel_id=1, source_target_pairs={{1,2},{3,4},{5,6},{9,10},{11,12},{13,14},{2,1},{4,3},{6,5},{10,9},... | collective-permute-start | bytes 786440 | tf_op jit(solution)/shard_map/ppermute | solution.py:558
  19.6 4.9 %collective-permute-start.4 = (bf16[64,2048]{1,0:T(8,128)(2,1)S(1)}, bf16[64,2048]{1,0:T(8,128)(2,1)S(1)}, u32[]{:S(2)}, u32[]{:S(2)}) collective-permute-start(bf16[64,2048]{1,0:T(8,128)(2,1)S(1)} %get-tuple-element.19.mid_ref), channel_id=1, source_target_pairs={{0,1},{1,0},{2,3},{3,2},{4,5},{5,4},{6,7},{7,6},{8,9},{9,8},{10,11... | collective-permute-start | bytes 786440 | tf_op jit(solution)/shard_map/ppermute | solution.py:570
  24.5 10.8 %copy-start.10 = (s32[8,3,128]{2,0,1:T(8,128)S(1)}, s32[8,3,128]{2,0,1:T(8,128)}, u32[]{:S(2)}) copy-start(s32[8,3,128]{2,0,1:T(8,128)} %param.24) | copy-start | bytes 36868
  24.5 10.8 %copy-start.12 = (s32[8,3]{0,1:T(4,128)S(1)}, s32[8,3]{0,1:T(4,128)}, u32[]{:S(2)}) copy-start(s32[8,3]{0,1:T(4,128)} %param.23) | copy-start | bytes 292
  24.5 17.7 %copy-start.1 = (f32[1,16,64,128]{3,2,1,0:T(8,128)S(1)}, f32[1,16,64,128]{3,2,1,0:T(8,128)}, u32[]{:S(2)}) copy-start(f32[1,16,64,128]{3,2,1,0:T(8,128)} %param.19) | copy-start | bytes 1572868
  25.9 16.3 %copy-start.6 = (bf16[256,256]{1,0:T(8,128)(2,1)S(1)}, bf16[256,256]{1,0:T(8,128)(2,1)}, u32[]{:S(2)}) copy-start(bf16[256,256]{1,0:T(8,128)(2,1)} %constant.35.clone.band_ref) | copy-start | bytes 393220
  26.5 15.6 %all-to-all-start = ((bf16[16,16,128]{2,1,0:T(8,128)(2,1)}), bf16[16,16,128]{2,1,0:T(8,128)(2,1)S(1)}, u32[]{:S(2)}, u32[]{:S(2)}) async-start(bf16[16,16,128]{2,1,0:T(8,128)(2,1)} %broadcast_in_dim.13), calls=%async_computation | async-start | bytes 131072 | tf_op jit(solution)/shard_map/all_to_all | solution.py:607
  35.3 7.0 %copy-start.9 = (bf16[64,64]{1,0:T(8,128)(2,1)S(1)}, bf16[64,64]{1,0:T(8,128)(2,1)}, u32[]{:S(2)}) copy-start(bf16[64,64]{1,0:T(8,128)(2,1)} %constant.32.clone.tall_ref) | copy-start | bytes 24580

commit v4 on v3

--- a/solution.py
+++ b/solution.py
@@ -165,27 +165,46 @@
     )(near, mid, far, beyond, weight, head)
 
 
-def band_matrix():
-    band = np.zeros((FX, FX), np.float64)
+def band_matrix(length, diagonal):
+    band = np.zeros((length, length), np.float64)
     for reach, weight in enumerate(stencil_weights):
-        for at in range(FX):
+        for at in range(length):
             if reach == 0:
-                band[at, at] = 3.0 * weight
-            elif at + reach < FX:
+                band[at, at] = diagonal
+            elif at + reach < length:
                 band[at, at + reach] = band[at + reach, at] = weight
     high = band.astype(jnp.bfloat16)
-    low = (band - high.astype(np.float64)).astype(jnp.bfloat16)
+    return high, (band - high.astype(np.float64)).astype(jnp.bfloat16)
+
+
+def row_band():
+    high, low = band_matrix(FX, 3.0 * stencil_weights[0])
     return jnp.asarray(np.block([[high, low], [high, np.zeros_like(low)]]))
 
 
+def column_band():
+    high, low = band_matrix(FY, 0.0)
+    return jnp.asarray(np.concatenate([high, high, low], axis=1))
+
+
 INNER = slice(PAD, PAD + FY)
 
 
-def laplace(field, first, band, use):
+def laplace(field, first, bands, use):
     planes = field[pl.ds(first, CHUNK), INNER, :].reshape(CHUNK * FY, FX)
     high, low = halves(planes)
     across = jnp.dot(
-        jnp.concatenate([high, low], axis=1), band, preferred_element_type=jnp.float32
+        jnp.concatenate([high, low], axis=1), bands[0][...], preferred_element_type=jnp.float32
+    )
+
+    def abreast(value):
+        return jnp.concatenate([value[k * FY : (k + 1) * FY] for k in range(CHUNK)], axis=1)
+
+    high, low = abreast(high), abreast(low)
+    down = jnp.dot(
+        bands[1][...],
+        jnp.concatenate([high, low, high], axis=0),
+        preferred_element_type=jnp.float32,
     )
     for row in range(0, FY, 8):
         column = [
@@ -195,12 +214,9 @@
         for k in range(CHUNK):
             begin = k * FY + row
             total = across[begin : begin + 8, :FX] + across[begin : begin + 8, FX:]
+            total = total + down[row : row + 8, k * FX : (k + 1) * FX]
             for reach in range(1, REACH + 1):
                 near = column[k + REACH - reach] + column[k + REACH + reach]
-                begin = PAD + row - reach
-                near = near + field[first + k, begin : begin + 8, :]
-                begin = PAD + row + reach
-                near = near + field[first + k, begin : begin + 8, :]
                 total = total + stencil_weights[reach] * near
             use(k, slice(row, row + 8), column[k + REACH], total)
 
@@ -298,7 +314,8 @@
     tall_ref,
     short_ref,
     narrow_ref,
-    band_ref,
+    row_band_ref,
+    column_band_ref,
     final_out,
     terms_ref,
     copied,
@@ -311,7 +328,7 @@
     rows_ref,
 ):
     slab, has_low, has_high = slab_place()
-    band = band_ref[...]
+    bands = (row_band_ref, column_band_ref)
     for field in (field_a, field_b):
         clear_rows(field, 0, EXT)
         clear_beyond(field, has_low, has_high)
@@ -387,16 +404,17 @@
     lane_row = lax.broadcasted_iota(jnp.int32, (1, FX), 1)
 
     def inject(field, step, first, last):
-        @pl.when((source_plane >= first) & (source_plane < last))
-        def _():
-            place = (source_plane, pl.ds(source_row, 1), slice(None))
-            field[place] = field[place] + jnp.where(
-                lane_row == plan[3, 0], pulses_ref[step : step + 1, :], 0.0
-            )
+        inside = (source_plane >= first) & (source_plane < last)
+        plane = jnp.clip(source_plane, first, last - 1)
+        place = (plane, pl.ds(source_row, 1), slice(None))
+        field[place] = field[place] + jnp.where(
+            inside & (lane_row == plan[3, 0]), pulses_ref[step : step + 1, :], 0.0
+        )
 
     def collect(field, step, k):
         rows_ref[step, pl.ds(k, 1), :] = field.reshape(EXT * ROWS, FX)[pl.ds(plan[0, k], 1), :]
 
+    stores = []
     for step in range(STEPS):
         now, out = (field_a, field_b) if step % 2 == 0 else (field_b, field_a)
         reach_out = CUR_RIM - REACH * (step + 1)
@@ -410,7 +428,7 @@
             def use(k, rows, centre, lap):
                 advance(chunk * CHUNK + k, rows, centre, lap)
 
-            laplace(now, chunk * CHUNK, band, use)
+            laplace(now, chunk * CHUNK, bands, use)
 
         def own_planes(chunk):
             begin = chunk * CHUNK
@@ -422,7 +440,7 @@
                 total[begin + k, rows, :] = term
                 advance(CUR_RIM + begin + k, rows, centre, lap)
 
-            laplace(now, CUR_RIM + begin, band, use)
+            laplace(now, CUR_RIM + begin, bands, use)
             share = NREC * CHUNK // PLANES if step > 0 else 0
             for k in range(share):
                 collect(now, step - 1, chunk * share + k)
@@ -430,14 +448,21 @@
         first, last = stretch(has_low, has_high, reach_out)
         for chunk in range(PLANES // CHUNK):
             own_planes(chunk)
+            if reach_out == 0:
+                begin = CUR_RIM + chunk * CHUNK
+                inject(out, step, begin, begin + CHUNK)
+                stores.append(
+                    pltpu.make_async_copy(
+                        out.at[pl.ds(begin, CHUNK), pl.ds(PAD, FY), :],
+                        final_out.at[pl.ds(chunk * CHUNK, CHUNK)],
+                        copied.at[chunk],
+                    )
+                )
+                stores[-1].start()
         if reach_out > 0:
             over_rims(has_low, has_high, reach_out, CHUNK, rim_planes)
-        inject(out, step, first, last)
-
-    store = pltpu.make_async_copy(
-        field_a.at[pl.ds(CUR_RIM, PLANES), pl.ds(PAD, FY), :], final_out, copied
-    )
-    store.start()
+            inject(out, step, first, last)
+
     for k in range(NREC):
         collect(field_a, STEPS - 1, k)
     record = jnp.concatenate(
@@ -492,7 +517,8 @@
     def _():
         terms_ref[slab * SHOTS + SHOTS, :16, :] = above.astype(jnp.bfloat16)
 
-    store.wait()
+    for store in stores:
+        store.wait()
 
 
 def wave(*args):
@@ -503,10 +529,10 @@
             jax.ShapeDtypeStruct((PLANES, FY, FX), jnp.float32),
             jax.ShapeDtypeStruct((devices, 32, 128), jnp.bfloat16),
         ),
-        in_specs=[pl.BlockSpec(memory_space=pltpu.SMEM)] + [VMEM] * 13,
+        in_specs=[pl.BlockSpec(memory_space=pltpu.SMEM)] + [VMEM] * 14,
         out_specs=(ANY, VMEM),
         scratch_shapes=[
-            pltpu.SemaphoreType.DMA,
+            pltpu.SemaphoreType.DMA((PLANES // CHUNK,)),
             pltpu.VMEM((EXT, ROWS, FX), jnp.float32),
             pltpu.VMEM((EXT, ROWS, FX), jnp.float32),
             pltpu.VMEM((EXT, FY, FX), jnp.float32),
@@ -623,7 +649,8 @@
         adjoint,
         speeds,
         *plane_matrices(),
-        band_matrix(),
+        row_band(),
+        column_band(),
     )
 
     gradient, traces = finish(lax.all_to_all(terms, "slab", 0, 0))

time: 60.5 us -> 59.5 us (0.983)
  Pallas kernels: 10.4 us -> 9.32 us
    pallas_call x1, Pallas kernels: 6.81 us -> 5.75 us  [wave(): pl.pallas_call(wave_kernel, out_shape=(jax.ShapeDtypeStruct((PLANES, FY,...]
where the time goes in v4:
time: 59.5 us; the launch traced here: 59.2 us
  starting transfers between devices  28.4 us (48%)
  blocking collectives  10.5 us (18%)
  Pallas kernels  9.32 us (16%)
  waiting for transfers between devices  7.89 us (13%)
  other arithmetic  1.24 us (2%)
  between operations  0.96 us (2%)
  local copies, waits for them, and re-layouts  0.79 us (1%)
    ppermute x3, starting transfers between devices, partner(): lax.ppermute(value, 'slab', [(source, source ^ mask) for source in range(...  17.4 us
    all_to_all x1, blocking collectives, body(): gradient, traces = finish(lax.all_to_all(terms, 'slab', 0, 0))  10.5 us
    all_to_all x1, starting transfers between devices, body(): lax.all_to_all(jnp.broadcast_to(velocity[None], (devices,) + velocity.sha...  8.73 us
    all_to_all x1, waiting for transfers between devices, body(): lax.all_to_all(jnp.broadcast_to(velocity[None], (devices,) + velocity.sha...  6.72 us
    pallas_call x1, Pallas kernels, wave(): pl.pallas_call(wave_kernel, out_shape=(jax.ShapeDtypeStruct((PLANES, FY,...  5.75 us
    ppermute x2, starting transfers between devices, across_chips(): return lax.ppermute(value, 'slab', pairs + [(b, a) for a, b in pairs])  1.47 us
    pallas_call x1, Pallas kernels, first_conv(): pl.pallas_call(first_kernel, out_shape=(plane, plane), in_specs=[VMEM] *...  1.47 us
    pallas_call x1, Pallas kernels, second_conv(): pl.pallas_call(second_kernel, out_shape=jax.ShapeDtypeStruct((16, 128), j...  1.34 us
  transfers between devices with their start and end apart: 7, of which 2 were waited for; matrix products, arithmetic and copies ran while one was open for 3% of the time, Pallas kernels for 5%

profile of v4, /device:TPU:0, one launch (start us, length us, event | category | flops | bytes accessed | tf_op | source)
XLA Modules:
  0.0 59.2 jit_solution(8186202713347674819)
XLA Ops:
  0.6 0.0 copy-start
  0.6 0.8 %collective-permute-start.2 = (bf16[64,2048]{1,0:T(8,128)(2,1)}, bf16[64,2048]{1,0:T(8,128)(2,1)S(1)}, u32[]{:S(2)}, u32[]{:S(2)}) collective-permute-start(bf16[64,2048]{1,0:T(8,128)(2,1)} %bitcast.17), channel_id=1, source_target_pairs={{9,7},{6,8},{25,23},{22,24}} | collective-permute-start | bytes 786440 | tf_op jit(solution)/shard_map/ppermute | solution.py:591
  1.5 0.5 collective-permute-start.1
  2.0 0.7 %collective-permute-start = (bf16[64,2048]{1,0:T(8,128)(2,1)}, bf16[64,2048]{1,0:T(8,128)(2,1)S(1)}, u32[]{:S(2)}, u32[]{:S(2)}) collective-permute-start(bf16[64,2048]{1,0:T(8,128)(2,1)} %bitcast.19), channel_id=1, source_target_pairs={{1,2},{3,4},{5,6},{7,8},{9,10},{11,12},{13,14},{2,1},{4,3},{6,5},{... | collective-permute-start | bytes 786440 | tf_op jit(solution)/shard_map/ppermute | solution.py:584
  2.7 1.1 %convert.12 = bf16[1,16,64,128]{3,2,1,0:T(8,128)(2,1)S(1)} convert(f32[1,16,64,128]{3,2,1,0:T(8,128)} %param.20) | non-fusion elementwise | flops 131072 | bytes 786432 | tf_op jit(solution)/shard_map/convert.7
  3.8 0.0 copy-done
  3.8 0.1 slice_bitcast_fusion
  3.9 0.1 pad_maximum_fusion
  4.0 0.0 collective-permute-done.2.extra_ref
  4.0 0.0 collective-permute-done.1.near_ref
  4.0 0.0 collective-permute-done.far_ref
  4.0 0.0 copy-start.3
  4.0 0.0 copy-start.5
  4.0 0.1 broadcast_select_fusion
  4.1 0.0 copy-start.4
  4.1 13.1 %collective-permute-start.3 = (bf16[28,64,128]{2,1,0:T(8,128)(2,1)S(1)}, bf16[28,64,128]{2,1,0:T(8,128)(2,1)S(1)}, u32[]{:S(2)}, u32[]{:S(2)}) collective-permute-start(bf16[28,64,128]{2,1,0:T(8,128)(2,1)S(1)} %broadcast_select_fusion), channel_id=1, source_target_pairs={{0,8},{1,9},{2,10},{3,11},{4,12},{5,13},{6,14},{7,15},{8,0},{9,1},... | collective-permute-start | bytes 1376264 | tf_op jit(solution)/shard_map/ppermute | solution.py:596
  17.2 0.0 copy-done.3
  17.2 0.0 copy-done.5
  17.2 0.0 copy-start.15
  17.2 0.0 copy-start.14
  17.2 0.0 copy-start.7
  17.3 0.0 copy-start.8
  17.3 0.0 copy-start.9
  17.3 0.0 copy-start.12
  17.3 1.5 %shard_map.176 = (bf16[64,2048]{1,0:T(8,128)(2,1)S(1)}, bf16[64,2048]{1,0:T(8,128)(2,1)S(1)}) custom-call(bf16[64,2048]{1,0:T(8,128)(2,1)S(1)} %collective-permute-done.1.near_ref, bf16[64,2048]{1,0:T(8,128)(2,1)S(1)} %bitcast.20, bf16[64,2048]{1,0:T(8,128)(2,1)S(1)} %collective-permute-done.far_ref, bf16[64,2048]{1,0:T(8,128)(2,1)S(1)} %collective-permute-done.2.extra_ref, ...), custom_call_target="tpu_custom_call" | custom-call | tf_op jit(solution)/shard_map/pallas_call | solution.py:147
  18.8 0.0 copy-start.2
  18.8 0.8 %collective-permute-start.5 = (bf16[64,2048]{1,0:T(8,128)(2,1)S(1)}, bf16[64,2048]{1,0:T(8,128)(2,1)S(1)}, u32[]{:S(2)}, u32[]{:S(2)}) collective-permute-start(bf16[64,2048]{1,0:T(8,128)(2,1)S(1)} %get-tuple-element.19.mid_ref), channel_id=1, source_target_pairs={{1,2},{3,4},{5,6},{9,10},{11,12},{13,14},{2,1},{4,3},{6,5},{10,9},... | collective-permute-start | bytes 786440 | tf_op jit(solution)/shard_map/ppermute | solution.py:584
  19.6 3.8 %collective-permute-start.4 = (bf16[64,2048]{1,0:T(8,128)(2,1)S(1)}, bf16[64,2048]{1,0:T(8,128)(2,1)S(1)}, u32[]{:S(2)}, u32[]{:S(2)}) collective-permute-start(bf16[64,2048]{1,0:T(8,128)(2,1)S(1)} %get-tuple-element.19.mid_ref), channel_id=1, source_target_pairs={{0,1},{1,0},{2,3},{3,2},{4,5},{5,4},{6,7},{7,6},{8,9},{9,8},{10,11... | collective-permute-start | bytes 786440 | tf_op jit(solution)/shard_map/ppermute | solution.py:596
  23.4 0.0 collective-permute-done.5.far_ref
  23.4 1.2 %collective-permute-done.4.near_ref = bf16[64,2048]{1,0:T(8,128)(2,1)S(1)} collective-permute-done((bf16[64,2048]{1,0:T(8,128)(2,1)S(1)}, bf16[64,2048]{1,0:T(8,128)(2,1)S(1)}, u32[]{:S(2)}, u32[]{:S(2)}) %collective-permute-start.4) | collective-permute-done | bytes 262176 | tf_op jit(solution)/shard_map/ppermute | solution.py:596
  24.5 0.0 copy-done.4
  24.5 0.0 copy-done.15
  24.5 0.0 copy-start.11
  24.5 0.0 copy-start.13
  24.5 0.0 copy-start.1
  24.6 1.3 %shard_map.177 = bf16[16,128]{1,0:T(8,128)(2,1)S(1)} custom-call(bf16[64,2048]{1,0:T(8,128)(2,1)S(1)} %collective-permute-done.4.near_ref, bf16[64,2048]{1,0:T(8,128)(2,1)S(1)} %get-tuple-element.19.mid_ref, bf16[64,2048]{1,0:T(8,128)(2,1)S(1)} %collective-permute-done.5.far_ref, bf16[64,2048]{1,0:T(8,128)(2,1)S(1)} %get-tuple-element.20.beyond_ref, ...), custom_call_target="tpu_custom_call" | custom-call | tf_op jit(solution)/shard_map/pallas_call | solution.py:158
  25.9 0.0 copy-start.6
  25.9 0.6 %broadcast_in_dim.13 = bf16[16,16,128]{2,1,0:T(8,128)(2,1)} broadcast(bf16[16,128]{1,0:T(8,128)(2,1)S(1)} %shard_map.177), dimensions={1,2} | broadcast | bytes 69632 | tf_op jit(solution)/shard_map/broadcast_in_dim | solution.py:634
  26.6 8.7 %all-to-all-start = ((bf16[16,16,128]{2,1,0:T(8,128)(2,1)}), bf16[16,16,128]{2,1,0:T(8,128)(2,1)S(1)}, u32[]{:S(2)}, u32[]{:S(2)}) async-start(bf16[16,16,128]{2,1,0:T(8,128)(2,1)} %broadcast_in_dim.13), calls=%async_computation | async-start | bytes 131072 | tf_op jit(solution)/shard_map/all_to_all | solution.py:633
  35.3 0.0 copy-start.10
  35.3 0.0 copy-done.14
  35.3 0.0 copy-done.11
  35.3 0.0 copy-done.13
  35.3 0.1 shard_map.175
  35.5 6.7 %all-to-all-done.speeds_ref = bf16[16,16,128]{2,1,0:T(8,128)(2,1)S(1)} async-done(((bf16[16,16,128]{2,1,0:T(8,128)(2,1)}), bf16[16,16,128]{2,1,0:T(8,128)(2,1)S(1)}, u32[]{:S(2)}, u32[]{:S(2)}) %all-to-all-start) | async-done | bytes 65568 | tf_op jit(solution)/shard_map/all_to_all | solution.py:633
  42.2 0.0 collective-permute-done.3.low_0.high_0
  42.2 0.0 copy-done.7
  42.2 0.0 copy-done.8
  42.2 0.0 copy-done.9
  42.2 0.0 copy-done.12
  42.2 0.0 copy-done.2
  42.2 0.0 copy-done.1
  42.2 0.0 copy-done.6
  42.2 0.0 copy-done.10
  42.3 5.8 %shard_map.178 = (f32[16,64,128]{2,1,0:T(8,128)}, bf16[16,32,128]{2,1,0:T(8,128)(2,1)S(1)}) custom-call(s32[4,128]{1,0:T(4,128)S(1)} %get-tuple-element.14.plan, f32[128,128]{1,0:T(8,128)S(1)} %get-tuple-element.15.pick_ref, f32[4,128]{1,0:T(4,128)S(1)} %get-tuple-element.16.pulses_ref, f32[16,64,128]{2,1,0:T(8,128)S(1)} %bitcast.14, ...), custom_call_target="tpu_custom_call" | custom-call | tf_op jit(solution)/shard_map/pallas_call | solution.py:526
  48.0 10.5 %all_to_all.10.terms_ref = bf16[16,32,128]{2,1,0:T(8,128)(2,1)S(1)} all-to-all(bf16[16,32,128]{2,1,0:T(8,128)(2,1)S(1)} %get-tuple-element.22), channel_id=1, replica_groups=mesh['groups'=2,'slab'=16] {'slab'}, dimensions={0} | all-to-all | bytes 262144 | tf_op jit(solution)/shard_map/all_to_all | solution.py:656
  58.5 0.6 %shard_map.179 = (f32[1,2048]{1,0:T(1,128)}, f32[8,4,128]{2,1,0:T(4,128)}) custom-call(bf16[16,32,128]{2,1,0:T(8,128)(2,1)S(1)} %all_to_all.10.terms_ref), custom_call_target="tpu_custom_call" | custom-call | tf_op jit(solution)/shard_map/pallas_call | solution.py:563
  (1 shorter events, 0.0 us)
Async XLA Ops:
  0.6 3.1 %copy-start = (f32[1,16,64,128]{3,2,1,0:T(8,128)S(1)}, f32[1,16,64,128]{3,2,1,0:T(8,128)}, u32[]{:S(2)}) copy-start(f32[1,16,64,128]{3,2,1,0:T(8,128)} %param.21) | copy-start | bytes 1572868
  0.6 3.3 %collective-permute-start.2 = (bf16[64,2048]{1,0:T(8,128)(2,1)}, bf16[64,2048]{1,0:T(8,128)(2,1)S(1)}, u32[]{:S(2)}, u32[]{:S(2)}) collective-permute-start(bf16[64,2048]{1,0:T(8,128)(2,1)} %bitcast.17), channel_id=1, source_target_pairs={{9,7},{6,8},{25,23},{22,24}} | collective-permute-start | bytes 786440 | tf_op jit(solution)/shard_map/ppermute | solution.py:591
  1.5 2.5 %collective-permute-start.1 = (bf16[64,2048]{1,0:T(8,128)(2,1)}, bf16[64,2048]{1,0:T(8,128)(2,1)S(1)}, u32[]{:S(2)}, u32[]{:S(2)}) collective-permute-start(bf16[64,2048]{1,0:T(8,128)(2,1)} %bitcast.18), channel_id=1, source_target_pairs={{0,1},{1,0},{2,3},{3,2},{4,5},{5,4},{6,7},{7,6},{8,9},{9,8},{10,11... | collective-permute-start | bytes 786440 | tf_op jit(solution)/shard_map/ppermute | solution.py:596
  2.0 2.0 %collective-permute-start = (bf16[64,2048]{1,0:T(8,128)(2,1)}, bf16[64,2048]{1,0:T(8,128)(2,1)S(1)}, u32[]{:S(2)}, u32[]{:S(2)}) collective-permute-start(bf16[64,2048]{1,0:T(8,128)(2,1)} %bitcast.19), channel_id=1, source_target_pairs={{1,2},{3,4},{5,6},{7,8},{9,10},{11,12},{13,14},{2,1},{4,3},{6,5},{... | collective-permute-start | bytes 786440 | tf_op jit(solution)/shard_map/ppermute | solution.py:584
  4.0 13.2 %copy-start.3 = (bf16[27,64,64]{2,1,0:T(8,128)(2,1)S(1)}, bf16[27,64,64]{2,1,0:T(8,128)(2,1)}, u32[]{:S(2)}) copy-start(bf16[27,64,64]{2,1,0:T(8,128)(2,1)} %weight_ref.2) | copy-start | bytes 663556
  4.0 13.2 %copy-start.5 = (bf16[64,1,2048]{2,0,1:T(8,128)(2,1)S(1)}, bf16[64,1,2048]{2,0,1:T(8,128)(2,1)}, u32[]{:S(2)}) copy-start(bf16[64,1,2048]{2,0,1:T(8,128)(2,1)} %param.16) | copy-start | bytes 786436
  4.1 20.5 %copy-start.4 = (bf16[27,64,64]{2,1,0:T(8,128)(2,1)S(1)}, bf16[27,64,64]{2,1,0:T(8,128)(2,1)}, u32[]{:S(2)}) copy-start(bf16[27,64,64]{2,1,0:T(8,128)(2,1)} %weight_ref.3) | copy-start | bytes 663556
  4.1 38.1 %collective-permute-start.3 = (bf16[28,64,128]{2,1,0:T(8,128)(2,1)S(1)}, bf16[28,64,128]{2,1,0:T(8,128)(2,1)S(1)}, u32[]{:S(2)}, u32[]{:S(2)}) collective-permute-start(bf16[28,64,128]{2,1,0:T(8,128)(2,1)S(1)} %broadcast_select_fusion), channel_id=1, source_target_pairs={{0,8},{1,9},{2,10},{3,11},{4,12},{5,13},{6,14},{7,15},{8,0},{9,1},... | collective-permute-start | bytes 1376264 | tf_op jit(solution)/shard_map/ppermute | solution.py:596
  17.2 7.3 %copy-start.15 = (bf16[64]{0:T(256)(128)(2,1)S(1)}, bf16[64]{0:T(256)(128)(2,1)}, u32[]{:S(2)}) copy-start(bf16[64]{0:T(256)(128)(2,1)} %param.19) | copy-start | bytes 388
  17.2 18.1 %copy-start.14 = (f32[8,4]{0,1:T(4,128)S(1)}, f32[8,4]{0,1:T(4,128)}, u32[]{:S(2)}) copy-start(f32[8,4]{0,1:T(4,128)} %param.23) | copy-start | bytes 388
  17.2 24.9 %copy-start.7 = (bf16[256,128]{1,0:T(8,128)(2,1)S(1)}, bf16[256,128]{1,0:T(8,128)(2,1)}, u32[]{:S(2)}) copy-start(bf16[256,128]{1,0:T(8,128)(2,1)} %constant.36.clone.narrow_ref) | copy-start | bytes 196612
  17.3 24.9 %copy-start.8 = (bf16[128,256]{1,0:T(8,128)(2,1)S(1)}, bf16[128,256]{1,0:T(8,128)(2,1)}, u32[]{:S(2)}) copy-start(bf16[128,256]{1,0:T(8,128)(2,1)} %constant.33.clone.widen_ref) | copy-start | bytes 196612
  17.3 24.9 %copy-start.9 = (bf16[64,192]{1,0:T(8,128)(2,1)S(1)}, bf16[64,192]{1,0:T(8,128)(2,1)}, u32[]{:S(2)}) copy-start(bf16[64,192]{1,0:T(8,128)(2,1)} %constant.38.clone.column_band_ref) | copy-start | bytes 73732
  17.3 24.9 %copy-start.12 = (bf16[32,128]{1,0:T(8,128)(2,1)S(1)}, bf16[32,128]{1,0:T(8,128)(2,1)}, u32[]{:S(2)}) copy-start(bf16[32,128]{1,0:T(8,128)(2,1)} %constant.35.clone.short_ref) | copy-start | bytes 24580
  18.8 23.4 %copy-start.2 = (bf16[4,1,16,64,128]{4,3,2,1,0:T(8,128)(2,1)S(1)}, bf16[4,1,16,64,128]{4,3,2,1,0:T(8,128)(2,1)}, u32[]{:S(2)}) copy-start(bf16[4,1,16,64,128]{4,3,2,1,0:T(8,128)(2,1)} %param.22) | copy-start | bytes 3145732
  18.8 4.6 %collective-permute-start.5 = (bf16[64,2048]{1,0:T(8,128)(2,1)S(1)}, bf16[64,2048]{1,0:T(8,128)(2,1)S(1)}, u32[]{:S(2)}, u32[]{:S(2)}) collective-permute-start(bf16[64,2048]{1,0:T(8,128)(2,1)S(1)} %get-tuple-element.19.mid_ref), channel_id=1, source_target_pairs={{1,2},{3,4},{5,6},{9,10},{11,12},{13,14},{2,1},{4,3},{6,5},{10,9},... | collective-permute-start | bytes 786440 | tf_op jit(solution)/shard_map/ppermute | solution.py:584
  19.6 4.9 %collective-permute-start.4 = (bf16[64,2048]{1,0:T(8,128)(2,1)S(1)}, bf16[64,2048]{1,0:T(8,128)(2,1)S(1)}, u32[]{:S(2)}, u32[]{:S(2)}) collective-permute-start(bf16[64,2048]{1,0:T(8,128)(2,1)S(1)} %get-tuple-element.19.mid_ref), channel_id=1, source_target_pairs={{0,1},{1,0},{2,3},{3,2},{4,5},{5,4},{6,7},{7,6},{8,9},{9,8},{10,11... | collective-permute-start | bytes 786440 | tf_op jit(solution)/shard_map/ppermute | solution.py:596
  24.5 10.8 %copy-start.11 = (s32[8,3,128]{2,0,1:T(8,128)S(1)}, s32[8,3,128]{2,0,1:T(8,128)}, u32[]{:S(2)}) copy-start(s32[8,3,128]{2,0,1:T(8,128)} %param.25) | copy-start | bytes 36868
  24.5 10.8 %copy-start.13 = (s32[8,3]{0,1:T(4,128)S(1)}, s32[8,3]{0,1:T(4,128)}, u32[]{:S(2)}) copy-start(s32[8,3]{0,1:T(4,128)} %param.24) | copy-start | bytes 292
  24.5 17.7 %copy-start.1 = (f32[1,16,64,128]{3,2,1,0:T(8,128)S(1)}, f32[1,16,64,128]{3,2,1,0:T(8,128)}, u32[]{:S(2)}) copy-start(f32[1,16,64,128]{3,2,1,0:T(8,128)} %param.20) | copy-start | bytes 1572868
  25.9 16.3 %copy-start.6 = (bf16[256,256]{1,0:T(8,128)(2,1)S(1)}, bf16[256,256]{1,0:T(8,128)(2,1)}, u32[]{:S(2)}) copy-start(bf16[256,256]{1,0:T(8,128)(2,1)} %constant.37.clone.row_band_ref) | copy-start | bytes 393220
  26.6 15.6 %all-to-all-start = ((bf16[16,16,128]{2,1,0:T(8,128)(2,1)}), bf16[16,16,128]{2,1,0:T(8,128)(2,1)S(1)}, u32[]{:S(2)}, u32[]{:S(2)}) async-start(bf16[16,16,128]{2,1,0:T(8,128)(2,1)} %broadcast_in_dim.13), calls=%async_computation | async-start | bytes 131072 | tf_op jit(solution)/shard_map/all_to_all | solution.py:633
  35.3 7.0 %copy-start.10 = (bf16[64,64]{1,0:T(8,128)(2,1)S(1)}, bf16[64,64]{1,0:T(8,128)(2,1)}, u32[]{:S(2)}) copy-start(bf16[64,64]{1,0:T(8,128)(2,1)} %constant.34.clone.tall_ref) | copy-start | bytes 24580

commit v5 on v4

--- a/solution.py
+++ b/solution.py
@@ -111,17 +111,18 @@
     return jnp.sum(jnp.where(here == there, row, 0), axis=1, keepdims=True)
 
 
-def first_kernel(
-    near_ref, mid_ref, far_ref, extra_ref, weight_ref, out_ref, beyond_ref, fields, packed
-):
-    near, mid, far = near_ref[...], mid_ref[...], far_ref[...]
-    hidden = leaky(conv(near, mid, far, weight_ref, fields, packed))
+def first_kernel(near_ref, mid_ref, far_ref, weight_ref, out_ref, fields, packed):
+    hidden = leaky(conv(near_ref[...], mid_ref[...], far_ref[...], weight_ref, fields, packed))
     out_ref[...] = hidden.astype(jnp.bfloat16)
 
+
+def beyond_kernel(mid_ref, far_ref, extra_ref, weight_ref, out_ref, fields, packed):
     @pl.when(at_boundary())
     def _():
-        hidden = leaky(conv(mid, far, extra_ref[...], weight_ref, fields, packed))
-        beyond_ref[...] = hidden.astype(jnp.bfloat16)
+        hidden = leaky(
+            conv(mid_ref[...], far_ref[...], extra_ref[...], weight_ref, fields, packed)
+        )
+        out_ref[...] = hidden.astype(jnp.bfloat16)
 
 
 def second_kernel(
@@ -142,16 +143,15 @@
 ]
 
 
-def first_conv(near, mid, far, extra, weight):
-    plane = jax.ShapeDtypeStruct((CH, CELLS), jnp.bfloat16)
+def first_conv(kernel, *args):
     return pl.pallas_call(
-        first_kernel,
-        out_shape=(plane, plane),
-        in_specs=[VMEM] * 5,
-        out_specs=(VMEM, VMEM),
+        kernel,
+        out_shape=jax.ShapeDtypeStruct((CH, CELLS), jnp.bfloat16),
+        in_specs=[VMEM] * 4,
+        out_specs=VMEM,
         scratch_shapes=CONV_SCRATCH,
         compiler_params=PARAMS,
-    )(near, mid, far, extra, weight)
+    )(*args)
 
 
 def second_conv(near, mid, far, beyond, weight, head):
@@ -627,8 +627,9 @@
     )
     low_0, high_0 = exchange(to_low, to_high)
 
-    hidden, beyond = first_conv(latent_near, latent, latent_far, latent_extra, conv1_weight)
+    hidden = first_conv(first_kernel, latent_near, latent, latent_far, conv1_weight)
     hidden_far, hidden_near = across_chips(hidden, False), partner(hidden, 1)
+    beyond = first_conv(beyond_kernel, latent, latent_far, latent_extra, conv1_weight)
     velocity = second_conv(hidden_near, hidden, hidden_far, beyond, conv2_weight, head[None])
     speeds = lax.all_to_all(
         jnp.broadcast_to(velocity[None], (devices,) + velocity.shape), "slab", 0, 0

time: 59.5 us -> 59.4 us (level)
    pallas_call x1 -> x2, Pallas kernels: 1.47 us -> 1.26 us  [first_conv(): pl.pallas_call(kernel, out_shape=jax.ShapeDtypeStruct((CH, CELLS), jnp.bf...]
where the time goes in v5:
time: 59.4 us; the launch traced here: 59 us
  starting transfers between devices  28.6 us (48%)
  blocking collectives  10.5 us (18%)
  Pallas kernels  9.1 us (15%)
  waiting for transfers between devices  7.79 us (13%)
  other arithmetic  1.24 us (2%)
  between operations  0.96 us (2%)
  local copies, waits for them, and re-layouts  0.79 us (1%)
    ppermute x3, starting transfers between devices, partner(): lax.ppermute(value, 'slab', [(source, source ^ mask) for source in range(...  17.4 us
    all_to_all x1, blocking collectives, body(): gradient, traces = finish(lax.all_to_all(terms, 'slab', 0, 0))  10.5 us
    all_to_all x1, starting transfers between devices, body(): lax.all_to_all(jnp.broadcast_to(velocity[None], (devices,) + velocity.sha...  8.9 us
    all_to_all x1, waiting for transfers between devices, body(): lax.all_to_all(jnp.broadcast_to(velocity[None], (devices,) + velocity.sha...  6.7 us
    pallas_call x1, Pallas kernels, wave(): pl.pallas_call(wave_kernel, out_shape=(jax.ShapeDtypeStruct((PLANES, FY,...  5.75 us
    ppermute x2, starting transfers between devices, across_chips(): return lax.ppermute(value, 'slab', pairs + [(b, a) for a, b in pairs])  1.47 us
    pallas_call x1, Pallas kernels, second_conv(): pl.pallas_call(second_kernel, out_shape=jax.ShapeDtypeStruct((16, 128), j...  1.34 us
    pallas_call x2, Pallas kernels, first_conv(): pl.pallas_call(kernel, out_shape=jax.ShapeDtypeStruct((CH, CELLS), jnp.bf...  1.26 us
  transfers between devices with their start and end apart: 7, of which 2 were waited for; matrix products, arithmetic and copies ran while one was open for 3% of the time, Pallas kernels for 5%

profile of v5, /device:TPU:0, one launch (start us, length us, event | category | flops | bytes accessed | tf_op | source)
XLA Modules:
  0.0 59.0 jit_solution(8187775698157259965)
XLA Ops:
  0.6 0.0 copy-start
  0.6 0.8 %collective-permute-start.2 = (bf16[64,2048]{1,0:T(8,128)(2,1)}, bf16[64,2048]{1,0:T(8,128)(2,1)S(1)}, u32[]{:S(2)}, u32[]{:S(2)}) collective-permute-start(bf16[64,2048]{1,0:T(8,128)(2,1)} %bitcast.17), channel_id=1, source_target_pairs={{9,7},{6,8},{25,23},{22,24}} | collective-permute-start | bytes 786440 | tf_op jit(solution)/shard_map/ppermute | solution.py:591
  1.5 0.5 collective-permute-start.1
  2.0 0.7 %collective-permute-start = (bf16[64,2048]{1,0:T(8,128)(2,1)}, bf16[64,2048]{1,0:T(8,128)(2,1)S(1)}, u32[]{:S(2)}, u32[]{:S(2)}) collective-permute-start(bf16[64,2048]{1,0:T(8,128)(2,1)} %bitcast.19), channel_id=1, source_target_pairs={{1,2},{3,4},{5,6},{7,8},{9,10},{11,12},{13,14},{2,1},{4,3},{6,5},{... | collective-permute-start | bytes 786440 | tf_op jit(solution)/shard_map/ppermute | solution.py:584
  2.7 1.1 %convert.12 = bf16[1,16,64,128]{3,2,1,0:T(8,128)(2,1)S(1)} convert(f32[1,16,64,128]{3,2,1,0:T(8,128)} %param.20) | non-fusion elementwise | flops 131072 | bytes 786432 | tf_op jit(solution)/shard_map/convert.7
  3.8 0.0 copy-done
  3.8 0.1 slice_bitcast_fusion
  3.9 0.1 pad_maximum_fusion
  4.0 0.0 collective-permute-done.2.extra_ref
  4.0 0.0 collective-permute-done.1.near_ref
  4.0 0.0 collective-permute-done.far_ref
  4.0 0.0 copy-start.2
  4.0 0.0 copy-start.4
  4.0 0.1 broadcast_select_fusion
  4.1 13.1 %collective-permute-start.3 = (bf16[28,64,128]{2,1,0:T(8,128)(2,1)S(1)}, bf16[28,64,128]{2,1,0:T(8,128)(2,1)S(1)}, u32[]{:S(2)}, u32[]{:S(2)}) collective-permute-start(bf16[28,64,128]{2,1,0:T(8,128)(2,1)S(1)} %broadcast_select_fusion), channel_id=1, source_target_pairs={{0,8},{1,9},{2,10},{3,11},{4,12},{5,13},{6,14},{7,15},{8,0},{9,1},... | collective-permute-start | bytes 1376264 | tf_op jit(solution)/shard_map/ppermute | solution.py:596
  17.2 0.0 copy-done.2
  17.2 0.0 copy-done.4
  17.2 1.2 %shard_map.176.mid_ref = bf16[64,2048]{1,0:T(8,128)(2,1)S(1)} custom-call(bf16[64,2048]{1,0:T(8,128)(2,1)S(1)} %collective-permute-done.1.near_ref, bf16[64,2048]{1,0:T(8,128)(2,1)S(1)} %bitcast.20, bf16[64,2048]{1,0:T(8,128)(2,1)S(1)} %collective-permute-done.far_ref, bf16[27,64,64]{2,1,0:T(8,128)(2,1)S(1)} %copy-done.2), custom_call_target="tpu_custom_call" | custom-call | tf_op jit(solution)/shard_map/pallas_call | solution.py:147
  18.5 0.0 copy-start.5
  18.5 0.8 %collective-permute-start.5 = (bf16[64,2048]{1,0:T(8,128)(2,1)S(1)}, bf16[64,2048]{1,0:T(8,128)(2,1)S(1)}, u32[]{:S(2)}, u32[]{:S(2)}) collective-permute-start(bf16[64,2048]{1,0:T(8,128)(2,1)S(1)} %shard_map.176.mid_ref), channel_id=1, source_target_pairs={{1,2},{3,4},{5,6},{9,10},{11,12},{13,14},{2,1},{4,3},{6,5},{10,9},... | collective-permute-start | bytes 786440 | tf_op jit(solution)/shard_map/ppermute | solution.py:584
  19.3 3.8 %collective-permute-start.4 = (bf16[64,2048]{1,0:T(8,128)(2,1)S(1)}, bf16[64,2048]{1,0:T(8,128)(2,1)S(1)}, u32[]{:S(2)}, u32[]{:S(2)}) collective-permute-start(bf16[64,2048]{1,0:T(8,128)(2,1)S(1)} %shard_map.176.mid_ref), channel_id=1, source_target_pairs={{0,1},{1,0},{2,3},{3,2},{4,5},{5,4},{6,7},{7,6},{8,9},{9,8},{10,11... | collective-permute-start | bytes 786440 | tf_op jit(solution)/shard_map/ppermute | solution.py:596
  23.1 0.0 copy-start.15
  23.1 0.0 copy-start.11
  23.1 0.0 copy-start.14
  23.1 0.0 copy-start.7
  23.1 0.0 copy-start.8
  23.1 0.0 copy-start.9
  23.1 0.0 copy-start.3
  23.1 0.0 collective-permute-done.5.far_ref
  23.1 1.1 %collective-permute-done.4.near_ref = bf16[64,2048]{1,0:T(8,128)(2,1)S(1)} collective-permute-done((bf16[64,2048]{1,0:T(8,128)(2,1)S(1)}, bf16[64,2048]{1,0:T(8,128)(2,1)S(1)}, u32[]{:S(2)}, u32[]{:S(2)}) %collective-permute-start.4) | collective-permute-done | bytes 262176 | tf_op jit(solution)/shard_map/ppermute | solution.py:596
  24.2 0.0 copy-done.5
  24.2 0.0 copy-done.15
  24.2 0.0 copy-start.13
  24.2 0.0 copy-start.1
  24.2 1.3 %shard_map.178 = bf16[16,128]{1,0:T(8,128)(2,1)S(1)} custom-call(bf16[64,2048]{1,0:T(8,128)(2,1)S(1)} %collective-permute-done.4.near_ref, bf16[64,2048]{1,0:T(8,128)(2,1)S(1)} %shard_map.176.mid_ref, bf16[64,2048]{1,0:T(8,128)(2,1)S(1)} %collective-permute-done.5.far_ref, bf16[64,2048]{1,0:T(8,128)(2,1)S(1)} %shard_map.177.beyond_ref, ...), custom_call_target="tpu_custom_call" | custom-call | tf_op jit(solution)/shard_map/pallas_call | solution.py:158
  25.6 0.0 copy-start.6
  25.6 0.6 %broadcast_in_dim.13 = bf16[16,16,128]{2,1,0:T(8,128)(2,1)} broadcast(bf16[16,128]{1,0:T(8,128)(2,1)S(1)} %shard_map.178), dimensions={1,2} | broadcast | bytes 69632 | tf_op jit(solution)/shard_map/broadcast_in_dim | solution.py:635
  26.2 8.9 %all-to-all-start = ((bf16[16,16,128]{2,1,0:T(8,128)(2,1)}), bf16[16,16,128]{2,1,0:T(8,128)(2,1)S(1)}, u32[]{:S(2)}, u32[]{:S(2)}) async-start(bf16[16,16,128]{2,1,0:T(8,128)(2,1)} %broadcast_in_dim.13), calls=%async_computation | async-start | bytes 131072 | tf_op jit(solution)/shard_map/all_to_all | solution.py:634
  35.1 0.0 copy-start.10
  35.1 0.0 copy-done.11
  35.2 0.0 copy-done.14
  35.2 0.0 copy-done.13
  35.2 0.1 shard_map.175
  35.3 0.0 copy-start.12
  35.3 6.7 %all-to-all-done.speeds_ref = bf16[16,16,128]{2,1,0:T(8,128)(2,1)S(1)} async-done(((bf16[16,16,128]{2,1,0:T(8,128)(2,1)}), bf16[16,16,128]{2,1,0:T(8,128)(2,1)S(1)}, u32[]{:S(2)}, u32[]{:S(2)}) %all-to-all-start) | async-done | bytes 65568 | tf_op jit(solution)/shard_map/all_to_all | solution.py:634
  42.0 0.0 collective-permute-done.3.low_0.high_0
  42.0 0.0 copy-done.7
  42.0 0.0 copy-done.8
  42.0 0.0 copy-done.9
  42.1 0.0 copy-done.3
  42.1 0.0 copy-done.1
  42.1 0.0 copy-done.6
  42.1 0.0 copy-done.10
  42.1 0.0 copy-done.12
  42.1 5.8 %shard_map.179 = (f32[16,64,128]{2,1,0:T(8,128)}, bf16[16,32,128]{2,1,0:T(8,128)(2,1)S(1)}) custom-call(s32[4,128]{1,0:T(4,128)S(1)} %get-tuple-element.12.plan, f32[128,128]{1,0:T(8,128)S(1)} %get-tuple-element.13.pick_ref, f32[4,128]{1,0:T(4,128)S(1)} %get-tuple-element.14.pulses_ref, f32[16,64,128]{2,1,0:T(8,128)S(1)} %bitcast.14, ...), custom_call_target="tpu_custom_call" | custom-call | tf_op jit(solution)/shard_map/pallas_call | solution.py:526
  47.9 10.5 %all_to_all.10.terms_ref = bf16[16,32,128]{2,1,0:T(8,128)(2,1)S(1)} all-to-all(bf16[16,32,128]{2,1,0:T(8,128)(2,1)S(1)} %get-tuple-element.18), channel_id=1, replica_groups=mesh['groups'=2,'slab'=16] {'slab'}, dimensions={0} | all-to-all | bytes 262144 | tf_op jit(solution)/shard_map/all_to_all | solution.py:657
  58.4 0.6 %shard_map.180 = (f32[1,2048]{1,0:T(1,128)}, f32[8,4,128]{2,1,0:T(4,128)}) custom-call(bf16[16,32,128]{2,1,0:T(8,128)(2,1)S(1)} %all_to_all.10.terms_ref), custom_call_target="tpu_custom_call" | custom-call | tf_op jit(solution)/shard_map/pallas_call | solution.py:563
  (2 shorter events, 0.1 us)
Async XLA Ops:
  0.6 3.1 %copy-start = (f32[1,16,64,128]{3,2,1,0:T(8,128)S(1)}, f32[1,16,64,128]{3,2,1,0:T(8,128)}, u32[]{:S(2)}) copy-start(f32[1,16,64,128]{3,2,1,0:T(8,128)} %param.21) | copy-start | bytes 1572868
  0.6 3.3 %collective-permute-start.2 = (bf16[64,2048]{1,0:T(8,128)(2,1)}, bf16[64,2048]{1,0:T(8,128)(2,1)S(1)}, u32[]{:S(2)}, u32[]{:S(2)}) collective-permute-start(bf16[64,2048]{1,0:T(8,128)(2,1)} %bitcast.17), channel_id=1, source_target_pairs={{9,7},{6,8},{25,23},{22,24}} | collective-permute-start | bytes 786440 | tf_op jit(solution)/shard_map/ppermute | solution.py:591
  1.5 2.5 %collective-permute-start.1 = (bf16[64,2048]{1,0:T(8,128)(2,1)}, bf16[64,2048]{1,0:T(8,128)(2,1)S(1)}, u32[]{:S(2)}, u32[]{:S(2)}) collective-permute-start(bf16[64,2048]{1,0:T(8,128)(2,1)} %bitcast.18), channel_id=1, source_target_pairs={{0,1},{1,0},{2,3},{3,2},{4,5},{5,4},{6,7},{7,6},{8,9},{9,8},{10,11... | collective-permute-start | bytes 786440 | tf_op jit(solution)/shard_map/ppermute | solution.py:596
  2.0 2.0 %collective-permute-start = (bf16[64,2048]{1,0:T(8,128)(2,1)}, bf16[64,2048]{1,0:T(8,128)(2,1)S(1)}, u32[]{:S(2)}, u32[]{:S(2)}) collective-permute-start(bf16[64,2048]{1,0:T(8,128)(2,1)} %bitcast.19), channel_id=1, source_target_pairs={{1,2},{3,4},{5,6},{7,8},{9,10},{11,12},{13,14},{2,1},{4,3},{6,5},{... | collective-permute-start | bytes 786440 | tf_op jit(solution)/shard_map/ppermute | solution.py:584
  4.0 13.2 %copy-start.2 = (bf16[27,64,64]{2,1,0:T(8,128)(2,1)S(1)}, bf16[27,64,64]{2,1,0:T(8,128)(2,1)}, u32[]{:S(2)}) copy-start(bf16[27,64,64]{2,1,0:T(8,128)(2,1)} %weight_ref.4) | copy-start | bytes 663556
  4.0 13.2 %copy-start.4 = (bf16[64,1,2048]{2,0,1:T(8,128)(2,1)S(1)}, bf16[64,1,2048]{2,0,1:T(8,128)(2,1)}, u32[]{:S(2)}) copy-start(bf16[64,1,2048]{2,0,1:T(8,128)(2,1)} %param.16) | copy-start | bytes 786436
  4.1 38.0 %collective-permute-start.3 = (bf16[28,64,128]{2,1,0:T(8,128)(2,1)S(1)}, bf16[28,64,128]{2,1,0:T(8,128)(2,1)S(1)}, u32[]{:S(2)}, u32[]{:S(2)}) collective-permute-start(bf16[28,64,128]{2,1,0:T(8,128)(2,1)S(1)} %broadcast_select_fusion), channel_id=1, source_target_pairs={{0,8},{1,9},{2,10},{3,11},{4,12},{5,13},{6,14},{7,15},{8,0},{9,1},... | collective-permute-start | bytes 1376264 | tf_op jit(solution)/shard_map/ppermute | solution.py:596
  18.5 5.8 %copy-start.5 = (bf16[27,64,64]{2,1,0:T(8,128)(2,1)S(1)}, bf16[27,64,64]{2,1,0:T(8,128)(2,1)}, u32[]{:S(2)}) copy-start(bf16[27,64,64]{2,1,0:T(8,128)(2,1)} %weight_ref.5) | copy-start | bytes 663556
  18.5 4.7 %collective-permute-start.5 = (bf16[64,2048]{1,0:T(8,128)(2,1)S(1)}, bf16[64,2048]{1,0:T(8,128)(2,1)S(1)}, u32[]{:S(2)}, u32[]{:S(2)}) collective-permute-start(bf16[64,2048]{1,0:T(8,128)(2,1)S(1)} %shard_map.176.mid_ref), channel_id=1, source_target_pairs={{1,2},{3,4},{5,6},{9,10},{11,12},{13,14},{2,1},{4,3},{6,5},{10,9},... | collective-permute-start | bytes 786440 | tf_op jit(solution)/shard_map/ppermute | solution.py:584
  19.3 4.9 %collective-permute-start.4 = (bf16[64,2048]{1,0:T(8,128)(2,1)S(1)}, bf16[64,2048]{1,0:T(8,128)(2,1)S(1)}, u32[]{:S(2)}, u32[]{:S(2)}) collective-permute-start(bf16[64,2048]{1,0:T(8,128)(2,1)S(1)} %shard_map.176.mid_ref), channel_id=1, source_target_pairs={{0,1},{1,0},{2,3},{3,2},{4,5},{5,4},{6,7},{7,6},{8,9},{9,8},{10,11... | collective-permute-start | bytes 786440 | tf_op jit(solution)/shard_map/ppermute | solution.py:596
  23.1 1.2 %copy-start.15 = (bf16[64]{0:T(256)(128)(2,1)S(1)}, bf16[64]{0:T(256)(128)(2,1)}, u32[]{:S(2)}) copy-start(bf16[64]{0:T(256)(128)(2,1)} %param.19) | copy-start | bytes 388
  23.1 12.1 %copy-start.11 = (s32[8,3,128]{2,0,1:T(8,128)S(1)}, s32[8,3,128]{2,0,1:T(8,128)}, u32[]{:S(2)}) copy-start(s32[8,3,128]{2,0,1:T(8,128)} %param.25) | copy-start | bytes 36868
  23.1 12.1 %copy-start.14 = (f32[8,4]{0,1:T(4,128)S(1)}, f32[8,4]{0,1:T(4,128)}, u32[]{:S(2)}) copy-start(f32[8,4]{0,1:T(4,128)} %param.23) | copy-start | bytes 388
  23.1 19.0 %copy-start.7 = (bf16[256,128]{1,0:T(8,128)(2,1)S(1)}, bf16[256,128]{1,0:T(8,128)(2,1)}, u32[]{:S(2)}) copy-start(bf16[256,128]{1,0:T(8,128)(2,1)} %constant.36.clone.narrow_ref) | copy-start | bytes 196612
  23.1 19.0 %copy-start.8 = (bf16[128,256]{1,0:T(8,128)(2,1)S(1)}, bf16[128,256]{1,0:T(8,128)(2,1)}, u32[]{:S(2)}) copy-start(bf16[128,256]{1,0:T(8,128)(2,1)} %constant.33.clone.widen_ref) | copy-start | bytes 196612
  23.1 19.0 %copy-start.9 = (bf16[64,192]{1,0:T(8,128)(2,1)S(1)}, bf16[64,192]{1,0:T(8,128)(2,1)}, u32[]{:S(2)}) copy-start(bf16[64,192]{1,0:T(8,128)(2,1)} %constant.38.clone.column_band_ref) | copy-start | bytes 73732
  23.1 18.9 %copy-start.3 = (bf16[4,1,16,64,128]{4,3,2,1,0:T(8,128)(2,1)S(1)}, bf16[4,1,16,64,128]{4,3,2,1,0:T(8,128)(2,1)}, u32[]{:S(2)}) copy-start(bf16[4,1,16,64,128]{4,3,2,1,0:T(8,128)(2,1)} %param.22) | copy-start | bytes 3145732
  24.2 10.9 %copy-start.13 = (s32[8,3]{0,1:T(4,128)S(1)}, s32[8,3]{0,1:T(4,128)}, u32[]{:S(2)}) copy-start(s32[8,3]{0,1:T(4,128)} %param.24) | copy-start | bytes 292
  24.2 17.8 %copy-start.1 = (f32[1,16,64,128]{3,2,1,0:T(8,128)S(1)}, f32[1,16,64,128]{3,2,1,0:T(8,128)}, u32[]{:S(2)}) copy-start(f32[1,16,64,128]{3,2,1,0:T(8,128)} %param.20) | copy-start | bytes 1572868
  25.6 16.5 %copy-start.6 = (bf16[256,256]{1,0:T(8,128)(2,1)S(1)}, bf16[256,256]{1,0:T(8,128)(2,1)}, u32[]{:S(2)}) copy-start(bf16[256,256]{1,0:T(8,128)(2,1)} %constant.37.clone.row_band_ref) | copy-start | bytes 393220
  26.2 15.8 %all-to-all-start = ((bf16[16,16,128]{2,1,0:T(8,128)(2,1)}), bf16[16,16,128]{2,1,0:T(8,128)(2,1)S(1)}, u32[]{:S(2)}, u32[]{:S(2)}) async-start(bf16[16,16,128]{2,1,0:T(8,128)(2,1)} %broadcast_in_dim.13), calls=%async_computation | async-start | bytes 131072 | tf_op jit(solution)/shard_map/all_to_all | solution.py:634
  35.1 7.0 %copy-start.10 = (bf16[64,64]{1,0:T(8,128)(2,1)S(1)}, bf16[64,64]{1,0:T(8,128)(2,1)}, u32[]{:S(2)}) copy-start(bf16[64,64]{1,0:T(8,128)(2,1)} %constant.34.clone.tall_ref) | copy-start | bytes 24580
  35.3 6.8 %copy-start.12 = (bf16[32,128]{1,0:T(8,128)(2,1)S(1)}, bf16[32,128]{1,0:T(8,128)(2,1)}, u32[]{:S(2)}) copy-start(bf16[32,128]{1,0:T(8,128)(2,1)} %constant.35.clone.short_ref) | copy-start | bytes 24580
